TPU v7x, 32 devices: a whole 2x2x4 slice. The times are simulated.
32 devices in a mesh: meet: 2 (over x), tm: 16 (over z, y, core).
Axes of the slice: x: 2, y: 2, z: 4, core: 2. Of those that a mesh axis runs over, the one named last changes fastest.
Arguments:
- waveform: bfloat16 [8, 327680], P(None, ('meet', 'tm')), parts along dimension 1, may hold values from -16 to 16
- masks: int32 [2, 2048, 257], P(None, ('meet', 'tm')), parts along dimension 1, may hold values from 0 to 255, as said below
- valid: int32 [2], P('meet'), parts along dimension 0, may hold values from 512 to 1024, as said below
- ref_mic: int32 [2], P('meet'), parts along dimension 0, may hold values from 0 to 7
- conv1_w: bfloat16 [9, 256], replicated, may hold values from -2 to 2
- conv1_b: float32 [256], replicated, may hold values from -4 to 4
- conv2_w: bfloat16 [9, 256, 256], replicated, may hold values from -0.125 to 0.125
- conv2_b: float32 [256], replicated, may hold values from -4 to 4
- proj_w: bfloat16 [4864, 256], replicated, may hold values from -0.078125 to 0.078125
- proj_b: float32 [256], replicated, may hold values from -4 to 4
Outputs:
- features: bfloat16 [1, 512, 256], P(None, ('meet', 'tm')), parts along dimension 1
There are 2 independent parts, one for each index of `meet`. A program takes and returns all parts, laid end to end along the dimension named above; an argument that names none is the same for every part. Nothing has to cross between parts.
Inputs may be any that keep to these rules, and one draw needn't show every extreme that they name: `masks`: mask levels; level / 255 is the weight of a time-frequency cell for a speaker or, in the last row, for the noise. `valid`: frames of the meeting that hold speech data; all 1024 in some meetings.
All inputs are finite; a program needn't handle non-finite values.
Results may differ from a plain program's by a relative error of at most 0.003.
The roundings to bfloat16 on the way count: a program that leaves them out, or rounds other values in their place, can miss the bound.
Values may be sent and summed in bfloat16 or wider, within the bound.
No kernel may reach another device: no remote copies, remote signals or barrier semaphores. Data moves between devices by JAX's collectives and lax.ppermute only.
A program may use at most 64 MiB of HBM per device.

v0:
```python
import functools
import math

import jax
import jax.numpy as jnp
import numpy as np
from jax import lax
from jax.experimental import pallas as pl
from jax.experimental.pallas import tpu as pltpu
from jax.sharding import PartitionSpec as P

NFFT = 512
HOP = 160
MELS = 80
BINS = NFFT // 2 + 1
LANES = 128
MICS = 8
PAD_BINS = -(-BINS // LANES) * LANES
TILES = PAD_BINS // LANES
HALO = 3
LEAD = 512
TAIL = 384
STATS = 2 * MICS * MICS
SPAN = 42

loading = 0.03
epsilon = 1e-06
sample_rate = 16000.0


def passed_along(block, axis, distance):
    devices = range(lax.axis_size(axis))
    route = [(i - distance, i) for i in devices if i - distance in devices]
    return lax.ppermute(block, axis, route)


def dft_table():
    n = np.arange(NFFT)
    f = np.arange(BINS)
    phase = 2.0 * math.pi * ((n[:, None] * f[None, :]) % NFFT) / NFFT
    window = 0.5 - 0.5 * np.cos(2.0 * math.pi * n / NFFT)
    table = np.zeros((NFFT, 2, PAD_BINS), np.float32)
    table[:, 0, :BINS] = window[:, None] * np.cos(phase)
    table[:, 1, :BINS] = -window[:, None] * np.sin(phase)
    return jnp.asarray(table.reshape(NFFT, 2 * PAD_BINS)).astype(jnp.bfloat16)


def mel_bank():
    mel_top = 2595.0 * math.log10(1.0 + sample_rate / 2.0 / 700.0)
    points = np.arange(MELS + 2) * (mel_top / (MELS + 1))
    edges = 700.0 * (np.power(10.0, points / 2595.0) - 1.0)
    freq = np.arange(BINS) * (sample_rate / 2.0 / (BINS - 1))
    lower, centre, upper = edges[:-2], edges[1:-1], edges[2:]
    rising = (freq[:, None] - lower[None, :]) / (centre - lower)[None, :]
    falling = (upper[None, :] - freq[:, None]) / (upper - centre)[None, :]
    return np.maximum(np.minimum(rising, falling), 0.0).astype(np.float32)


def packed_mel_bank():
    bank = mel_bank()
    packed = np.zeros((PAD_BINS, 2, LANES), np.float32)
    for half in range(2):
        part = bank[:, half * 40 : half * 40 + SPAN]
        for copy in range(3):
            packed[:BINS, half, copy * SPAN : copy * SPAN + part.shape[1]] = part
    return jnp.asarray(packed.reshape(PAD_BINS, 2 * LANES))


def packed_conv1(conv1_w):
    rows = []
    for shift_t in range(3):
        rows.append(conv1_w[3 * shift_t : 3 * shift_t + 3])
        rows.append(jnp.zeros((SPAN - 3, conv1_w.shape[1]), conv1_w.dtype))
    rows.append(jnp.zeros((LANES - 3 * SPAN, conv1_w.shape[1]), conv1_w.dtype))
    return jnp.concatenate(rows, axis=0)


def stats_kernel(frames, prev_ref, wave_ref, next_ref, masks_ref, valid_ref, table_ref, spec_ref, stats_ref, framed_ref, weight_ref):
    position = lax.axis_index("tm")
    span = frames + HALO
    extended = jnp.concatenate(
        [prev_ref[...].astype(jnp.float32), wave_ref[...].astype(jnp.float32), next_ref[...].astype(jnp.float32)], axis=1
    )
    width = extended.shape[1]
    rolled = {}
    for frame in range(span):
        start = LEAD - HALO * HOP + frame * HOP
        base, shift = start // LANES * LANES, start % LANES
        if shift not in rolled:
            rolled[shift] = extended if shift == 0 else pltpu.roll(extended, width - shift, 1)
        framed_ref[MICS * frame : MICS * (frame + 1), :] = rolled[shift][:, base : base + NFFT]
    rest = framed_ref.shape[0] - MICS * span
    framed_ref[MICS * span :, :] = jnp.zeros((rest, NFFT), jnp.float32)
    spec = jnp.dot(framed_ref[...].astype(jnp.bfloat16), table_ref[...], preferred_element_type=jnp.float32)
    for tile in range(2 * TILES):
        spec_ref[tile] = spec[:, tile * LANES : (tile + 1) * LANES]

    row = lax.broadcasted_iota(jnp.int32, (frames, 1), 0)
    live = jnp.where(position * frames + row < valid_ref[0], 1.0 / 255.0, 0.0)
    weight_ref[:, :, PAD_BINS - LANES :] = jnp.zeros((2, frames, LANES), jnp.float32)
    for k in range(2):
        weight_ref[k, :, :BINS] = masks_ref[k].astype(jnp.float32) * live

    low = lax.broadcasted_iota(jnp.int32, (MICS, LANES), 0) < MICS // 2
    for tile in range(TILES):
        at_re = slice(tile * LANES, (tile + 1) * LANES)

        def add_frames(group, sums):
            first = pl.multiple_of(group * MICS, MICS)
            weights = [weight_ref[k, pl.ds(first, MICS), at_re] for k in range(2)]
            for frame in range(MICS):
                rows = pl.ds(pl.multiple_of((first + frame + HALO) * MICS, MICS), MICS)
                x_re = spec_ref[tile, rows, :]
                x_im = spec_ref[TILES + tile, rows, :]
                pairs = [x_re * x_re + x_im * x_im]
                for shift in range(1, MICS // 2 + 1):
                    y_re = pltpu.roll(x_re, MICS - shift, 0)
                    y_im = pltpu.roll(x_im, MICS - shift, 0)
                    pairs.append(x_re * y_re + x_im * y_im)
                    pairs.append(x_im * y_re - x_re * y_im)
                out = []
                for k in range(2):
                    w = jnp.broadcast_to(weights[k][frame : frame + 1], (MICS, LANES))
                    out.extend(sums[k * len(pairs) + i] + w * pair for i, pair in enumerate(pairs))
                sums = tuple(out)
            return sums

        zero = jnp.zeros((MICS, LANES), jnp.float32)
        sums = lax.fori_loop(0, frames // MICS, add_frames, (zero,) * 18)
        for k in range(2):
            own = sums[9 * k : 9 * k + 9]
            kept = list(own[:7]) + [jnp.where(low, own[7], own[8])]
            for i, value in enumerate(kept):
                first = tile * STATS + (k * MICS + i) * MICS
                stats_ref[first : first + MICS, :] = value


def columns_of(kept, sub):
    low = sub < MICS // 2
    diag_re = [kept[0], kept[1], kept[3], kept[5]]
    diag_im = [jnp.zeros_like(kept[0]), kept[2], kept[4], kept[6]]
    turned = pltpu.roll(kept[7], MICS // 2, 0)
    diag_re.append(jnp.where(low, kept[7], turned))
    diag_im.append(jnp.where(low, -turned, kept[7]))
    for shift in range(MICS // 2 + 1, MICS):
        diag_re.append(pltpu.roll(diag_re[MICS - shift], MICS - shift, 0))
        diag_im.append(-pltpu.roll(diag_im[MICS - shift], MICS - shift, 0))
    columns = []
    for n in range(MICS):
        re, im = diag_re[n], diag_im[n]
        for m in range(1, MICS):
            re = jnp.where(sub == m, diag_re[(n - m) % MICS], re)
            im = jnp.where(sub == m, diag_im[(n - m) % MICS], im)
        columns.append((re, im))
    return columns


def beams_of(stats, ref_mic):
    sub = lax.broadcasted_iota(jnp.int32, stats[0].shape, 0)
    answer = columns_of(stats[:MICS], sub)
    matrix = columns_of(stats[MICS:], sub)
    spread = jnp.sum(stats[MICS], axis=0, keepdims=True)
    ridge = loading * spread / MICS + epsilon
    matrix = [(jnp.where(sub == n, re + ridge, re), im) for n, (re, im) in enumerate(matrix)]
    for pivot in range(MICS):
        col_re, col_im = matrix[pivot]
        pivot_re = col_re[pivot : pivot + 1]
        pivot_im = col_im[pivot : pivot + 1]
        modulus = pivot_re * pivot_re + pivot_im * pivot_im
        inverse_re = pivot_re / modulus
        inverse_im = -pivot_im / modulus

        def eliminated(column):
            re, im = column
            row_re, row_im = re[pivot : pivot + 1], im[pivot : pivot + 1]
            lead_re = row_re * inverse_re - row_im * inverse_im
            lead_im = row_re * inverse_im + row_im * inverse_re
            return (
                jnp.where(sub == pivot, lead_re, re - (col_re * lead_re - col_im * lead_im)),
                jnp.where(sub == pivot, lead_im, im - (col_re * lead_im + col_im * lead_re)),
            )

        matrix = [eliminated(c) if n > pivot else c for n, c in enumerate(matrix)]
        answer = [eliminated(c) for c in answer]
    trace = answer[0][0][0:1]
    beam_re, beam_im = answer[0]
    for n in range(1, MICS):
        trace = trace + answer[n][0][n : n + 1]
        beam_re = jnp.where(ref_mic == n, answer[n][0], beam_re)
        beam_im = jnp.where(ref_mic == n, answer[n][1], beam_im)
    scale = 1.0 / (trace + epsilon)
    return beam_re * scale, beam_im * scale


def stem_kernel(frames, stats_ref, spec_ref, valid_ref, ref_mic_ref, bank_ref, conv1_w_ref, conv1_b_ref, conv2_w_ref, conv2_b_ref, proj_w_ref, proj_b_ref, out_ref, power_ref, logmel_ref):
    position = lax.axis_index("tm")
    valid = valid_ref[0]
    quarter = frames // 4
    groups = power_ref.shape[0] // MICS
    for tile in range(TILES):
        kept = [stats_ref[tile * STATS + i * MICS : tile * STATS + (i + 1) * MICS, :] for i in range(2 * MICS)]
        beam_re, beam_im = beams_of(kept, ref_mic_ref[0])
        at_re = slice(tile * LANES, (tile + 1) * LANES)
        for group in range(groups):
            sum_re = sum_im = None
            for m in range(MICS):
                rows = pl.ds(group * MICS * MICS + m, MICS, stride=MICS)
                x_re, x_im = spec_ref[tile, rows, :], spec_ref[TILES + tile, rows, :]
                b_re, b_im = beam_re[m : m + 1], beam_im[m : m + 1]
                part_re = b_re * x_re + b_im * x_im
                part_im = b_re * x_im - b_im * x_re
                sum_re = part_re if sum_re is None else sum_re + part_re
                sum_im = part_im if sum_im is None else sum_im + part_im
            power_ref[group * MICS : (group + 1) * MICS, at_re] = sum_re * sum_re + sum_im * sum_im
    mel = jnp.dot(power_ref[...], bank_ref[...], precision=lax.Precision.HIGHEST, preferred_element_type=jnp.float32)
    time = position * frames - HALO + lax.broadcasted_iota(jnp.int32, (power_ref.shape[0], 1), 0)
    live = (time >= 0) & (time < valid)
    logmel = jnp.where(live, jnp.log(mel + epsilon), 0.0)
    logmel = logmel.astype(jnp.bfloat16).astype(jnp.float32)
    for half in range(2):
        logmel_ref[half] = logmel[:, half * LANES : (half + 1) * LANES]

    q_first = (MELS - 3) // 2 + 1
    q_second = (q_first - 3) // 2 + 1
    order = list(range(0, q_first, 2)) + list(range(1, q_first, 2))
    evens = (q_first + 1) // 2
    lane = lax.broadcasted_iota(jnp.int32, (quarter, LANES), 1)
    row = lax.broadcasted_iota(jnp.int32, (quarter, 1), 0)
    windows = []
    for tap in range(3):
        packs = []
        for half in range(2):
            rows = [logmel_ref[half, pl.ds(2 * tap + a, quarter, stride=4), :] for a in range(3)]
            packs.append(jnp.where(lane < SPAN, rows[0], jnp.where(lane < 2 * SPAN, rows[1], rows[2])))
        patches = []
        for q in order:
            half, shift = (0, 2 * q) if q < 20 else (1, 2 * q - 40)
            patches.append(packs[half] if shift == 0 else pltpu.roll(packs[half], LANES - shift, 1))
        patches = jnp.concatenate(patches, axis=0).astype(jnp.bfloat16)
        layer = jnp.dot(patches, conv1_w_ref[...], preferred_element_type=jnp.float32) + conv1_b_ref[...]
        layer = jnp.maximum(layer, 0.0)
        if tap == 0:
            keep = jnp.concatenate([row + 2 * quarter * position >= 1] * q_first, axis=0)
            layer = jnp.where(keep, layer, 0.0)
        layer = layer.astype(jnp.bfloat16)
        count = quarter * q_second
        windows.append(layer[:count])
        windows.append(layer[quarter * evens : quarter * evens + count])
        windows.append(layer[quarter : quarter + count])
    second = jnp.dot(jnp.concatenate(windows, axis=1), conv2_w_ref[...], preferred_element_type=jnp.float32)
    second = jnp.maximum(second + conv2_b_ref[...], 0.0).astype(jnp.bfloat16)
    flat = jnp.concatenate([second[quarter * r : quarter * (r + 1)] for r in range(q_second)], axis=1)
    features = jnp.dot(flat, proj_w_ref[...], preferred_element_type=jnp.float32) + proj_b_ref[...]
    features = jnp.where(position * frames + 4 * row < valid, features, 0.0)
    out_ref[0] = features.astype(jnp.bfloat16)


def summed(block, axis):
    size = lax.axis_size(axis)
    if size & (size - 1):
        return lax.psum(block, axis)
    step = 1
    while step < size:
        block = block + lax.ppermute(block, axis, [(i, i ^ step) for i in range(size)])
        step *= 2
    return block


def per_device(waveform, masks, valid, ref_mic, conv1_w, conv1_b, conv2_w, conv2_b, proj_w, proj_b):
    frames = masks.shape[1]
    channels = conv1_w.shape[1]
    width = proj_w.shape[1]
    rows = -(-(frames + HALO) // MICS) * MICS
    prev_rim = passed_along(waveform[:, -LEAD:], "tm", 1)
    next_rim = passed_along(waveform[:, :TAIL], "tm", -1)
    vmem = pl.BlockSpec(memory_space=pltpu.VMEM)
    smem = pl.BlockSpec(memory_space=pltpu.SMEM)
    params = pltpu.CompilerParams(vmem_limit_bytes=48 * 1024 * 1024)
    spec, stats = pl.pallas_call(
        functools.partial(stats_kernel, frames),
        out_shape=(
            jax.ShapeDtypeStruct((2 * TILES, rows * MICS, LANES), jnp.float32),
            jax.ShapeDtypeStruct((TILES * STATS, LANES), jnp.float32),
        ),
        in_specs=[vmem, vmem, vmem, vmem, smem, vmem],
        out_specs=(vmem, vmem),
        scratch_shapes=[
            pltpu.VMEM((rows * MICS, NFFT), jnp.float32),
            pltpu.VMEM((2, frames, PAD_BINS), jnp.float32),
        ],
        compiler_params=params,
        name="stats",
    )(prev_rim, waveform, next_rim, masks, valid, dft_table())
    stats = summed(stats, "tm")
    return pl.pallas_call(
        functools.partial(stem_kernel, frames),
        out_shape=jax.ShapeDtypeStruct((1, frames // 4, width), jnp.bfloat16),
        in_specs=[vmem, vmem, smem, smem] + [vmem] * 7,
        out_specs=vmem,
        scratch_shapes=[
            pltpu.VMEM((rows, PAD_BINS), jnp.float32),
            pltpu.VMEM((2, rows, LANES), jnp.float32),
        ],
        compiler_params=params,
        name="stem",
    )(
        stats,
        spec,
        valid,
        ref_mic,
        packed_mel_bank(),
        packed_conv1(conv1_w),
        conv1_b[None],
        conv2_w.reshape(-1, channels),
        conv2_b[None],
        proj_w,
        proj_b[None],
    )


def solution(mesh):
    return jax.shard_map(
        per_device,
        mesh=mesh,
        in_specs=(
            P(None, ("meet", "tm")),
            P(None, ("meet", "tm"), None),
            P("meet"),
            P("meet"),
            P(),
            P(),
            P(),
            P(),
            P(),
            P(),
        ),
        out_specs=P(None, ("meet", "tm"), None),
        check_vma=False,
    )
```

profile of v0, /device:TPU:0, one launch (start us, length us, event | category | flops | bytes accessed | tf_op | source)
XLA Modules:
  0.0 51.6 jit_solution(15713073102761705904)
XLA Ops:
  0.0 0.7 %slice.15 = bf16[8,512]{1,0:T(8,128)(2,1)S(1)} slice(bf16[8,10240]{1,0:T(8,128)(2,1)} %wave_ref.1), slice={[0:8], [9728:10240]} | slice | bytes 16384 | tf_op jit(solution)/shard_map/slice | solution.py:274
  0.7 2.3 %collective-permute-start = (bf16[8,512]{1,0:T(8,128)(2,1)S(1)}, bf16[8,512]{1,0:T(8,128)(2,1)S(1)}, u32[]{:S(2)}, u32[]{:S(2)}) collective-permute-start(bf16[8,512]{1,0:T(8,128)(2,1)S(1)} %slice.15), channel_id=1, source_target_pairs={{0,1},{1,2},{2,3},{3,4},{4,5},{5,6},{6,7},{7,8},{8,9},{9,10},{10,1... | collective-permute-start | bytes 24584 | tf_op jit(solution)/shard_map/ppermute | solution.py:34
  3.1 0.7 %slice.16 = bf16[8,384]{1,0:T(8,128)(2,1)S(1)} slice(bf16[8,10240]{1,0:T(8,128)(2,1)} %wave_ref.1), slice={[0:8], [0:384]} | slice | bytes 12288 | tf_op jit(solution)/shard_map/slice | solution.py:275
  3.8 1.3 %collective-permute-start.1 = (bf16[8,384]{1,0:T(8,128)(2,1)S(1)}, bf16[8,384]{1,0:T(8,128)(2,1)S(1)}, u32[]{:S(2)}, u32[]{:S(2)}) collective-permute-start(bf16[8,384]{1,0:T(8,128)(2,1)S(1)} %slice.16), channel_id=1, source_target_pairs={{1,0},{2,1},{3,2},{4,3},{5,4},{6,5},{7,6},{8,7},{9,8},{10,9},{11,1... | collective-permute-start | bytes 18440 | tf_op jit(solution)/shard_map/ppermute | solution.py:34
  5.1 0.0 copy-start.8
  5.7 0.0 copy-start
  5.7 3.2 %collective-permute-done.1.next_ref = bf16[8,384]{1,0:T(8,128)(2,1)S(1)} collective-permute-done((bf16[8,384]{1,0:T(8,128)(2,1)S(1)}, bf16[8,384]{1,0:T(8,128)(2,1)S(1)}, u32[]{:S(2)}, u32[]{:S(2)}) %collective-permute-start.1) | collective-permute-done | bytes 6176 | tf_op jit(solution)/shard_map/ppermute | solution.py:34
  8.9 0.0 collective-permute-done.prev_ref
  9.0 1.1 %copy-done.4 = bf16[512,768]{1,0:T(8,128)(2,1)S(1)} copy-done((bf16[512,768]{1,0:T(8,128)(2,1)S(1)}, bf16[512,768]{1,0:T(8,128)(2,1)}, u32[]{:S(2)}) %copy-start.4) | copy-done | bytes 786456
  10.1 0.9 %copy-done.6 = s32[2,64,257]{2,1,0:T(8,128)S(1)} copy-done((s32[2,64,257]{2,1,0:T(8,128)S(1)}, s32[2,64,257]{2,1,0:T(8,128)}, u32[]{:S(2)}) %copy-start.6) | copy-done | bytes 131608
  11.0 0.9 %copy-done.7 = bf16[8,10240]{1,0:T(8,128)(2,1)S(1)} copy-done((bf16[8,10240]{1,0:T(8,128)(2,1)S(1)}, bf16[8,10240]{1,0:T(8,128)(2,1)}, u32[]{:S(2)}) %copy-start.7) | copy-done | bytes 163864
  11.9 2.6 %stats.1 = (f32[6,576,128]{2,1,0:T(8,128)S(1)}, f32[384,128]{1,0:T(8,128)S(1)}) custom-call(bf16[8,512]{1,0:T(8,128)(2,1)S(1)} %collective-permute-done.prev_ref, bf16[8,10240]{1,0:T(8,128)(2,1)S(1)} %copy-done.7, bf16[8,384]{1,0:T(8,128)(2,1)S(1)} %collective-permute-done.1.next_ref, s32[2,64,257]{2,1,0:T(8,128)S(1)} %copy-done.6, s32[1]{0:T(128)S(6)} %copy.13.valid_ref, ...), custom_call_target="tpu_custom_call" | custom-call | tf_op jit(solution)/shard_map/stats/pallas_call | solution.py:279
  14.5 0.0 copy-start.1
  14.6 1.2 %copy-done.1 = f32[6,576,128]{2,1,0:T(8,128)} copy-done((f32[6,576,128]{2,1,0:T(8,128)}, f32[6,576,128]{2,1,0:T(8,128)S(1)}, u32[]{:S(2)}) %copy-start.1) | copy-done | bytes 1769496
  15.8 2.4 %collective-permute-start.2 = (f32[384,128]{1,0:T(8,128)S(1)}, f32[384,128]{1,0:T(8,128)S(1)}, u32[]{:S(2)}, u32[]{:S(2)}) collective-permute-start(f32[384,128]{1,0:T(8,128)S(1)} %get-tuple-element.7), channel_id=1, source_target_pairs={{0,1},{1,0},{2,3},{3,2},{4,5},{5,4},{6,7},{7,6},{8,9},{9,8},{10,11... | collective-permute-start | bytes 589832 | tf_op jit(solution)/shard_map/ppermute | solution.py:264
  18.2 1.1 %collective-permute-done.2 = f32[384,128]{1,0:T(8,128)S(1)} collective-permute-done((f32[384,128]{1,0:T(8,128)S(1)}, f32[384,128]{1,0:T(8,128)S(1)}, u32[]{:S(2)}, u32[]{:S(2)}) %collective-permute-start.2) | collective-permute-done | bytes 196640 | tf_op jit(solution)/shard_map/ppermute | solution.py:264
  19.3 2.5 %collective-permute-start.3 = (f32[384,128]{1,0:T(8,128)S(1)}, f32[384,128]{1,0:T(8,128)S(1)}, u32[]{:S(2)}, u32[]{:S(2)}) collective-permute-start(f32[384,128]{1,0:T(8,128)S(1)} %add.12), channel_id=1, source_target_pairs={{0,2},{1,3},{2,0},{3,1},{4,6},{5,7},{6,4},{7,5},{8,10},{9,11},{10,... | collective-permute-start | bytes 589832 | tf_op jit(solution)/shard_map/ppermute | solution.py:264
  21.8 5.4 %collective-permute-done.3 = f32[384,128]{1,0:T(8,128)S(1)} collective-permute-done((f32[384,128]{1,0:T(8,128)S(1)}, f32[384,128]{1,0:T(8,128)S(1)}, u32[]{:S(2)}, u32[]{:S(2)}) %collective-permute-start.3) | collective-permute-done | bytes 196640 | tf_op jit(solution)/shard_map/ppermute | solution.py:264
  27.2 1.6 %collective-permute-start.4 = (f32[384,128]{1,0:T(8,128)S(1)}, f32[384,128]{1,0:T(8,128)S(1)}, u32[]{:S(2)}, u32[]{:S(2)}) collective-permute-start(f32[384,128]{1,0:T(8,128)S(1)} %add.13), channel_id=1, source_target_pairs={{0,4},{1,5},{2,6},{3,7},{4,0},{5,1},{6,2},{7,3},{8,12},{9,13},{10,... | collective-permute-start | bytes 589832 | tf_op jit(solution)/shard_map/ppermute | solution.py:264
  29.5 4.4 %collective-permute-done.4 = f32[384,128]{1,0:T(8,128)S(1)} collective-permute-done((f32[384,128]{1,0:T(8,128)S(1)}, f32[384,128]{1,0:T(8,128)S(1)}, u32[]{:S(2)}, u32[]{:S(2)}) %collective-permute-start.4) | collective-permute-done | bytes 196640 | tf_op jit(solution)/shard_map/ppermute | solution.py:264
  33.9 2.7 %collective-permute-start.5 = (f32[384,128]{1,0:T(8,128)S(1)}, f32[384,128]{1,0:T(8,128)S(1)}, u32[]{:S(2)}, u32[]{:S(2)}) collective-permute-start(f32[384,128]{1,0:T(8,128)S(1)} %add.14), channel_id=1, source_target_pairs={{0,8},{1,9},{2,10},{3,11},{4,12},{5,13},{6,14},{7,15},{8,0},{9,1},... | collective-permute-start | bytes 589832 | tf_op jit(solution)/shard_map/ppermute | solution.py:264
  36.6 0.0 copy-done.11
  36.6 0.5 concatenate.3.conv1_w_ref
  37.1 7.7 %collective-permute-done.5 = f32[384,128]{1,0:T(8,128)S(1)} collective-permute-done((f32[384,128]{1,0:T(8,128)S(1)}, f32[384,128]{1,0:T(8,128)S(1)}, u32[]{:S(2)}, u32[]{:S(2)}) %collective-permute-start.5) | collective-permute-done | bytes 196640 | tf_op jit(solution)/shard_map/ppermute | solution.py:264
  44.8 0.0 copy-done.8
  44.9 0.0 copy-done
  44.9 0.0 copy-done.5
  44.9 0.0 copy-done.9
  44.9 0.0 copy-done.10
  44.9 1.5 %copy-done.2 = f32[6,576,128]{2,1,0:T(8,128)S(1)} copy-done((f32[6,576,128]{2,1,0:T(8,128)S(1)}, f32[6,576,128]{2,1,0:T(8,128)}, u32[]{:S(2)}) %copy-start.2) | copy-done | bytes 1769496
  46.4 1.3 %copy-done.3 = bf16[9,256,256]{2,1,0:T(8,128)(2,1)S(1)} copy-done((bf16[9,256,256]{2,1,0:T(8,128)(2,1)S(1)}, bf16[9,256,256]{2,1,0:T(8,128)(2,1)}, u32[]{:S(2)}) %copy-start.3) | copy-done | bytes 1179672
  47.6 4.0 %stem.1 = bf16[1,16,256]{2,1,0:T(8,128)(2,1)} custom-call(f32[384,128]{1,0:T(8,128)S(1)} %add.15.stats_ref, f32[6,576,128]{2,1,0:T(8,128)S(1)} %copy-done.2, s32[1]{0:T(128)S(6)} %copy.13.valid_ref, s32[1]{0:T(128)S(6)} %copy.14.ref_mic_ref, f32[384,256]{1,0:T(8,128)S(1)} %copy-done.5, bf16[128,256]{1,0:T(8,128)(2,1)S(1)} %concatenate.3.conv1_w_ref, ...), custom_call_target="tpu_custom_call" | custom-call | tf_op jit(solution)/shard_map/stem/pallas_call | solution.py:295
  (16 shorter events, 0.1 us)
Async XLA Ops:
  0.0 36.6 %copy-start.11 = (bf16[9,256]{1,0:T(8,128)(2,1)S(1)}, bf16[9,256]{1,0:T(8,128)(2,1)}, u32[]{:S(2)}) copy-start(bf16[9,256]{1,0:T(8,128)(2,1)} %param.16) | copy-start | bytes 13828
  0.7 8.2 %collective-permute-start = (bf16[8,512]{1,0:T(8,128)(2,1)S(1)}, bf16[8,512]{1,0:T(8,128)(2,1)S(1)}, u32[]{:S(2)}, u32[]{:S(2)}) collective-permute-start(bf16[8,512]{1,0:T(8,128)(2,1)S(1)} %slice.15), channel_id=1, source_target_pairs={{0,1},{1,2},{2,3},{3,4},{4,5},{5,6},{6,7},{7,8},{8,9},{9,10},{10,1... | collective-permute-start | bytes 24584 | tf_op jit(solution)/shard_map/ppermute | solution.py:34
  3.8 5.2 %collective-permute-start.1 = (bf16[8,384]{1,0:T(8,128)(2,1)S(1)}, bf16[8,384]{1,0:T(8,128)(2,1)S(1)}, u32[]{:S(2)}, u32[]{:S(2)}) collective-permute-start(bf16[8,384]{1,0:T(8,128)(2,1)S(1)} %slice.16), channel_id=1, source_target_pairs={{1,0},{2,1},{3,2},{4,3},{5,4},{6,5},{7,6},{8,7},{9,8},{10,9},{11,1... | collective-permute-start | bytes 18440 | tf_op jit(solution)/shard_map/ppermute | solution.py:34
  5.1 39.8 %copy-start.8 = (f32[256]{0:T(256)S(1)}, f32[256]{0:T(256)}, u32[]{:S(2)}) copy-start(f32[256]{0:T(256)} %param.17) | copy-start | bytes 3076
  5.7 39.1 %copy-start = (bf16[4864,256]{1,0:T(8,128)(2,1)S(1)}, bf16[4864,256]{1,0:T(8,128)(2,1)}, u32[]{:S(2)}) copy-start(bf16[4864,256]{1,0:T(8,128)(2,1)} %proj_w_ref.1) | copy-start | bytes 7471108
  9.0 1.1 %copy-start.4 = (bf16[512,768]{1,0:T(8,128)(2,1)S(1)}, bf16[512,768]{1,0:T(8,128)(2,1)}, u32[]{:S(2)}) copy-start(bf16[512,768]{1,0:T(8,128)(2,1)} %constant.11.table_ref) | copy-start | bytes 2359300
  10.1 0.9 %copy-start.6 = (s32[2,64,257]{2,1,0:T(8,128)S(1)}, s32[2,64,257]{2,1,0:T(8,128)}, u32[]{:S(2)}) copy-start(s32[2,64,257]{2,1,0:T(8,128)} %masks_ref.1) | copy-start | bytes 394756
  11.0 0.9 %copy-start.7 = (bf16[8,10240]{1,0:T(8,128)(2,1)S(1)}, bf16[8,10240]{1,0:T(8,128)(2,1)}, u32[]{:S(2)}) copy-start(bf16[8,10240]{1,0:T(8,128)(2,1)} %wave_ref.1) | copy-start | bytes 491524
  11.9 32.9 %copy-start.5 = (f32[384,256]{1,0:T(8,128)S(1)}, f32[384,256]{1,0:T(8,128)}, u32[]{:S(2)}) copy-start(f32[384,256]{1,0:T(8,128)} %constant.8.clone.bank_ref) | copy-start | bytes 1179652
  11.9 32.9 %copy-start.9 = (f32[256]{0:T(256)S(1)}, f32[256]{0:T(256)}, u32[]{:S(2)}) copy-start(f32[256]{0:T(256)} %param.19) | copy-start | bytes 3076
  11.9 32.9 %copy-start.10 = (f32[256]{0:T(256)S(1)}, f32[256]{0:T(256)}, u32[]{:S(2)}) copy-start(f32[256]{0:T(256)} %param.21) | copy-start | bytes 3076
  14.5 1.3 %copy-start.1 = (f32[6,576,128]{2,1,0:T(8,128)}, f32[6,576,128]{2,1,0:T(8,128)S(1)}, u32[]{:S(2)}) copy-start(f32[6,576,128]{2,1,0:T(8,128)S(1)} %get-tuple-element.8.spec_ref) | copy-start | bytes 5308420
  15.8 3.5 %collective-permute-start.2 = (f32[384,128]{1,0:T(8,128)S(1)}, f32[384,128]{1,0:T(8,128)S(1)}, u32[]{:S(2)}, u32[]{:S(2)}) collective-permute-start(f32[384,128]{1,0:T(8,128)S(1)} %get-tuple-element.7), channel_id=1, source_target_pairs={{0,1},{1,0},{2,3},{3,2},{4,5},{5,4},{6,7},{7,6},{8,9},{9,8},{10,11... | collective-permute-start | bytes 589832 | tf_op jit(solution)/shard_map/ppermute | solution.py:264
  19.3 7.9 %collective-permute-start.3 = (f32[384,128]{1,0:T(8,128)S(1)}, f32[384,128]{1,0:T(8,128)S(1)}, u32[]{:S(2)}, u32[]{:S(2)}) collective-permute-start(f32[384,128]{1,0:T(8,128)S(1)} %add.12), channel_id=1, source_target_pairs={{0,2},{1,3},{2,0},{3,1},{4,6},{5,7},{6,4},{7,5},{8,10},{9,11},{10,... | collective-permute-start | bytes 589832 | tf_op jit(solution)/shard_map/ppermute | solution.py:264
  27.2 6.7 %collective-permute-start.4 = (f32[384,128]{1,0:T(8,128)S(1)}, f32[384,128]{1,0:T(8,128)S(1)}, u32[]{:S(2)}, u32[]{:S(2)}) collective-permute-start(f32[384,128]{1,0:T(8,128)S(1)} %add.13), channel_id=1, source_target_pairs={{0,4},{1,5},{2,6},{3,7},{4,0},{5,1},{6,2},{7,3},{8,12},{9,13},{10,... | collective-permute-start | bytes 589832 | tf_op jit(solution)/shard_map/ppermute | solution.py:264
  33.9 10.9 %collective-permute-start.5 = (f32[384,128]{1,0:T(8,128)S(1)}, f32[384,128]{1,0:T(8,128)S(1)}, u32[]{:S(2)}, u32[]{:S(2)}) collective-permute-start(f32[384,128]{1,0:T(8,128)S(1)} %add.14), channel_id=1, source_target_pairs={{0,8},{1,9},{2,10},{3,11},{4,12},{5,13},{6,14},{7,15},{8,0},{9,1},... | collective-permute-start | bytes 589832 | tf_op jit(solution)/shard_map/ppermute | solution.py:264
  44.9 1.5 %copy-start.2 = (f32[6,576,128]{2,1,0:T(8,128)S(1)}, f32[6,576,128]{2,1,0:T(8,128)}, u32[]{:S(2)}) copy-start(f32[6,576,128]{2,1,0:T(8,128)} %copy-done.1) | copy-start | bytes 5308420
  46.4 1.3 %copy-start.3 = (bf16[9,256,256]{2,1,0:T(8,128)(2,1)S(1)}, bf16[9,256,256]{2,1,0:T(8,128)(2,1)}, u32[]{:S(2)}) copy-start(bf16[9,256,256]{2,1,0:T(8,128)(2,1)} %param.18) | copy-start | bytes 3538948
where the time goes:
time: 52 us; the launch traced here: 51.6 us
  waiting for transfers between devices  21.8 us (42%)
  starting transfers between devices  12.8 us (25%)
  local copies, waits for them, and re-layouts  8.88 us (17%)
  Pallas kernels  6.6 us (13%)
  between operations  1.45 us (3%)
    ppermute x4, waiting for transfers between devices, summed(): lax.ppermute(block, axis, [(i, i ^ step) for i in range(size)])  18.6 us
    ppermute x4, starting transfers between devices, summed(): lax.ppermute(block, axis, [(i, i ^ step) for i in range(size)])  9.18 us
    unnamed x24, local copies, waits for them, and re-layouts  6.99 us
    pallas_call x1, Pallas kernels, per_device(): pl.pallas_call(functools.partial(stem_kernel, frames), out_shape=jax.Shap...  4 us
    ppermute x2, starting transfers between devices, passed_along(): return lax.ppermute(block, axis, route)  3.62 us
    ppermute x2, waiting for transfers between devices, passed_along(): return lax.ppermute(block, axis, route)  3.22 us
    pallas_call x1, Pallas kernels, per_device(): pl.pallas_call(functools.partial(stats_kernel, frames), out_shape=(jax.Sh...  2.6 us
  transfers between devices with their start and end apart: 6, of which 5 were waited for; matrix products, arithmetic and copies ran while one was open for 2% of the time, Pallas kernels for 0%

commit v1 on v0

--- a/solution.py
+++ b/solution.py
@@ -75,7 +75,7 @@
     return jnp.concatenate(rows, axis=0)
 
 
-def stats_kernel(frames, prev_ref, wave_ref, next_ref, masks_ref, valid_ref, table_ref, spec_ref, stats_ref, framed_ref, weight_ref):
+def stats_kernel(frames, prev_ref, wave_ref, next_ref, masks_ref, valid_ref, table_ref, spec_ref, mine_ref, theirs_ref, framed_ref, weight_ref):
     position = lax.axis_index("tm")
     span = frames + HALO
     extended = jnp.concatenate(
@@ -97,17 +97,20 @@
 
     row = lax.broadcasted_iota(jnp.int32, (frames, 1), 0)
     live = jnp.where(position * frames + row < valid_ref[0], 1.0 / 255.0, 0.0)
-    weight_ref[:, :, PAD_BINS - LANES :] = jnp.zeros((2, frames, LANES), jnp.float32)
+    weight_ref[TILES - 1] = jnp.zeros((2, frames, LANES), jnp.float32)
     for k in range(2):
-        weight_ref[k, :, :BINS] = masks_ref[k].astype(jnp.float32) * live
+        weight = masks_ref[k].astype(jnp.float32) * live
+        for tile in range(TILES):
+            kept_lanes = min(LANES, BINS - tile * LANES)
+            weight_ref[tile, k, :, :kept_lanes] = weight[:, tile * LANES : tile * LANES + kept_lanes]
 
     low = lax.broadcasted_iota(jnp.int32, (MICS, LANES), 0) < MICS // 2
-    for tile in range(TILES):
-        at_re = slice(tile * LANES, (tile + 1) * LANES)
+    core = position % 2
+    for slot, tile in enumerate((core, 1 - core, TILES - 1)):
 
         def add_frames(group, sums):
             first = pl.multiple_of(group * MICS, MICS)
-            weights = [weight_ref[k, pl.ds(first, MICS), at_re] for k in range(2)]
+            weights = [weight_ref[tile, k, pl.ds(first, MICS), :] for k in range(2)]
             for frame in range(MICS):
                 rows = pl.ds(pl.multiple_of((first + frame + HALO) * MICS, MICS), MICS)
                 x_re = spec_ref[tile, rows, :]
@@ -127,12 +130,19 @@
 
         zero = jnp.zeros((MICS, LANES), jnp.float32)
         sums = lax.fori_loop(0, frames // MICS, add_frames, (zero,) * 18)
+        kept = []
         for k in range(2):
             own = sums[9 * k : 9 * k + 9]
-            kept = list(own[:7]) + [jnp.where(low, own[7], own[8])]
-            for i, value in enumerate(kept):
-                first = tile * STATS + (k * MICS + i) * MICS
-                stats_ref[first : first + MICS, :] = value
+            kept.extend(list(own[:7]) + [jnp.where(low, own[7], own[8])])
+        kept = jnp.concatenate(kept, axis=0)
+        if slot == 0:
+            mine_ref[:STATS, :] = kept
+        elif slot == 1:
+            theirs_ref[:STATS, :] = kept
+        else:
+            last_bin = jnp.transpose(kept)[:MICS]
+            mine_ref[STATS:, :] = last_bin
+            theirs_ref[STATS:, :] = last_bin
 
 
 def columns_of(kept, sub):
@@ -192,16 +202,25 @@
     return beam_re * scale, beam_im * scale
 
 
-def stem_kernel(frames, stats_ref, spec_ref, valid_ref, ref_mic_ref, bank_ref, conv1_w_ref, conv1_b_ref, conv2_w_ref, conv2_b_ref, proj_w_ref, proj_b_ref, out_ref, power_ref, logmel_ref):
+def solve_kernel(stats_ref, ref_mic_ref, beam_ref, last_ref):
+    blank = jnp.zeros((LANES - MICS, LANES), jnp.float32)
+    last_bin = jnp.transpose(jnp.concatenate([stats_ref[STATS:, :], blank], axis=0))
+    for out_ref, stats in ((beam_ref, stats_ref[:STATS, :]), (last_ref, last_bin)):
+        kept = [stats[i * MICS : (i + 1) * MICS] for i in range(2 * MICS)]
+        beam_re, beam_im = beams_of(kept, ref_mic_ref[0])
+        out_ref[:MICS, :] = beam_re
+        out_ref[MICS:, :] = beam_im
+
+
+def stem_kernel(frames, mine_ref, theirs_ref, last_ref, spec_ref, valid_ref, bank_ref, conv1_w_ref, conv1_b_ref, conv2_w_ref, conv2_b_ref, proj_w_ref, proj_b_ref, out_ref, power_ref, logmel_ref):
     position = lax.axis_index("tm")
     valid = valid_ref[0]
     quarter = frames // 4
-    groups = power_ref.shape[0] // MICS
-    for tile in range(TILES):
-        kept = [stats_ref[tile * STATS + i * MICS : tile * STATS + (i + 1) * MICS, :] for i in range(2 * MICS)]
-        beam_re, beam_im = beams_of(kept, ref_mic_ref[0])
-        at_re = slice(tile * LANES, (tile + 1) * LANES)
-        for group in range(groups):
+    span = power_ref.shape[1]
+    core = position % 2
+    for beam_ref, tile in ((mine_ref, core), (theirs_ref, 1 - core), (last_ref, TILES - 1)):
+        beam_re, beam_im = beam_ref[:MICS, :], beam_ref[MICS:, :]
+        for group in range(span // MICS):
             sum_re = sum_im = None
             for m in range(MICS):
                 rows = pl.ds(group * MICS * MICS + m, MICS, stride=MICS)
@@ -211,9 +230,10 @@
                 part_im = b_re * x_im - b_im * x_re
                 sum_re = part_re if sum_re is None else sum_re + part_re
                 sum_im = part_im if sum_im is None else sum_im + part_im
-            power_ref[group * MICS : (group + 1) * MICS, at_re] = sum_re * sum_re + sum_im * sum_im
-    mel = jnp.dot(power_ref[...], bank_ref[...], precision=lax.Precision.HIGHEST, preferred_element_type=jnp.float32)
-    time = position * frames - HALO + lax.broadcasted_iota(jnp.int32, (power_ref.shape[0], 1), 0)
+            power_ref[tile, group * MICS : (group + 1) * MICS, :] = sum_re * sum_re + sum_im * sum_im
+    power = jnp.concatenate([power_ref[tile] for tile in range(TILES)], axis=1)
+    mel = jnp.dot(power, bank_ref[...], precision=lax.Precision.HIGHEST, preferred_element_type=jnp.float32)
+    time = position * frames - HALO + lax.broadcasted_iota(jnp.int32, (span, 1), 0)
     live = (time >= 0) & (time < valid)
     logmel = jnp.where(live, jnp.log(mel + epsilon), 0.0)
     logmel = logmel.astype(jnp.bfloat16).astype(jnp.float32)
@@ -255,13 +275,18 @@
     out_ref[0] = features.astype(jnp.bfloat16)
 
 
-def summed(block, axis):
+def flipped(block, axis, step):
+    size = lax.axis_size(axis)
+    return lax.ppermute(block, axis, [(i, i ^ step) for i in range(size)])
+
+
+def summed_over_chips(block, axis):
     size = lax.axis_size(axis)
     if size & (size - 1):
-        return lax.psum(block, axis)
-    step = 1
+        return lax.psum(block, axis, axis_index_groups=[list(range(c, size, 2)) for c in range(2)])
+    step = 2
     while step < size:
-        block = block + lax.ppermute(block, axis, [(i, i ^ step) for i in range(size)])
+        block = block + flipped(block, axis, step)
         step *= 2
     return block
 
@@ -275,39 +300,51 @@
     next_rim = passed_along(waveform[:, :TAIL], "tm", -1)
     vmem = pl.BlockSpec(memory_space=pltpu.VMEM)
     smem = pl.BlockSpec(memory_space=pltpu.SMEM)
-    params = pltpu.CompilerParams(vmem_limit_bytes=48 * 1024 * 1024)
-    spec, stats = pl.pallas_call(
+    params = pltpu.CompilerParams(vmem_limit_bytes=16 * 1024 * 1024)
+    spec, mine, theirs = pl.pallas_call(
         functools.partial(stats_kernel, frames),
         out_shape=(
             jax.ShapeDtypeStruct((2 * TILES, rows * MICS, LANES), jnp.float32),
-            jax.ShapeDtypeStruct((TILES * STATS, LANES), jnp.float32),
+            jax.ShapeDtypeStruct((STATS + MICS, LANES), jnp.float32),
+            jax.ShapeDtypeStruct((STATS + MICS, LANES), jnp.float32),
         ),
         in_specs=[vmem, vmem, vmem, vmem, smem, vmem],
-        out_specs=(vmem, vmem),
+        out_specs=(vmem, vmem, vmem),
         scratch_shapes=[
             pltpu.VMEM((rows * MICS, NFFT), jnp.float32),
-            pltpu.VMEM((2, frames, PAD_BINS), jnp.float32),
+            pltpu.VMEM((TILES, 2, frames, LANES), jnp.float32),
         ],
         compiler_params=params,
         name="stats",
     )(prev_rim, waveform, next_rim, masks, valid, dft_table())
-    stats = summed(stats, "tm")
+    stats = summed_over_chips(mine + flipped(theirs, "tm", 1), "tm")
+    beam = jax.ShapeDtypeStruct((2 * MICS, LANES), jnp.float32)
+    beam_mine, beam_last = pl.pallas_call(
+        solve_kernel,
+        out_shape=(beam, beam),
+        in_specs=[vmem, smem],
+        out_specs=(vmem, vmem),
+        compiler_params=params,
+        name="solve",
+    )(stats, ref_mic)
+    beam_theirs = flipped(beam_mine, "tm", 1)
     return pl.pallas_call(
         functools.partial(stem_kernel, frames),
         out_shape=jax.ShapeDtypeStruct((1, frames // 4, width), jnp.bfloat16),
-        in_specs=[vmem, vmem, smem, smem] + [vmem] * 7,
+        in_specs=[vmem] * 4 + [smem] + [vmem] * 7,
         out_specs=vmem,
         scratch_shapes=[
-            pltpu.VMEM((rows, PAD_BINS), jnp.float32),
+            pltpu.VMEM((TILES, rows, LANES), jnp.float32),
             pltpu.VMEM((2, rows, LANES), jnp.float32),
         ],
         compiler_params=params,
         name="stem",
     )(
-        stats,
+        beam_mine,
+        beam_theirs,
+        beam_last,
         spec,
         valid,
-        ref_mic,
         packed_mel_bank(),
         packed_conv1(conv1_w),
         conv1_b[None],

time: 52 us -> 40 us (0.77)
  waiting for transfers between devices: 21.8 us -> 12.2 us
  local copies, waits for them, and re-layouts: 8.88 us -> 6.67 us
    ppermute x4 -> x5, waiting for transfers between devices: 18.6 us -> 8.94 us  [flipped(): return lax.ppermute(block, axis, [(i, i ^ step) for i in range(size)])]
    unnamed x24 -> x20, local copies, waits for them, and re-layouts: 6.99 us -> 4.7 us
    pallas_call x1, Pallas kernels: 4 us -> 3.21 us  [per_device(): pl.pallas_call(functools.partial(stem_kernel, frames), out_shape=jax.Shap...]
    pallas_call x0 -> x1, Pallas kernels: none -> 0.59 us  [per_device(): pl.pallas_call(solve_kernel, out_shape=(beam, beam), in_specs=[vmem, smem...]
    ppermute x4 -> x5, starting transfers between devices: 9.18 us -> 9.27 us  [flipped(): return lax.ppermute(block, axis, [(i, i ^ step) for i in range(size)])]
  transfers between devices with their start and end apart: 6 -> 7, of which waited for: 5 -> 6; matrix products, arithmetic and copies ran while one was open for 2% -> 3% of each run, Pallas kernels for 0% -> 0%
where the time goes in v1:
time: 40 us; the launch traced here: 39.7 us
  starting transfers between devices  12.9 us (32%)
  waiting for transfers between devices  12.2 us (30%)
  local copies, waits for them, and re-layouts  6.67 us (17%)
  Pallas kernels  6.47 us (16%)
  between operations  1.42 us (4%)
    ppermute x5, starting transfers between devices, flipped(): return lax.ppermute(block, axis, [(i, i ^ step) for i in range(size)])  9.27 us
    ppermute x5, waiting for transfers between devices, flipped(): return lax.ppermute(block, axis, [(i, i ^ step) for i in range(size)])  8.94 us
    unnamed x20, local copies, waits for them, and re-layouts  4.7 us
    ppermute x2, starting transfers between devices, passed_along(): return lax.ppermute(block, axis, route)  3.62 us
    ppermute x2, waiting for transfers between devices, passed_along(): return lax.ppermute(block, axis, route)  3.25 us
    pallas_call x1, Pallas kernels, per_device(): pl.pallas_call(functools.partial(stem_kernel, frames), out_shape=jax.Shap...  3.21 us
    pallas_call x1, Pallas kernels, per_device(): pl.pallas_call(functools.partial(stats_kernel, frames), out_shape=(jax.Sh...  2.67 us
  transfers between devices with their start and end apart: 7, of which 6 were waited for; matrix products, arithmetic and copies ran while one was open for 3% of the time, Pallas kernels for 0%

profile of v1, /device:TPU:0, one launch (start us, length us, event | category | flops | bytes accessed | tf_op | source)
XLA Modules:
  0.0 39.7 jit_solution(10088573565018940531)
XLA Ops:
  0.0 0.8 %slice.15 = bf16[8,512]{1,0:T(8,128)(2,1)S(1)} slice(bf16[8,10240]{1,0:T(8,128)(2,1)} %wave_ref.1), slice={[0:8], [9728:10240]} | slice | bytes 16384 | tf_op jit(solution)/shard_map/slice | solution.py:299
  0.8 2.3 %collective-permute-start = (bf16[8,512]{1,0:T(8,128)(2,1)S(1)}, bf16[8,512]{1,0:T(8,128)(2,1)S(1)}, u32[]{:S(2)}, u32[]{:S(2)}) collective-permute-start(bf16[8,512]{1,0:T(8,128)(2,1)S(1)} %slice.15), channel_id=1, source_target_pairs={{0,1},{1,2},{2,3},{3,4},{4,5},{5,6},{6,7},{7,8},{8,9},{9,10},{10,1... | collective-permute-start | bytes 24584 | tf_op jit(solution)/shard_map/ppermute | solution.py:34
  3.1 0.7 %slice.16 = bf16[8,384]{1,0:T(8,128)(2,1)S(1)} slice(bf16[8,10240]{1,0:T(8,128)(2,1)} %wave_ref.1), slice={[0:8], [0:384]} | slice | bytes 12288 | tf_op jit(solution)/shard_map/slice | solution.py:300
  3.8 1.3 %collective-permute-start.1 = (bf16[8,384]{1,0:T(8,128)(2,1)S(1)}, bf16[8,384]{1,0:T(8,128)(2,1)S(1)}, u32[]{:S(2)}, u32[]{:S(2)}) collective-permute-start(bf16[8,384]{1,0:T(8,128)(2,1)S(1)} %slice.16), channel_id=1, source_target_pairs={{1,0},{2,1},{3,2},{4,3},{5,4},{6,5},{7,6},{8,7},{9,8},{10,9},{11,1... | collective-permute-start | bytes 18440 | tf_op jit(solution)/shard_map/ppermute | solution.py:34
  5.8 3.3 %collective-permute-done.1.next_ref = bf16[8,384]{1,0:T(8,128)(2,1)S(1)} collective-permute-done((bf16[8,384]{1,0:T(8,128)(2,1)S(1)}, bf16[8,384]{1,0:T(8,128)(2,1)S(1)}, u32[]{:S(2)}, u32[]{:S(2)}) %collective-permute-start.1) | collective-permute-done | bytes 6176 | tf_op jit(solution)/shard_map/ppermute | solution.py:34
  9.0 0.0 collective-permute-done.prev_ref
  9.0 1.1 %copy-done.2 = bf16[512,768]{1,0:T(8,128)(2,1)S(1)} copy-done((bf16[512,768]{1,0:T(8,128)(2,1)S(1)}, bf16[512,768]{1,0:T(8,128)(2,1)}, u32[]{:S(2)}) %copy-start.2) | copy-done | bytes 786456
  10.2 0.9 %copy-done.4 = s32[2,64,257]{2,1,0:T(8,128)S(1)} copy-done((s32[2,64,257]{2,1,0:T(8,128)S(1)}, s32[2,64,257]{2,1,0:T(8,128)}, u32[]{:S(2)}) %copy-start.4) | copy-done | bytes 131608
  11.1 0.9 %copy-done.5 = bf16[8,10240]{1,0:T(8,128)(2,1)S(1)} copy-done((bf16[8,10240]{1,0:T(8,128)(2,1)S(1)}, bf16[8,10240]{1,0:T(8,128)(2,1)}, u32[]{:S(2)}) %copy-start.5) | copy-done | bytes 163864
  12.0 0.0 copy-start.8
  12.0 2.7 %stats.1 = (f32[6,576,128]{2,1,0:T(8,128)S(1)}, f32[136,128]{1,0:T(8,128)S(1)}, f32[136,128]{1,0:T(8,128)S(1)}) custom-call(bf16[8,512]{1,0:T(8,128)(2,1)S(1)} %collective-permute-done.prev_ref, bf16[8,10240]{1,0:T(8,128)(2,1)S(1)} %copy-done.5, bf16[8,384]{1,0:T(8,128)(2,1)S(1)} %collective-permute-done.1.next_ref, s32[2,64,257]{2,1,0:T(8,128)S(1)} %copy-done.4, ...), custom_call_target="tpu_custom_call" | custom-call | tf_op jit(solution)/shard_map/stats/pallas_call | solution.py:304
  14.7 2.4 %collective-permute-start.2 = (f32[136,128]{1,0:T(8,128)S(1)}, f32[136,128]{1,0:T(8,128)S(1)}, u32[]{:S(2)}, u32[]{:S(2)}) collective-permute-start(f32[136,128]{1,0:T(8,128)S(1)} %get-tuple-element.11), channel_id=1, source_target_pairs={{0,1},{1,0},{2,3},{3,2},{4,5},{5,4},{6,7},{7,6},{8,9},{9,8},{10,11... | collective-permute-start | bytes 208904 | tf_op jit(solution)/shard_map/ppermute | solution.py:280
  17.1 0.9 %collective-permute-done.2 = f32[136,128]{1,0:T(8,128)S(1)} collective-permute-done((f32[136,128]{1,0:T(8,128)S(1)}, f32[136,128]{1,0:T(8,128)S(1)}, u32[]{:S(2)}, u32[]{:S(2)}) %collective-permute-start.2) | collective-permute-done | bytes 69664 | tf_op jit(solution)/shard_map/ppermute | solution.py:280
  18.0 2.5 %collective-permute-start.3 = (f32[136,128]{1,0:T(8,128)S(1)}, f32[136,128]{1,0:T(8,128)S(1)}, u32[]{:S(2)}, u32[]{:S(2)}) collective-permute-start(f32[136,128]{1,0:T(8,128)S(1)} %add.12), channel_id=1, source_target_pairs={{0,2},{1,3},{2,0},{3,1},{4,6},{5,7},{6,4},{7,5},{8,10},{9,11},{10,... | collective-permute-start | bytes 208904 | tf_op jit(solution)/shard_map/ppermute | solution.py:280
  20.5 2.7 %collective-permute-done.3 = f32[136,128]{1,0:T(8,128)S(1)} collective-permute-done((f32[136,128]{1,0:T(8,128)S(1)}, f32[136,128]{1,0:T(8,128)S(1)}, u32[]{:S(2)}, u32[]{:S(2)}) %collective-permute-start.3) | collective-permute-done | bytes 69664 | tf_op jit(solution)/shard_map/ppermute | solution.py:280
  23.2 1.6 %collective-permute-start.4 = (f32[136,128]{1,0:T(8,128)S(1)}, f32[136,128]{1,0:T(8,128)S(1)}, u32[]{:S(2)}, u32[]{:S(2)}) collective-permute-start(f32[136,128]{1,0:T(8,128)S(1)} %add.13), channel_id=1, source_target_pairs={{0,4},{1,5},{2,6},{3,7},{4,0},{5,1},{6,2},{7,3},{8,12},{9,13},{10,... | collective-permute-start | bytes 208904 | tf_op jit(solution)/shard_map/ppermute | solution.py:280
  24.9 2.7 %collective-permute-done.4 = f32[136,128]{1,0:T(8,128)S(1)} collective-permute-done((f32[136,128]{1,0:T(8,128)S(1)}, f32[136,128]{1,0:T(8,128)S(1)}, u32[]{:S(2)}, u32[]{:S(2)}) %collective-permute-start.4) | collective-permute-done | bytes 69664 | tf_op jit(solution)/shard_map/ppermute | solution.py:280
  27.6 2.7 %collective-permute-start.5 = (f32[136,128]{1,0:T(8,128)S(1)}, f32[136,128]{1,0:T(8,128)S(1)}, u32[]{:S(2)}, u32[]{:S(2)}) collective-permute-start(f32[136,128]{1,0:T(8,128)S(1)} %add.14), channel_id=1, source_target_pairs={{0,8},{1,9},{2,10},{3,11},{4,12},{5,13},{6,14},{7,15},{8,0},{9,1},... | collective-permute-start | bytes 208904 | tf_op jit(solution)/shard_map/ppermute | solution.py:280
  30.9 2.0 %collective-permute-done.5 = f32[136,128]{1,0:T(8,128)S(1)} collective-permute-done((f32[136,128]{1,0:T(8,128)S(1)}, f32[136,128]{1,0:T(8,128)S(1)}, u32[]{:S(2)}, u32[]{:S(2)}) %collective-permute-start.5) | collective-permute-done | bytes 69664 | tf_op jit(solution)/shard_map/ppermute | solution.py:280
  32.9 0.6 %solve.1 = (f32[16,128]{1,0:T(8,128)S(1)}, f32[16,128]{1,0:T(8,128)S(1)}) custom-call(f32[136,128]{1,0:T(8,128)S(1)} %add.15.stats_ref, s32[1]{0:T(128)S(6)} %copy.14.ref_mic_ref), custom_call_target="tpu_custom_call" | custom-call | tf_op jit(solution)/shard_map/solve/pallas_call | solution.py:322
  33.5 0.1 collective-permute-start.6
  33.6 0.0 copy-done.9
  33.6 0.5 %concatenate.3.conv1_w_ref = bf16[128,256]{1,0:T(8,128)(2,1)S(1)} concatenate(bf16[3,256]{1,0:T(4,128)(2,1)S(1)} %get-tuple-element.16, bf16[39,256]{1,0:T(8,128)(2,1)S(1)} %broadcast.3, bf16[3,256]{1,0:T(4,128)(2,1)S(1)} %get-tuple-element.17, bf16[39,256]{1,0:T(8,128)(2,1)S(1)} %broadcast.3, bf16[3,256]{1,0:T(4,128)(2,1)S(1)} %get-tuple-element.15, ...), dimensions={0} | concatenate | bytes 131072 | tf_op jit(solution)/shard_map/concatenate | solution.py:75
  34.1 0.6 %collective-permute-done.6.theirs_ref = f32[16,128]{1,0:T(8,128)S(1)} collective-permute-done((f32[16,128]{1,0:T(8,128)S(1)}, f32[16,128]{1,0:T(8,128)S(1)}, u32[]{:S(2)}, u32[]{:S(2)}) %collective-permute-start.6) | collective-permute-done | bytes 8224 | tf_op jit(solution)/shard_map/ppermute | solution.py:280
  34.7 0.0 copy-done.1
  34.7 0.0 copy-done.3
  34.8 0.0 copy-done.6
  34.8 0.0 copy-done.7
  34.8 0.0 copy-done.8
  34.8 0.0 copy-start
  34.8 1.7 %copy-done = bf16[4864,256]{1,0:T(8,128)(2,1)S(1)} copy-done((bf16[4864,256]{1,0:T(8,128)(2,1)S(1)}, bf16[4864,256]{1,0:T(8,128)(2,1)}, u32[]{:S(2)}) %copy-start) | copy-done | bytes 2490392
  36.5 3.2 %stem.1 = bf16[1,16,256]{2,1,0:T(8,128)(2,1)} custom-call(f32[16,128]{1,0:T(8,128)S(1)} %get-tuple-element.12.mine_ref, f32[16,128]{1,0:T(8,128)S(1)} %collective-permute-done.6.theirs_ref, f32[16,128]{1,0:T(8,128)S(1)} %get-tuple-element.13.last_ref, f32[6,576,128]{2,1,0:T(8,128)S(1)} %get-tuple-element.14.spec_ref, s32[1]{0:T(128)S(6)} %copy.13.valid_ref, ...), custom_call_target="tpu_custom_call" | custom-call | tf_op jit(solution)/shard_map/stem/pallas_call | solution.py:331
  (15 shorter events, 0.1 us)
Async XLA Ops:
  0.0 34.7 %copy-start.1 = (bf16[9,256,256]{2,1,0:T(8,128)(2,1)S(1)}, bf16[9,256,256]{2,1,0:T(8,128)(2,1)}, u32[]{:S(2)}) copy-start(bf16[9,256,256]{2,1,0:T(8,128)(2,1)} %param.18) | copy-start | bytes 3538948
  0.8 8.2 %collective-permute-start = (bf16[8,512]{1,0:T(8,128)(2,1)S(1)}, bf16[8,512]{1,0:T(8,128)(2,1)S(1)}, u32[]{:S(2)}, u32[]{:S(2)}) collective-permute-start(bf16[8,512]{1,0:T(8,128)(2,1)S(1)} %slice.15), channel_id=1, source_target_pairs={{0,1},{1,2},{2,3},{3,4},{4,5},{5,6},{6,7},{7,8},{8,9},{9,10},{10,1... | collective-permute-start | bytes 24584 | tf_op jit(solution)/shard_map/ppermute | solution.py:34
  3.8 5.2 %collective-permute-start.1 = (bf16[8,384]{1,0:T(8,128)(2,1)S(1)}, bf16[8,384]{1,0:T(8,128)(2,1)S(1)}, u32[]{:S(2)}, u32[]{:S(2)}) collective-permute-start(bf16[8,384]{1,0:T(8,128)(2,1)S(1)} %slice.16), channel_id=1, source_target_pairs={{1,0},{2,1},{3,2},{4,3},{5,4},{6,5},{7,6},{8,7},{9,8},{10,9},{11,1... | collective-permute-start | bytes 18440 | tf_op jit(solution)/shard_map/ppermute | solution.py:34
  9.0 1.1 %copy-start.2 = (bf16[512,768]{1,0:T(8,128)(2,1)S(1)}, bf16[512,768]{1,0:T(8,128)(2,1)}, u32[]{:S(2)}) copy-start(bf16[512,768]{1,0:T(8,128)(2,1)} %constant.11.table_ref) | copy-start | bytes 2359300
  10.2 0.9 %copy-start.4 = (s32[2,64,257]{2,1,0:T(8,128)S(1)}, s32[2,64,257]{2,1,0:T(8,128)}, u32[]{:S(2)}) copy-start(s32[2,64,257]{2,1,0:T(8,128)} %masks_ref.1) | copy-start | bytes 394756
  11.1 0.9 %copy-start.5 = (bf16[8,10240]{1,0:T(8,128)(2,1)S(1)}, bf16[8,10240]{1,0:T(8,128)(2,1)}, u32[]{:S(2)}) copy-start(bf16[8,10240]{1,0:T(8,128)(2,1)} %wave_ref.1) | copy-start | bytes 491524
  12.0 21.6 %copy-start.9 = (bf16[9,256]{1,0:T(8,128)(2,1)S(1)}, bf16[9,256]{1,0:T(8,128)(2,1)}, u32[]{:S(2)}) copy-start(bf16[9,256]{1,0:T(8,128)(2,1)} %param.16) | copy-start | bytes 13828
  12.0 22.7 %copy-start.3 = (f32[384,256]{1,0:T(8,128)S(1)}, f32[384,256]{1,0:T(8,128)}, u32[]{:S(2)}) copy-start(f32[384,256]{1,0:T(8,128)} %constant.8.clone.bank_ref) | copy-start | bytes 1179652
  12.0 22.7 %copy-start.6 = (f32[256]{0:T(256)S(1)}, f32[256]{0:T(256)}, u32[]{:S(2)}) copy-start(f32[256]{0:T(256)} %param.17) | copy-start | bytes 3076
  12.0 22.7 %copy-start.7 = (f32[256]{0:T(256)S(1)}, f32[256]{0:T(256)}, u32[]{:S(2)}) copy-start(f32[256]{0:T(256)} %param.19) | copy-start | bytes 3076
  12.0 22.7 %copy-start.8 = (f32[256]{0:T(256)S(1)}, f32[256]{0:T(256)}, u32[]{:S(2)}) copy-start(f32[256]{0:T(256)} %param.21) | copy-start | bytes 3076
  14.7 3.3 %collective-permute-start.2 = (f32[136,128]{1,0:T(8,128)S(1)}, f32[136,128]{1,0:T(8,128)S(1)}, u32[]{:S(2)}, u32[]{:S(2)}) collective-permute-start(f32[136,128]{1,0:T(8,128)S(1)} %get-tuple-element.11), channel_id=1, source_target_pairs={{0,1},{1,0},{2,3},{3,2},{4,5},{5,4},{6,7},{7,6},{8,9},{9,8},{10,11... | collective-permute-start | bytes 208904 | tf_op jit(solution)/shard_map/ppermute | solution.py:280
  18.0 5.2 %collective-permute-start.3 = (f32[136,128]{1,0:T(8,128)S(1)}, f32[136,128]{1,0:T(8,128)S(1)}, u32[]{:S(2)}, u32[]{:S(2)}) collective-permute-start(f32[136,128]{1,0:T(8,128)S(1)} %add.12), channel_id=1, source_target_pairs={{0,2},{1,3},{2,0},{3,1},{4,6},{5,7},{6,4},{7,5},{8,10},{9,11},{10,... | collective-permute-start | bytes 208904 | tf_op jit(solution)/shard_map/ppermute | solution.py:280
  23.2 4.4 %collective-permute-start.4 = (f32[136,128]{1,0:T(8,128)S(1)}, f32[136,128]{1,0:T(8,128)S(1)}, u32[]{:S(2)}, u32[]{:S(2)}) collective-permute-start(f32[136,128]{1,0:T(8,128)S(1)} %add.13), channel_id=1, source_target_pairs={{0,4},{1,5},{2,6},{3,7},{4,0},{5,1},{6,2},{7,3},{8,12},{9,13},{10,... | collective-permute-start | bytes 208904 | tf_op jit(solution)/shard_map/ppermute | solution.py:280
  27.6 5.3 %collective-permute-start.5 = (f32[136,128]{1,0:T(8,128)S(1)}, f32[136,128]{1,0:T(8,128)S(1)}, u32[]{:S(2)}, u32[]{:S(2)}) collective-permute-start(f32[136,128]{1,0:T(8,128)S(1)} %add.14), channel_id=1, source_target_pairs={{0,8},{1,9},{2,10},{3,11},{4,12},{5,13},{6,14},{7,15},{8,0},{9,1},... | collective-permute-start | bytes 208904 | tf_op jit(solution)/shard_map/ppermute | solution.py:280
  33.5 1.2 %collective-permute-start.6 = (f32[16,128]{1,0:T(8,128)S(1)}, f32[16,128]{1,0:T(8,128)S(1)}, u32[]{:S(2)}, u32[]{:S(2)}) collective-permute-start(f32[16,128]{1,0:T(8,128)S(1)} %get-tuple-element.12.mine_ref), channel_id=1, source_target_pairs={{0,1},{1,0},{2,3},{3,2},{4,5},{5,4},{6,7},{7,6},{8,9},{9,8},{10,11... | collective-permute-start | bytes 24584 | tf_op jit(solution)/shard_map/ppermute | solution.py:280
  34.8 1.7 %copy-start = (bf16[4864,256]{1,0:T(8,128)(2,1)S(1)}, bf16[4864,256]{1,0:T(8,128)(2,1)}, u32[]{:S(2)}) copy-start(bf16[4864,256]{1,0:T(8,128)(2,1)} %proj_w_ref.1) | copy-start | bytes 7471108

commit v2 on v1

--- a/solution.py
+++ b/solution.py
@@ -28,12 +28,6 @@
 sample_rate = 16000.0
 
 
-def passed_along(block, axis, distance):
-    devices = range(lax.axis_size(axis))
-    route = [(i - distance, i) for i in devices if i - distance in devices]
-    return lax.ppermute(block, axis, route)
-
-
 def dft_table():
     n = np.arange(NFFT)
     f = np.arange(BINS)
@@ -66,35 +60,75 @@
     return jnp.asarray(packed.reshape(PAD_BINS, 2 * LANES))
 
 
-def packed_conv1(conv1_w):
-    rows = []
-    for shift_t in range(3):
-        rows.append(conv1_w[3 * shift_t : 3 * shift_t + 3])
-        rows.append(jnp.zeros((SPAN - 3, conv1_w.shape[1]), conv1_w.dtype))
-    rows.append(jnp.zeros((LANES - 3 * SPAN, conv1_w.shape[1]), conv1_w.dtype))
-    return jnp.concatenate(rows, axis=0)
-
-
-def stats_kernel(frames, prev_ref, wave_ref, next_ref, masks_ref, valid_ref, table_ref, spec_ref, mine_ref, theirs_ref, framed_ref, weight_ref):
+def cyclic_pairs(x_re, x_im):
+    pairs = [x_re * x_re + x_im * x_im]
+    for shift in range(1, MICS // 2 + 1):
+        y_re = pltpu.roll(x_re, MICS - shift, 0)
+        y_im = pltpu.roll(x_im, MICS - shift, 0)
+        pairs.append(x_re * y_re + x_im * y_im)
+        pairs.append(x_im * y_re - x_re * y_im)
+    return pairs
+
+
+def add_frame(sums, x_re, x_im, weights):
+    pairs = cyclic_pairs(x_re, x_im)
+    out = []
+    for k in range(2):
+        w = jnp.broadcast_to(weights[k], (MICS, LANES))
+        out.extend(sums[k * len(pairs) + i] + w * pair for i, pair in enumerate(pairs))
+    return tuple(out)
+
+
+def kept_sums(sums):
+    low = lax.broadcasted_iota(jnp.int32, (MICS, LANES), 0) < MICS // 2
+    kept = []
+    for k in range(2):
+        own = sums[9 * k : 9 * k + 9]
+        kept.extend(list(own[:7]) + [jnp.where(low, own[7], own[8])])
+    return jnp.concatenate(kept, axis=0)
+
+
+def slot_tiles(position):
+    core = position % 2
+    return core, 1 - core, TILES - 1
+
+
+def rims_kernel(wave_ref, beside_ref, across_ref, sem):
+    even = lax.axis_index("tm") % 2 == 0
+    last = wave_ref.shape[1] - LEAD
+    copies = []
+    for i, (out_ref, start) in enumerate(((beside_ref, jnp.where(even, last, 0)), (across_ref, jnp.where(even, 0, last)))):
+        lanes = pl.ds(pl.multiple_of(start, LANES), LEAD)
+        copies.append(pltpu.make_async_copy(wave_ref.at[:, lanes], out_ref, sem.at[i]))
+        copies[-1].start()
+    for copy in copies:
+        copy.wait()
+
+
+def stats_kernel(frames, wave_hbm, masks_hbm, table_hbm, valid_ref, spec_ref, kept_ref, edge_weight_ref, table_ref, wave_ref, masks_ref, framed_ref, weight_ref, sem):
+    copies = [
+        pltpu.make_async_copy(source, target, sem.at[i])
+        for i, (source, target) in enumerate(((wave_hbm, wave_ref), (table_hbm, table_ref), (masks_hbm, masks_ref)))
+    ]
+    for copy in copies:
+        copy.start()
     position = lax.axis_index("tm")
-    span = frames + HALO
-    extended = jnp.concatenate(
-        [prev_ref[...].astype(jnp.float32), wave_ref[...].astype(jnp.float32), next_ref[...].astype(jnp.float32)], axis=1
-    )
-    width = extended.shape[1]
+    copies[0].wait()
+    wave = wave_ref[...].astype(jnp.float32)
+    width = wave.shape[1]
     rolled = {}
-    for frame in range(span):
-        start = LEAD - HALO * HOP + frame * HOP
-        base, shift = start // LANES * LANES, start % LANES
+    for frame in range(frames - HALO):
+        base, shift = frame * HOP // LANES * LANES, frame * HOP % LANES
         if shift not in rolled:
-            rolled[shift] = extended if shift == 0 else pltpu.roll(extended, width - shift, 1)
+            rolled[shift] = wave if shift == 0 else pltpu.roll(wave, width - shift, 1)
         framed_ref[MICS * frame : MICS * (frame + 1), :] = rolled[shift][:, base : base + NFFT]
-    rest = framed_ref.shape[0] - MICS * span
-    framed_ref[MICS * span :, :] = jnp.zeros((rest, NFFT), jnp.float32)
+    framed_ref[MICS * (frames - HALO) :, :] = jnp.zeros((MICS * HALO, NFFT), jnp.float32)
+    copies[1].wait()
     spec = jnp.dot(framed_ref[...].astype(jnp.bfloat16), table_ref[...], preferred_element_type=jnp.float32)
     for tile in range(2 * TILES):
         spec_ref[tile] = spec[:, tile * LANES : (tile + 1) * LANES]
 
+    copies[2].wait()
     row = lax.broadcasted_iota(jnp.int32, (frames, 1), 0)
     live = jnp.where(position * frames + row < valid_ref[0], 1.0 / 255.0, 0.0)
     weight_ref[TILES - 1] = jnp.zeros((2, frames, LANES), jnp.float32)
@@ -103,44 +137,60 @@
         for tile in range(TILES):
             kept_lanes = min(LANES, BINS - tile * LANES)
             weight_ref[tile, k, :, :kept_lanes] = weight[:, tile * LANES : tile * LANES + kept_lanes]
-
-    low = lax.broadcasted_iota(jnp.int32, (MICS, LANES), 0) < MICS // 2
-    core = position % 2
-    for slot, tile in enumerate((core, 1 - core, TILES - 1)):
+    edge_weight_ref[...] = weight_ref[:, :, frames - MICS :, :]
+
+    for slot, tile in enumerate(slot_tiles(position)):
 
         def add_frames(group, sums):
             first = pl.multiple_of(group * MICS, MICS)
             weights = [weight_ref[tile, k, pl.ds(first, MICS), :] for k in range(2)]
             for frame in range(MICS):
-                rows = pl.ds(pl.multiple_of((first + frame + HALO) * MICS, MICS), MICS)
-                x_re = spec_ref[tile, rows, :]
-                x_im = spec_ref[TILES + tile, rows, :]
-                pairs = [x_re * x_re + x_im * x_im]
-                for shift in range(1, MICS // 2 + 1):
-                    y_re = pltpu.roll(x_re, MICS - shift, 0)
-                    y_im = pltpu.roll(x_im, MICS - shift, 0)
-                    pairs.append(x_re * y_re + x_im * y_im)
-                    pairs.append(x_im * y_re - x_re * y_im)
-                out = []
-                for k in range(2):
-                    w = jnp.broadcast_to(weights[k][frame : frame + 1], (MICS, LANES))
-                    out.extend(sums[k * len(pairs) + i] + w * pair for i, pair in enumerate(pairs))
-                sums = tuple(out)
+                rows = pl.ds(pl.multiple_of((first + frame) * MICS, MICS), MICS)
+                sums = add_frame(
+                    sums, spec_ref[tile, rows, :], spec_ref[TILES + tile, rows, :], [w[frame : frame + 1] for w in weights]
+                )
             return sums
 
         zero = jnp.zeros((MICS, LANES), jnp.float32)
-        sums = lax.fori_loop(0, frames // MICS, add_frames, (zero,) * 18)
-        kept = []
-        for k in range(2):
-            own = sums[9 * k : 9 * k + 9]
-            kept.extend(list(own[:7]) + [jnp.where(low, own[7], own[8])])
-        kept = jnp.concatenate(kept, axis=0)
+        kept_ref[slot] = kept_sums(lax.fori_loop(0, frames // MICS, add_frames, (zero,) * 18))
+
+
+def edges_kernel(devices, own0_ref, own1_ref, got0_ref, got1_ref, table_ref, edge_weight_ref, kept_ref, spec_ref, mine_ref, theirs_ref, framed_ref):
+    position = lax.axis_index("tm")
+    even = position % 2 == 0
+    own = [own0_ref[...].astype(jnp.float32), own1_ref[...].astype(jnp.float32)]
+    got = [got0_ref[...].astype(jnp.float32), got1_ref[...].astype(jnp.float32)]
+    head, tail = jnp.where(even, own[1], own[0]), jnp.where(even, own[0], own[1])
+    prev, after = jnp.where(even, got[1], got[0]), jnp.where(even, got[0], got[1])
+    prev = jnp.where(position > 0, prev, 0.0)
+    after = jnp.where(position < devices - 1, after, 0.0)
+    joined = jnp.concatenate(
+        [jnp.concatenate([prev, head[:, :TAIL]], axis=1), jnp.concatenate([tail, after[:, :TAIL]], axis=1)], axis=0
+    )
+    for i in range(HALO):
+        start = LEAD - HALO * HOP + i * HOP
+        base, shift = start // LANES * LANES, start % LANES
+        turned = joined if shift == 0 else pltpu.roll(joined, joined.shape[1] - shift, 1)
+        framed_ref[2 * MICS * i : 2 * MICS * (i + 1), :] = turned[:, base : base + NFFT]
+    used = 2 * MICS * HALO
+    framed_ref[used:, :] = jnp.zeros((framed_ref.shape[0] - used, NFFT), jnp.float32)
+    spec = jnp.dot(framed_ref[...].astype(jnp.bfloat16), table_ref[...], preferred_element_type=jnp.float32)
+    for tile in range(2 * TILES):
+        spec_ref[tile] = spec[:, tile * LANES : (tile + 1) * LANES]
+    for slot, tile in enumerate(slot_tiles(position)):
+        sums = (jnp.zeros((MICS, LANES), jnp.float32),) * 18
+        for i in range(HALO):
+            rows = slice((2 * i + 1) * MICS, (2 * i + 2) * MICS)
+            at = MICS - HALO + i
+            weights = [edge_weight_ref[tile, k, at : at + 1, :] for k in range(2)]
+            sums = add_frame(sums, spec_ref[tile, rows, :], spec_ref[TILES + tile, rows, :], weights)
+        total = kept_ref[slot] + kept_sums(sums)
         if slot == 0:
-            mine_ref[:STATS, :] = kept
+            mine_ref[:STATS, :] = total
         elif slot == 1:
-            theirs_ref[:STATS, :] = kept
+            theirs_ref[:STATS, :] = total
         else:
-            last_bin = jnp.transpose(kept)[:MICS]
+            last_bin = jnp.transpose(total)[:MICS]
             mine_ref[STATS:, :] = last_bin
             theirs_ref[STATS:, :] = last_bin
 
@@ -212,19 +262,31 @@
         out_ref[MICS:, :] = beam_im
 
 
-def stem_kernel(frames, mine_ref, theirs_ref, last_ref, spec_ref, valid_ref, bank_ref, conv1_w_ref, conv1_b_ref, conv2_w_ref, conv2_b_ref, proj_w_ref, proj_b_ref, out_ref, power_ref, logmel_ref):
+def stem_kernel(frames, mine_ref, theirs_ref, last_ref, spec_ref, edge_spec_ref, valid_ref, bank_ref, conv1_w_ref, conv1_b_ref, conv2_w_hbm, conv2_b_ref, proj_w_hbm, proj_b_ref, out_ref, power_ref, logmel_ref, conv1_ref, conv2_w_ref, proj_w_ref, sem):
+    copies = [
+        pltpu.make_async_copy(source, target, sem.at[i])
+        for i, (source, target) in enumerate(((conv2_w_hbm, conv2_w_ref), (proj_w_hbm, proj_w_ref)))
+    ]
+    for copy in copies:
+        copy.start()
     position = lax.axis_index("tm")
     valid = valid_ref[0]
     quarter = frames // 4
-    span = power_ref.shape[1]
-    core = position % 2
-    for beam_ref, tile in ((mine_ref, core), (theirs_ref, 1 - core), (last_ref, TILES - 1)):
+    channels = conv1_w_ref.shape[1]
+    conv1_ref[...] = jnp.zeros((LANES, channels), jnp.float32)
+    for shift_t in range(3):
+        conv1_ref[SPAN * shift_t : SPAN * shift_t + 3, :] = conv1_w_ref[3 * shift_t : 3 * shift_t + 3, :].astype(jnp.float32)
+    conv1 = conv1_ref[...].astype(jnp.bfloat16)
+
+    groups = frames // MICS
+    for beam_ref, tile in zip((mine_ref, theirs_ref, last_ref), slot_tiles(position)):
         beam_re, beam_im = beam_ref[:MICS, :], beam_ref[MICS:, :]
-        for group in range(span // MICS):
+        for group in range(groups + 1):
+            from_ref, first = (spec_ref, group * MICS * MICS) if group < groups else (edge_spec_ref, 0)
             sum_re = sum_im = None
             for m in range(MICS):
-                rows = pl.ds(group * MICS * MICS + m, MICS, stride=MICS)
-                x_re, x_im = spec_ref[tile, rows, :], spec_ref[TILES + tile, rows, :]
+                rows = pl.ds(first + m, MICS, stride=MICS)
+                x_re, x_im = from_ref[tile, rows, :], from_ref[TILES + tile, rows, :]
                 b_re, b_im = beam_re[m : m + 1], beam_im[m : m + 1]
                 part_re = b_re * x_re + b_im * x_im
                 part_im = b_re * x_im - b_im * x_re
@@ -233,12 +295,18 @@
             power_ref[tile, group * MICS : (group + 1) * MICS, :] = sum_re * sum_re + sum_im * sum_im
     power = jnp.concatenate([power_ref[tile] for tile in range(TILES)], axis=1)
     mel = jnp.dot(power, bank_ref[...], precision=lax.Precision.HIGHEST, preferred_element_type=jnp.float32)
-    time = position * frames - HALO + lax.broadcasted_iota(jnp.int32, (span, 1), 0)
+    row = lax.broadcasted_iota(jnp.int32, (frames + MICS, 1), 0)
+    edge = (row - frames) // 2 + jnp.where((row - frames) % 2 == 0, -HALO, frames - HALO)
+    time = position * frames + jnp.where(row < frames, row, edge)
     live = (time >= 0) & (time < valid)
     logmel = jnp.where(live, jnp.log(mel + epsilon), 0.0)
     logmel = logmel.astype(jnp.bfloat16).astype(jnp.float32)
     for half in range(2):
-        logmel_ref[half] = logmel[:, half * LANES : (half + 1) * LANES]
+        part = logmel[:, half * LANES : (half + 1) * LANES]
+        logmel_ref[half, HALO : HALO + frames, :] = part[:frames]
+        for i in range(HALO):
+            logmel_ref[half, i : i + 1, :] = part[frames + 2 * i : frames + 2 * i + 1]
+            logmel_ref[half, frames + i : frames + i + 1, :] = part[frames + 2 * i + 1 : frames + 2 * i + 2]
 
     q_first = (MELS - 3) // 2 + 1
     q_second = (q_first - 3) // 2 + 1
@@ -257,7 +325,7 @@
             half, shift = (0, 2 * q) if q < 20 else (1, 2 * q - 40)
             patches.append(packs[half] if shift == 0 else pltpu.roll(packs[half], LANES - shift, 1))
         patches = jnp.concatenate(patches, axis=0).astype(jnp.bfloat16)
-        layer = jnp.dot(patches, conv1_w_ref[...], preferred_element_type=jnp.float32) + conv1_b_ref[...]
+        layer = jnp.dot(patches, conv1, preferred_element_type=jnp.float32) + conv1_b_ref[...]
         layer = jnp.maximum(layer, 0.0)
         if tap == 0:
             keep = jnp.concatenate([row + 2 * quarter * position >= 1] * q_first, axis=0)
@@ -267,9 +335,11 @@
         windows.append(layer[:count])
         windows.append(layer[quarter * evens : quarter * evens + count])
         windows.append(layer[quarter : quarter + count])
+    copies[0].wait()
     second = jnp.dot(jnp.concatenate(windows, axis=1), conv2_w_ref[...], preferred_element_type=jnp.float32)
     second = jnp.maximum(second + conv2_b_ref[...], 0.0).astype(jnp.bfloat16)
     flat = jnp.concatenate([second[quarter * r : quarter * (r + 1)] for r in range(q_second)], axis=1)
+    copies[1].wait()
     features = jnp.dot(flat, proj_w_ref[...], preferred_element_type=jnp.float32) + proj_b_ref[...]
     features = jnp.where(position * frames + 4 * row < valid, features, 0.0)
     out_ref[0] = features.astype(jnp.bfloat16)
@@ -291,32 +361,64 @@
     return block
 
 
+def paired(block, axis, first):
+    size = lax.axis_size(axis)
+    lower = range(first, size, 2)
+    route = [(i, (i + 1) % size) for i in lower] + [((i + 1) % size, i) for i in lower]
+    return lax.ppermute(block, axis, route)
+
+
 def per_device(waveform, masks, valid, ref_mic, conv1_w, conv1_b, conv2_w, conv2_b, proj_w, proj_b):
     frames = masks.shape[1]
     channels = conv1_w.shape[1]
     width = proj_w.shape[1]
-    rows = -(-(frames + HALO) // MICS) * MICS
-    prev_rim = passed_along(waveform[:, -LEAD:], "tm", 1)
-    next_rim = passed_along(waveform[:, :TAIL], "tm", -1)
     vmem = pl.BlockSpec(memory_space=pltpu.VMEM)
     smem = pl.BlockSpec(memory_space=pltpu.SMEM)
-    params = pltpu.CompilerParams(vmem_limit_bytes=16 * 1024 * 1024)
-    spec, mine, theirs = pl.pallas_call(
+    hbm = pl.BlockSpec(memory_space=pltpu.HBM)
+    params = pltpu.CompilerParams(vmem_limit_bytes=20 * 1024 * 1024)
+    rim = jax.ShapeDtypeStruct((MICS, LEAD), waveform.dtype)
+    beside, across = pl.pallas_call(
+        rims_kernel,
+        out_shape=(rim, rim),
+        in_specs=[hbm],
+        out_specs=(vmem, vmem),
+        scratch_shapes=[pltpu.SemaphoreType.DMA((2,))],
+        compiler_params=params,
+        name="rims",
+    )(waveform)
+    got_across = paired(across, "tm", 1)
+    got_beside = paired(beside, "tm", 0)
+    table = dft_table()
+    stat_block = jax.ShapeDtypeStruct((STATS + MICS, LANES), jnp.float32)
+    spec, kept, edge_weight, table = pl.pallas_call(
         functools.partial(stats_kernel, frames),
         out_shape=(
-            jax.ShapeDtypeStruct((2 * TILES, rows * MICS, LANES), jnp.float32),
-            jax.ShapeDtypeStruct((STATS + MICS, LANES), jnp.float32),
-            jax.ShapeDtypeStruct((STATS + MICS, LANES), jnp.float32),
+            jax.ShapeDtypeStruct((2 * TILES, frames * MICS, LANES), jnp.float32),
+            jax.ShapeDtypeStruct((TILES, STATS, LANES), jnp.float32),
+            jax.ShapeDtypeStruct((TILES, 2, MICS, LANES), jnp.float32),
+            jax.ShapeDtypeStruct(table.shape, table.dtype),
         ),
-        in_specs=[vmem, vmem, vmem, vmem, smem, vmem],
-        out_specs=(vmem, vmem, vmem),
+        in_specs=[hbm, hbm, hbm, smem],
+        out_specs=(vmem,) * 4,
         scratch_shapes=[
-            pltpu.VMEM((rows * MICS, NFFT), jnp.float32),
+            pltpu.VMEM(waveform.shape, waveform.dtype),
+            pltpu.VMEM(masks.shape, masks.dtype),
+            pltpu.VMEM((frames * MICS, NFFT), jnp.float32),
             pltpu.VMEM((TILES, 2, frames, LANES), jnp.float32),
+            pltpu.SemaphoreType.DMA((3,)),
         ],
         compiler_params=params,
         name="stats",
-    )(prev_rim, waveform, next_rim, masks, valid, dft_table())
+    )(waveform, masks, table, valid)
+    edge_spec, mine, theirs = pl.pallas_call(
+        functools.partial(edges_kernel, lax.axis_size("tm")),
+        out_shape=(jax.ShapeDtypeStruct((2 * TILES, MICS * MICS, LANES), jnp.float32), stat_block, stat_block),
+        in_specs=[vmem] * 7,
+        out_specs=(vmem,) * 3,
+        scratch_shapes=[pltpu.VMEM((MICS * MICS, NFFT), jnp.float32)],
+        compiler_params=params,
+        name="edges",
+    )(beside, across, got_beside, got_across, table, edge_weight, kept)
     stats = summed_over_chips(mine + flipped(theirs, "tm", 1), "tm")
     beam = jax.ShapeDtypeStruct((2 * MICS, LANES), jnp.float32)
     beam_mine, beam_last = pl.pallas_call(
@@ -328,14 +430,19 @@
         name="solve",
     )(stats, ref_mic)
     beam_theirs = flipped(beam_mine, "tm", 1)
+    rows = frames + MICS
     return pl.pallas_call(
         functools.partial(stem_kernel, frames),
         out_shape=jax.ShapeDtypeStruct((1, frames // 4, width), jnp.bfloat16),
-        in_specs=[vmem] * 4 + [smem] + [vmem] * 7,
+        in_specs=[vmem] * 5 + [smem] + [vmem] * 3 + [hbm, vmem, hbm, vmem],
         out_specs=vmem,
         scratch_shapes=[
             pltpu.VMEM((TILES, rows, LANES), jnp.float32),
             pltpu.VMEM((2, rows, LANES), jnp.float32),
+            pltpu.VMEM((LANES, channels), jnp.float32),
+            pltpu.VMEM((9 * channels, channels), conv2_w.dtype),
+            pltpu.VMEM(proj_w.shape, proj_w.dtype),
+            pltpu.SemaphoreType.DMA((2,)),
         ],
         compiler_params=params,
         name="stem",
@@ -344,9 +451,10 @@
         beam_theirs,
         beam_last,
         spec,
+        edge_spec,
         valid,
         packed_mel_bank(),
-        packed_conv1(conv1_w),
+        conv1_w,
         conv1_b[None],
         conv2_w.reshape(-1, channels),
         conv2_b[None],

time: 40 us -> 36.7 us (0.918)
  starting transfers between devices: 12.9 us -> 6.51 us
  waiting for transfers between devices: 12.2 us -> 15.7 us
  local copies, waits for them, and re-layouts: 6.67 us -> 4.26 us
  Pallas kernels: 6.47 us -> 8.41 us
    ppermute x5, starting transfers between devices: 9.27 us -> 0.33 us  [flipped(): return lax.ppermute(block, axis, [(i, i ^ step) for i in range(size)])]
    ppermute x5, waiting for transfers between devices: 8.94 us -> 15.7 us  [flipped(): return lax.ppermute(block, axis, [(i, i ^ step) for i in range(size)])]
    ppermute x2, waiting for transfers between devices: 3.25 us -> 0.01 us  [paired(): return lax.ppermute(block, axis, route)]
    ppermute x2, starting transfers between devices: 3.62 us -> 6.18 us  [paired(): return lax.ppermute(block, axis, route)]
    slice x3 -> x0, local copies, waits for them, and re-layouts: 1.5 us -> none  [the longest x1 0.79 us: per_device(): prev_rim = passed_along(waveform[:, -LEAD:], 'tm', 1)]
    pallas_call x1, Pallas kernels: 3.21 us -> 4.06 us  [per_device(): pl.pallas_call(functools.partial(stem_kernel, frames), out_shape=jax.Shap...]
    pallas_call x1, Pallas kernels: 2.67 us -> 3.26 us  [per_device(): pl.pallas_call(functools.partial(stats_kernel, frames), out_shape=(jax.Sh...]
    pallas_call x0 -> x2, Pallas kernels: none -> 0.5 us  [the longest x1 0.44 us: per_device(): pl.pallas_call(functools.partial(edges_kernel, lax.axis_size('tm')), out_...]
  transfers between devices with their start and end apart: 7 -> 7, of which waited for: 6 -> 5; matrix products, arithmetic and copies ran while one was open for 3% -> 0% of each run, Pallas kernels for 0% -> 9%
where the time goes in v2:
time: 36.7 us; the launch traced here: 36.4 us
  waiting for transfers between devices  15.7 us (43%)
  Pallas kernels  8.41 us (23%)
  starting transfers between devices  6.51 us (18%)
  local copies, waits for them, and re-layouts  4.26 us (12%)
  between operations  1.45 us (4%)
    ppermute x5, waiting for transfers between devices, flipped(): return lax.ppermute(block, axis, [(i, i ^ step) for i in range(size)])  15.7 us
    ppermute x2, starting transfers between devices, paired(): return lax.ppermute(block, axis, route)  6.18 us
    unnamed x20, local copies, waits for them, and re-layouts  4.26 us
    pallas_call x1, Pallas kernels, per_device(): pl.pallas_call(functools.partial(stem_kernel, frames), out_shape=jax.Shap...  4.06 us
    pallas_call x1, Pallas kernels, per_device(): pl.pallas_call(functools.partial(stats_kernel, frames), out_shape=(jax.Sh...  3.26 us
  transfers between devices with their start and end apart: 7, of which 5 were waited for; matrix products, arithmetic and copies ran while one was open for 0% of the time, Pallas kernels for 9%

profile of v2, /device:TPU:0, one launch (start us, length us, event | category | flops | bytes accessed | tf_op | source)
XLA Modules:
  0.0 36.4 jit_solution(3043778472654536935)
XLA Ops:
  0.0 0.9 %copy-done.3 = bf16[8,10240]{1,0:T(8,128)(2,1)S(1)} copy-done((bf16[8,10240]{1,0:T(8,128)(2,1)S(1)}, bf16[8,10240]{1,0:T(8,128)(2,1)}, u32[]{:S(2)}) %copy-start.3) | copy-done | bytes 163864
  0.9 0.1 rims.1
  1.0 0.0 copy-start
  1.0 0.5 %collective-permute-start = (bf16[8,512]{1,0:T(8,128)(2,1)S(1)}, bf16[8,512]{1,0:T(8,128)(2,1)S(1)}, u32[]{:S(2)}, u32[]{:S(2)}) collective-permute-start(bf16[8,512]{1,0:T(8,128)(2,1)S(1)} %get-tuple-element.16.own0_ref), channel_id=1, source_target_pairs={{0,1},{2,3},{4,5},{6,7},{8,9},{10,11},{12,13},{14,15},{1,0},{3,2},... | collective-permute-start | bytes 24584 | tf_op jit(solution)/shard_map/ppermute | solution.py:368
  1.5 5.7 %collective-permute-start.1 = (bf16[8,512]{1,0:T(8,128)(2,1)S(1)}, bf16[8,512]{1,0:T(8,128)(2,1)S(1)}, u32[]{:S(2)}, u32[]{:S(2)}) collective-permute-start(bf16[8,512]{1,0:T(8,128)(2,1)S(1)} %get-tuple-element.17.own1_ref), channel_id=1, source_target_pairs={{1,2},{3,4},{5,6},{7,8},{9,10},{11,12},{13,14},{15,0},{2,1},{4,3},... | collective-permute-start | bytes 24584 | tf_op jit(solution)/shard_map/ppermute | solution.py:368
  7.8 0.0 copy-start.2
  7.9 1.1 %copy-done.2 = bf16[512,768]{1,0:T(8,128)(2,1)S(1)} copy-done((bf16[512,768]{1,0:T(8,128)(2,1)S(1)}, bf16[512,768]{1,0:T(8,128)(2,1)}, u32[]{:S(2)}) %copy-start.2) | copy-done | bytes 786456
  9.0 0.9 %copy-done.5 = s32[2,64,257]{2,1,0:T(8,128)S(1)} copy-done((s32[2,64,257]{2,1,0:T(8,128)S(1)}, s32[2,64,257]{2,1,0:T(8,128)}, u32[]{:S(2)}) %copy-start.5) | copy-done | bytes 131608
  9.9 3.3 %stats.1 = (f32[6,512,128]{2,1,0:T(8,128)S(1)}, f32[3,128,128]{2,1,0:T(8,128)S(1)}, f32[3,2,8,128]{3,2,1,0:T(8,128)S(1)}, bf16[512,768]{1,0:T(8,128)(2,1)S(1)}) custom-call(bf16[8,10240]{1,0:T(8,128)(2,1)S(1)} %copy-done.3, s32[2,64,257]{2,1,0:T(8,128)S(1)} %copy-done.5, bf16[512,768]{1,0:T(8,128)(2,1)S(1)} %copy-done.2, s32[1]{0:T(128)S(6)} %copy.13.valid_ref), custom_call_target="tpu_custom_call" | custom-call | tf_op jit(solution)/shard_map/stats/pallas_call | solution.py:393
  13.2 0.0 collective-permute-done.got0_ref
  13.2 0.0 collective-permute-done.1.got1_ref
  13.2 0.4 %edges.1 = (f32[6,64,128]{2,1,0:T(8,128)S(1)}, f32[136,128]{1,0:T(8,128)S(1)}, f32[136,128]{1,0:T(8,128)S(1)}) custom-call(bf16[8,512]{1,0:T(8,128)(2,1)S(1)} %get-tuple-element.16.own0_ref, bf16[8,512]{1,0:T(8,128)(2,1)S(1)} %get-tuple-element.17.own1_ref, bf16[8,512]{1,0:T(8,128)(2,1)S(1)} %collective-permute-done.got0_ref, ...), custom_call_target="tpu_custom_call" | custom-call | tf_op jit(solution)/shard_map/edges/pallas_call | solution.py:413
  13.6 0.0 collective-permute-start.2
  13.7 1.2 %collective-permute-done.2 = f32[136,128]{1,0:T(8,128)S(1)} collective-permute-done((f32[136,128]{1,0:T(8,128)S(1)}, f32[136,128]{1,0:T(8,128)S(1)}, u32[]{:S(2)}, u32[]{:S(2)}) %collective-permute-start.2) | collective-permute-done | bytes 69664 | tf_op jit(solution)/shard_map/ppermute | solution.py:350
  14.9 0.1 collective-permute-start.3
  15.0 4.3 %collective-permute-done.3 = f32[136,128]{1,0:T(8,128)S(1)} collective-permute-done((f32[136,128]{1,0:T(8,128)S(1)}, f32[136,128]{1,0:T(8,128)S(1)}, u32[]{:S(2)}, u32[]{:S(2)}) %collective-permute-start.3) | collective-permute-done | bytes 69664 | tf_op jit(solution)/shard_map/ppermute | solution.py:350
  19.3 0.1 collective-permute-start.4
  19.4 4.3 %collective-permute-done.4 = f32[136,128]{1,0:T(8,128)S(1)} collective-permute-done((f32[136,128]{1,0:T(8,128)S(1)}, f32[136,128]{1,0:T(8,128)S(1)}, u32[]{:S(2)}, u32[]{:S(2)}) %collective-permute-start.4) | collective-permute-done | bytes 69664 | tf_op jit(solution)/shard_map/ppermute | solution.py:350
  23.7 0.1 collective-permute-start.5
  24.5 4.7 %collective-permute-done.5 = f32[136,128]{1,0:T(8,128)S(1)} collective-permute-done((f32[136,128]{1,0:T(8,128)S(1)}, f32[136,128]{1,0:T(8,128)S(1)}, u32[]{:S(2)}, u32[]{:S(2)}) %collective-permute-start.5) | collective-permute-done | bytes 69664 | tf_op jit(solution)/shard_map/ppermute | solution.py:350
  29.2 0.6 %solve.1 = (f32[16,128]{1,0:T(8,128)S(1)}, f32[16,128]{1,0:T(8,128)S(1)}) custom-call(f32[136,128]{1,0:T(8,128)S(1)} %add.15.stats_ref, s32[1]{0:T(128)S(6)} %copy.14.ref_mic_ref), custom_call_target="tpu_custom_call" | custom-call | tf_op jit(solution)/shard_map/solve/pallas_call | solution.py:424
  29.8 0.1 collective-permute-start.6
  29.9 1.2 %collective-permute-done.6.theirs_ref = f32[16,128]{1,0:T(8,128)S(1)} collective-permute-done((f32[16,128]{1,0:T(8,128)S(1)}, f32[16,128]{1,0:T(8,128)S(1)}, u32[]{:S(2)}, u32[]{:S(2)}) %collective-permute-start.6) | collective-permute-done | bytes 8224 | tf_op jit(solution)/shard_map/ppermute | solution.py:350
  31.0 0.0 copy-done.6
  31.0 0.0 copy-done.7
  31.0 0.0 copy-done.8
  31.0 0.0 copy-done.9
  31.1 0.0 copy-done
  31.1 0.0 copy-done.4
  31.1 0.0 copy-start.1
  31.1 1.3 %copy-done.1 = bf16[9,256,256]{2,1,0:T(8,128)(2,1)S(1)} copy-done((bf16[9,256,256]{2,1,0:T(8,128)(2,1)S(1)}, bf16[9,256,256]{2,1,0:T(8,128)(2,1)}, u32[]{:S(2)}) %copy-start.1) | copy-done | bytes 1179672
  32.4 4.1 %stem.1 = bf16[1,16,256]{2,1,0:T(8,128)(2,1)} custom-call(f32[16,128]{1,0:T(8,128)S(1)} %get-tuple-element.23.mine_ref, f32[16,128]{1,0:T(8,128)S(1)} %collective-permute-done.6.theirs_ref, f32[16,128]{1,0:T(8,128)S(1)} %get-tuple-element.24.last_ref, f32[6,512,128]{2,1,0:T(8,128)S(1)} %get-tuple-element.25.spec_ref, ...), custom_call_target="tpu_custom_call" | custom-call | tf_op jit(solution)/shard_map/stem/pallas_call | solution.py:434
  (11 shorter events, 0.1 us)
Async XLA Ops:
  0.0 0.9 %copy-start.3 = (bf16[8,10240]{1,0:T(8,128)(2,1)S(1)}, bf16[8,10240]{1,0:T(8,128)(2,1)}, u32[]{:S(2)}) copy-start(bf16[8,10240]{1,0:T(8,128)(2,1)} %wave_hbm.1) | copy-start | bytes 491524
  0.9 30.1 %copy-start.6 = (bf16[9,256]{1,0:T(8,128)(2,1)S(1)}, bf16[9,256]{1,0:T(8,128)(2,1)}, u32[]{:S(2)}) copy-start(bf16[9,256]{1,0:T(8,128)(2,1)} %conv1_w_ref.1) | copy-start | bytes 13828
  0.9 30.1 %copy-start.7 = (f32[256]{0:T(256)S(1)}, f32[256]{0:T(256)}, u32[]{:S(2)}) copy-start(f32[256]{0:T(256)} %param.17) | copy-start | bytes 3076
  0.9 30.1 %copy-start.8 = (f32[256]{0:T(256)S(1)}, f32[256]{0:T(256)}, u32[]{:S(2)}) copy-start(f32[256]{0:T(256)} %param.19) | copy-start | bytes 3076
  0.9 30.1 %copy-start.9 = (f32[256]{0:T(256)S(1)}, f32[256]{0:T(256)}, u32[]{:S(2)}) copy-start(f32[256]{0:T(256)} %param.21) | copy-start | bytes 3076
  1.0 30.1 %copy-start = (bf16[4864,256]{1,0:T(8,128)(2,1)S(1)}, bf16[4864,256]{1,0:T(8,128)(2,1)}, u32[]{:S(2)}) copy-start(bf16[4864,256]{1,0:T(8,128)(2,1)} %proj_w_hbm.1) | copy-start | bytes 7471108
  1.0 12.2 %collective-permute-start = (bf16[8,512]{1,0:T(8,128)(2,1)S(1)}, bf16[8,512]{1,0:T(8,128)(2,1)S(1)}, u32[]{:S(2)}, u32[]{:S(2)}) collective-permute-start(bf16[8,512]{1,0:T(8,128)(2,1)S(1)} %get-tuple-element.16.own0_ref), channel_id=1, source_target_pairs={{0,1},{2,3},{4,5},{6,7},{8,9},{10,11},{12,13},{14,15},{1,0},{3,2},... | collective-permute-start | bytes 24584 | tf_op jit(solution)/shard_map/ppermute | solution.py:368
  1.5 11.7 %collective-permute-start.1 = (bf16[8,512]{1,0:T(8,128)(2,1)S(1)}, bf16[8,512]{1,0:T(8,128)(2,1)S(1)}, u32[]{:S(2)}, u32[]{:S(2)}) collective-permute-start(bf16[8,512]{1,0:T(8,128)(2,1)S(1)} %get-tuple-element.17.own1_ref), channel_id=1, source_target_pairs={{1,2},{3,4},{5,6},{7,8},{9,10},{11,12},{13,14},{15,0},{2,1},{4,3},... | collective-permute-start | bytes 24584 | tf_op jit(solution)/shard_map/ppermute | solution.py:368
  7.8 1.1 %copy-start.2 = (bf16[512,768]{1,0:T(8,128)(2,1)S(1)}, bf16[512,768]{1,0:T(8,128)(2,1)}, u32[]{:S(2)}) copy-start(bf16[512,768]{1,0:T(8,128)(2,1)} %constant.8.table_hbm) | copy-start | bytes 2359300
  9.0 0.9 %copy-start.5 = (s32[2,64,257]{2,1,0:T(8,128)S(1)}, s32[2,64,257]{2,1,0:T(8,128)}, u32[]{:S(2)}) copy-start(s32[2,64,257]{2,1,0:T(8,128)} %masks_hbm.1) | copy-start | bytes 394756
  9.9 21.2 %copy-start.4 = (f32[384,256]{1,0:T(8,128)S(1)}, f32[384,256]{1,0:T(8,128)}, u32[]{:S(2)}) copy-start(f32[384,256]{1,0:T(8,128)} %constant.5.clone.bank_ref) | copy-start | bytes 1179652
  13.6 1.3 %collective-permute-start.2 = (f32[136,128]{1,0:T(8,128)S(1)}, f32[136,128]{1,0:T(8,128)S(1)}, u32[]{:S(2)}, u32[]{:S(2)}) collective-permute-start(f32[136,128]{1,0:T(8,128)S(1)} %get-tuple-element.22), channel_id=1, source_target_pairs={{0,1},{1,0},{2,3},{3,2},{4,5},{5,4},{6,7},{7,6},{8,9},{9,8},{10,11... | collective-permute-start | bytes 208904 | tf_op jit(solution)/shard_map/ppermute | solution.py:350
  14.9 4.4 %collective-permute-start.3 = (f32[136,128]{1,0:T(8,128)S(1)}, f32[136,128]{1,0:T(8,128)S(1)}, u32[]{:S(2)}, u32[]{:S(2)}) collective-permute-start(f32[136,128]{1,0:T(8,128)S(1)} %add.12), channel_id=1, source_target_pairs={{0,2},{1,3},{2,0},{3,1},{4,6},{5,7},{6,4},{7,5},{8,10},{9,11},{10,... | collective-permute-start | bytes 208904 | tf_op jit(solution)/shard_map/ppermute | solution.py:350
  19.3 4.4 %collective-permute-start.4 = (f32[136,128]{1,0:T(8,128)S(1)}, f32[136,128]{1,0:T(8,128)S(1)}, u32[]{:S(2)}, u32[]{:S(2)}) collective-permute-start(f32[136,128]{1,0:T(8,128)S(1)} %add.13), channel_id=1, source_target_pairs={{0,4},{1,5},{2,6},{3,7},{4,0},{5,1},{6,2},{7,3},{8,12},{9,13},{10,... | collective-permute-start | bytes 208904 | tf_op jit(solution)/shard_map/ppermute | solution.py:350
  23.7 5.5 %collective-permute-start.5 = (f32[136,128]{1,0:T(8,128)S(1)}, f32[136,128]{1,0:T(8,128)S(1)}, u32[]{:S(2)}, u32[]{:S(2)}) collective-permute-start(f32[136,128]{1,0:T(8,128)S(1)} %add.14), channel_id=1, source_target_pairs={{0,8},{1,9},{2,10},{3,11},{4,12},{5,13},{6,14},{7,15},{8,0},{9,1},... | collective-permute-start | bytes 208904 | tf_op jit(solution)/shard_map/ppermute | solution.py:350
  29.8 1.2 %collective-permute-start.6 = (f32[16,128]{1,0:T(8,128)S(1)}, f32[16,128]{1,0:T(8,128)S(1)}, u32[]{:S(2)}, u32[]{:S(2)}) collective-permute-start(f32[16,128]{1,0:T(8,128)S(1)} %get-tuple-element.23.mine_ref), channel_id=1, source_target_pairs={{0,1},{1,0},{2,3},{3,2},{4,5},{5,4},{6,7},{7,6},{8,9},{9,8},{10,11... | collective-permute-start | bytes 24584 | tf_op jit(solution)/shard_map/ppermute | solution.py:350
  31.1 1.3 %copy-start.1 = (bf16[9,256,256]{2,1,0:T(8,128)(2,1)S(1)}, bf16[9,256,256]{2,1,0:T(8,128)(2,1)}, u32[]{:S(2)}) copy-start(bf16[9,256,256]{2,1,0:T(8,128)(2,1)} %param.18) | copy-start | bytes 3538948

commit v3 on v2

--- a/solution.py
+++ b/solution.py
@@ -375,6 +375,7 @@
     vmem = pl.BlockSpec(memory_space=pltpu.VMEM)
     smem = pl.BlockSpec(memory_space=pltpu.SMEM)
     hbm = pl.BlockSpec(memory_space=pltpu.HBM)
+    in_hbm = functools.partial(pltpu.with_memory_space_constraint, memory_space=pltpu.HBM)
     params = pltpu.CompilerParams(vmem_limit_bytes=20 * 1024 * 1024)
     rim = jax.ShapeDtypeStruct((MICS, LEAD), waveform.dtype)
     beside, across = pl.pallas_call(
@@ -385,7 +386,7 @@
         scratch_shapes=[pltpu.SemaphoreType.DMA((2,))],
         compiler_params=params,
         name="rims",
-    )(waveform)
+    )(in_hbm(waveform))
     got_across = paired(across, "tm", 1)
     got_beside = paired(beside, "tm", 0)
     table = dft_table()
@@ -409,7 +410,7 @@
         ],
         compiler_params=params,
         name="stats",
-    )(waveform, masks, table, valid)
+    )(in_hbm(waveform), in_hbm(masks), in_hbm(table), valid)
     edge_spec, mine, theirs = pl.pallas_call(
         functools.partial(edges_kernel, lax.axis_size("tm")),
         out_shape=(jax.ShapeDtypeStruct((2 * TILES, MICS * MICS, LANES), jnp.float32), stat_block, stat_block),
@@ -456,9 +457,9 @@
         packed_mel_bank(),
         conv1_w,
         conv1_b[None],
-        conv2_w.reshape(-1, channels),
+        in_hbm(conv2_w.reshape(-1, channels)),
         conv2_b[None],
-        proj_w,
+        in_hbm(proj_w),
         proj_b[None],
     )
 

time: 36.7 us -> 34 us (0.926)
  local copies, waits for them, and re-layouts: 4.26 us -> 0.03 us
  Pallas kernels: 8.41 us -> 9.91 us
    unnamed x20 -> x10, local copies, waits for them, and re-layouts: 4.26 us -> 0.03 us
    pallas_call x1, Pallas kernels: 0.06 us -> 0.73 us  [per_device(): pl.pallas_call(rims_kernel, out_shape=(rim, rim), in_specs=[hbm], out_spe...]
    pallas_call x1, Pallas kernels: 3.26 us -> 3.8 us  [per_device(): pl.pallas_call(functools.partial(stats_kernel, frames), out_shape=(jax.Sh...]
  transfers between devices with their start and end apart: 7 -> 7, of which waited for: 5 -> 5; matrix products, arithmetic and copies ran while one was open for 0% -> 0% of each run, Pallas kernels for 9% -> 11%
where the time goes in v3:
time: 34 us; the launch traced here: 33.7 us
  waiting for transfers between devices  15.7 us (46%)
  Pallas kernels  9.91 us (29%)
  starting transfers between devices  6.51 us (19%)
  between operations  1.45 us (4%)
    ppermute x5, waiting for transfers between devices, flipped(): return lax.ppermute(block, axis, [(i, i ^ step) for i in range(size)])  15.7 us
    ppermute x2, starting transfers between devices, paired(): return lax.ppermute(block, axis, route)  6.18 us
    pallas_call x1, Pallas kernels, per_device(): pl.pallas_call(functools.partial(stem_kernel, frames), out_shape=jax.Shap...  4.36 us
    pallas_call x1, Pallas kernels, per_device(): pl.pallas_call(functools.partial(stats_kernel, frames), out_shape=(jax.Sh...  3.8 us
    pallas_call x1, Pallas kernels, per_device(): pl.pallas_call(rims_kernel, out_shape=(rim, rim), in_specs=[hbm], out_spe...  0.73 us
  transfers between devices with their start and end apart: 7, of which 5 were waited for; matrix products, arithmetic and copies ran while one was open for 0% of the time, Pallas kernels for 11%

profile of v3, /device:TPU:0, one launch (start us, length us, event | category | flops | bytes accessed | tf_op | source)
XLA Modules:
  0.0 33.7 jit_solution(13360154532295002825)
XLA Ops:
  0.0 0.7 %rims.1 = (bf16[8,512]{1,0:T(8,128)(2,1)S(1)}, bf16[8,512]{1,0:T(8,128)(2,1)S(1)}) custom-call(bf16[8,10240]{1,0:T(8,128)(2,1)} %wave_hbm.1), custom_call_target="tpu_custom_call" | custom-call | tf_op jit(solution)/shard_map/rims/pallas_call | solution.py:381
  0.7 0.0 copy-start
  0.8 0.0 copy-start.1
  0.8 0.0 copy-start.2
  0.8 0.0 copy-start.3
  0.8 0.0 copy-start.4
  0.8 0.5 %collective-permute-start = (bf16[8,512]{1,0:T(8,128)(2,1)S(1)}, bf16[8,512]{1,0:T(8,128)(2,1)S(1)}, u32[]{:S(2)}, u32[]{:S(2)}) collective-permute-start(bf16[8,512]{1,0:T(8,128)(2,1)S(1)} %get-tuple-element.16.own0_ref), channel_id=1, source_target_pairs={{0,1},{2,3},{4,5},{6,7},{8,9},{10,11},{12,13},{14,15},{1,0},{3,2},... | collective-permute-start | bytes 24584 | tf_op jit(solution)/shard_map/ppermute | solution.py:368
  1.3 5.7 %collective-permute-start.1 = (bf16[8,512]{1,0:T(8,128)(2,1)S(1)}, bf16[8,512]{1,0:T(8,128)(2,1)S(1)}, u32[]{:S(2)}, u32[]{:S(2)}) collective-permute-start(bf16[8,512]{1,0:T(8,128)(2,1)S(1)} %get-tuple-element.17.own1_ref), channel_id=1, source_target_pairs={{1,2},{3,4},{5,6},{7,8},{9,10},{11,12},{13,14},{15,0},{2,1},{4,3},... | collective-permute-start | bytes 24584 | tf_op jit(solution)/shard_map/ppermute | solution.py:368
  7.6 3.8 %stats.1 = (f32[6,512,128]{2,1,0:T(8,128)S(1)}, f32[3,128,128]{2,1,0:T(8,128)S(1)}, f32[3,2,8,128]{3,2,1,0:T(8,128)S(1)}, bf16[512,768]{1,0:T(8,128)(2,1)S(1)}) custom-call(bf16[8,10240]{1,0:T(8,128)(2,1)} %wave_hbm.1, s32[2,64,257]{2,1,0:T(8,128)} %masks_hbm.1, bf16[512,768]{1,0:T(8,128)(2,1)} %constant.8.table_hbm, s32[1]{0:T(128)S(6)} %copy.13.valid_ref), custom_call_target="tpu_custom_call" | custom-call | tf_op jit(solution)/shard_map/stats/pallas_call | solution.py:394
  11.4 0.0 collective-permute-done.got0_ref
  11.4 0.0 collective-permute-done.1.got1_ref
  11.5 0.4 %edges.1 = (f32[6,64,128]{2,1,0:T(8,128)S(1)}, f32[136,128]{1,0:T(8,128)S(1)}, f32[136,128]{1,0:T(8,128)S(1)}) custom-call(bf16[8,512]{1,0:T(8,128)(2,1)S(1)} %get-tuple-element.16.own0_ref, bf16[8,512]{1,0:T(8,128)(2,1)S(1)} %get-tuple-element.17.own1_ref, bf16[8,512]{1,0:T(8,128)(2,1)S(1)} %collective-permute-done.got0_ref, ...), custom_call_target="tpu_custom_call" | custom-call | tf_op jit(solution)/shard_map/edges/pallas_call | solution.py:414
  11.9 0.0 collective-permute-start.2
  11.9 1.2 %collective-permute-done.2 = f32[136,128]{1,0:T(8,128)S(1)} collective-permute-done((f32[136,128]{1,0:T(8,128)S(1)}, f32[136,128]{1,0:T(8,128)S(1)}, u32[]{:S(2)}, u32[]{:S(2)}) %collective-permute-start.2) | collective-permute-done | bytes 69664 | tf_op jit(solution)/shard_map/ppermute | solution.py:350
  13.2 0.1 collective-permute-start.3
  13.3 4.3 %collective-permute-done.3 = f32[136,128]{1,0:T(8,128)S(1)} collective-permute-done((f32[136,128]{1,0:T(8,128)S(1)}, f32[136,128]{1,0:T(8,128)S(1)}, u32[]{:S(2)}, u32[]{:S(2)}) %collective-permute-start.3) | collective-permute-done | bytes 69664 | tf_op jit(solution)/shard_map/ppermute | solution.py:350
  17.6 0.1 collective-permute-start.4
  17.7 4.3 %collective-permute-done.4 = f32[136,128]{1,0:T(8,128)S(1)} collective-permute-done((f32[136,128]{1,0:T(8,128)S(1)}, f32[136,128]{1,0:T(8,128)S(1)}, u32[]{:S(2)}, u32[]{:S(2)}) %collective-permute-start.4) | collective-permute-done | bytes 69664 | tf_op jit(solution)/shard_map/ppermute | solution.py:350
  22.0 0.1 collective-permute-start.5
  22.7 4.7 %collective-permute-done.5 = f32[136,128]{1,0:T(8,128)S(1)} collective-permute-done((f32[136,128]{1,0:T(8,128)S(1)}, f32[136,128]{1,0:T(8,128)S(1)}, u32[]{:S(2)}, u32[]{:S(2)}) %collective-permute-start.5) | collective-permute-done | bytes 69664 | tf_op jit(solution)/shard_map/ppermute | solution.py:350
  27.5 0.6 %solve.1 = (f32[16,128]{1,0:T(8,128)S(1)}, f32[16,128]{1,0:T(8,128)S(1)}) custom-call(f32[136,128]{1,0:T(8,128)S(1)} %add.15.stats_ref, s32[1]{0:T(128)S(6)} %copy.14.ref_mic_ref), custom_call_target="tpu_custom_call" | custom-call | tf_op jit(solution)/shard_map/solve/pallas_call | solution.py:425
  28.1 0.1 collective-permute-start.6
  28.1 1.2 %collective-permute-done.6.theirs_ref = f32[16,128]{1,0:T(8,128)S(1)} collective-permute-done((f32[16,128]{1,0:T(8,128)S(1)}, f32[16,128]{1,0:T(8,128)S(1)}, u32[]{:S(2)}, u32[]{:S(2)}) %collective-permute-start.6) | collective-permute-done | bytes 8224 | tf_op jit(solution)/shard_map/ppermute | solution.py:350
  29.3 0.0 copy-done
  29.3 0.0 copy-done.1
  29.3 0.0 copy-done.2
  29.3 0.0 copy-done.3
  29.3 0.0 copy-done.4
  29.3 4.4 %stem.1 = bf16[1,16,256]{2,1,0:T(8,128)(2,1)} custom-call(f32[16,128]{1,0:T(8,128)S(1)} %get-tuple-element.23.mine_ref, f32[16,128]{1,0:T(8,128)S(1)} %collective-permute-done.6.theirs_ref, f32[16,128]{1,0:T(8,128)S(1)} %get-tuple-element.24.last_ref, f32[6,512,128]{2,1,0:T(8,128)S(1)} %get-tuple-element.25.spec_ref, ...), custom_call_target="tpu_custom_call" | custom-call | tf_op jit(solution)/shard_map/stem/pallas_call | solution.py:435
  (4 shorter events, 0.0 us)
Async XLA Ops:
  0.7 28.6 %copy-start = (f32[384,256]{1,0:T(8,128)S(1)}, f32[384,256]{1,0:T(8,128)}, u32[]{:S(2)}) copy-start(f32[384,256]{1,0:T(8,128)} %constant.5.clone.bank_ref) | copy-start | bytes 1179652
  0.8 28.5 %copy-start.1 = (bf16[9,256]{1,0:T(8,128)(2,1)S(1)}, bf16[9,256]{1,0:T(8,128)(2,1)}, u32[]{:S(2)}) copy-start(bf16[9,256]{1,0:T(8,128)(2,1)} %conv1_w_ref.1) | copy-start | bytes 13828
  0.8 28.5 %copy-start.2 = (f32[256]{0:T(256)S(1)}, f32[256]{0:T(256)}, u32[]{:S(2)}) copy-start(f32[256]{0:T(256)} %param.17) | copy-start | bytes 3076
  0.8 28.5 %copy-start.3 = (f32[256]{0:T(256)S(1)}, f32[256]{0:T(256)}, u32[]{:S(2)}) copy-start(f32[256]{0:T(256)} %param.19) | copy-start | bytes 3076
  0.8 28.5 %copy-start.4 = (f32[256]{0:T(256)S(1)}, f32[256]{0:T(256)}, u32[]{:S(2)}) copy-start(f32[256]{0:T(256)} %param.21) | copy-start | bytes 3076
  0.8 10.6 %collective-permute-start = (bf16[8,512]{1,0:T(8,128)(2,1)S(1)}, bf16[8,512]{1,0:T(8,128)(2,1)S(1)}, u32[]{:S(2)}, u32[]{:S(2)}) collective-permute-start(bf16[8,512]{1,0:T(8,128)(2,1)S(1)} %get-tuple-element.16.own0_ref), channel_id=1, source_target_pairs={{0,1},{2,3},{4,5},{6,7},{8,9},{10,11},{12,13},{14,15},{1,0},{3,2},... | collective-permute-start | bytes 24584 | tf_op jit(solution)/shard_map/ppermute | solution.py:368
  1.3 10.1 %collective-permute-start.1 = (bf16[8,512]{1,0:T(8,128)(2,1)S(1)}, bf16[8,512]{1,0:T(8,128)(2,1)S(1)}, u32[]{:S(2)}, u32[]{:S(2)}) collective-permute-start(bf16[8,512]{1,0:T(8,128)(2,1)S(1)} %get-tuple-element.17.own1_ref), channel_id=1, source_target_pairs={{1,2},{3,4},{5,6},{7,8},{9,10},{11,12},{13,14},{15,0},{2,1},{4,3},... | collective-permute-start | bytes 24584 | tf_op jit(solution)/shard_map/ppermute | solution.py:368
  11.9 1.3 %collective-permute-start.2 = (f32[136,128]{1,0:T(8,128)S(1)}, f32[136,128]{1,0:T(8,128)S(1)}, u32[]{:S(2)}, u32[]{:S(2)}) collective-permute-start(f32[136,128]{1,0:T(8,128)S(1)} %get-tuple-element.22), channel_id=1, source_target_pairs={{0,1},{1,0},{2,3},{3,2},{4,5},{5,4},{6,7},{7,6},{8,9},{9,8},{10,11... | collective-permute-start | bytes 208904 | tf_op jit(solution)/shard_map/ppermute | solution.py:350
  13.2 4.4 %collective-permute-start.3 = (f32[136,128]{1,0:T(8,128)S(1)}, f32[136,128]{1,0:T(8,128)S(1)}, u32[]{:S(2)}, u32[]{:S(2)}) collective-permute-start(f32[136,128]{1,0:T(8,128)S(1)} %add.12), channel_id=1, source_target_pairs={{0,2},{1,3},{2,0},{3,1},{4,6},{5,7},{6,4},{7,5},{8,10},{9,11},{10,... | collective-permute-start | bytes 208904 | tf_op jit(solution)/shard_map/ppermute | solution.py:350
  17.6 4.4 %collective-permute-start.4 = (f32[136,128]{1,0:T(8,128)S(1)}, f32[136,128]{1,0:T(8,128)S(1)}, u32[]{:S(2)}, u32[]{:S(2)}) collective-permute-start(f32[136,128]{1,0:T(8,128)S(1)} %add.13), channel_id=1, source_target_pairs={{0,4},{1,5},{2,6},{3,7},{4,0},{5,1},{6,2},{7,3},{8,12},{9,13},{10,... | collective-permute-start | bytes 208904 | tf_op jit(solution)/shard_map/ppermute | solution.py:350
  22.0 5.5 %collective-permute-start.5 = (f32[136,128]{1,0:T(8,128)S(1)}, f32[136,128]{1,0:T(8,128)S(1)}, u32[]{:S(2)}, u32[]{:S(2)}) collective-permute-start(f32[136,128]{1,0:T(8,128)S(1)} %add.14), channel_id=1, source_target_pairs={{0,8},{1,9},{2,10},{3,11},{4,12},{5,13},{6,14},{7,15},{8,0},{9,1},... | collective-permute-start | bytes 208904 | tf_op jit(solution)/shard_map/ppermute | solution.py:350
  28.1 1.2 %collective-permute-start.6 = (f32[16,128]{1,0:T(8,128)S(1)}, f32[16,128]{1,0:T(8,128)S(1)}, u32[]{:S(2)}, u32[]{:S(2)}) collective-permute-start(f32[16,128]{1,0:T(8,128)S(1)} %get-tuple-element.23.mine_ref), channel_id=1, source_target_pairs={{0,1},{1,0},{2,3},{3,2},{4,5},{5,4},{6,7},{7,6},{8,9},{9,8},{10,11... | collective-permute-start | bytes 24584 | tf_op jit(solution)/shard_map/ppermute | solution.py:350

commit v4 on v2

--- a/solution.py
+++ b/solution.py
@@ -57,7 +57,7 @@
         part = bank[:, half * 40 : half * 40 + SPAN]
         for copy in range(3):
             packed[:BINS, half, copy * SPAN : copy * SPAN + part.shape[1]] = part
-    return jnp.asarray(packed.reshape(PAD_BINS, 2 * LANES))
+    return jnp.asarray(packed.reshape(TILES, LANES, 2 * LANES))
 
 
 def cyclic_pairs(x_re, x_im):
@@ -93,27 +93,28 @@
     return core, 1 - core, TILES - 1
 
 
-def rims_kernel(wave_ref, beside_ref, across_ref, sem):
-    even = lax.axis_index("tm") % 2 == 0
-    last = wave_ref.shape[1] - LEAD
-    copies = []
-    for i, (out_ref, start) in enumerate(((beside_ref, jnp.where(even, last, 0)), (across_ref, jnp.where(even, 0, last)))):
-        lanes = pl.ds(pl.multiple_of(start, LANES), LEAD)
-        copies.append(pltpu.make_async_copy(wave_ref.at[:, lanes], out_ref, sem.at[i]))
-        copies[-1].start()
-    for copy in copies:
-        copy.wait()
-
-
-def stats_kernel(frames, wave_hbm, masks_hbm, table_hbm, valid_ref, spec_ref, kept_ref, edge_weight_ref, table_ref, wave_ref, masks_ref, framed_ref, weight_ref, sem):
-    copies = [
-        pltpu.make_async_copy(source, target, sem.at[i])
-        for i, (source, target) in enumerate(((wave_hbm, wave_ref), (table_hbm, table_ref), (masks_hbm, masks_ref)))
-    ]
+def started(pairs, sem):
+    copies = [pltpu.make_async_copy(source, target, sem.at[i]) for i, (source, target) in enumerate(pairs)]
     for copy in copies:
         copy.start()
+    return copies
+
+
+def rims_kernel(wave_hbm, masks_hbm, table_hbm, beside_ref, across_ref, wave_ref, masks_ref, table_ref, sem):
+    copies = started(((wave_hbm, wave_ref), (table_hbm, table_ref), (masks_hbm, masks_ref)), sem)
+    even = lax.axis_index("tm") % 2 == 0
+    copies[0].wait()
+    head = wave_ref[:, :LEAD].astype(jnp.float32)
+    tail = wave_ref[:, wave_ref.shape[1] - LEAD :].astype(jnp.float32)
+    beside_ref[...] = jnp.where(even, tail, head).astype(beside_ref.dtype)
+    across_ref[...] = jnp.where(even, head, tail).astype(across_ref.dtype)
+    copies[1].wait()
+    copies[2].wait()
+
+
+def stats_kernel(frames, wave_ref, masks_ref, table_ref, conv2_w_hbm, proj_w_hbm, valid_ref, spec_ref, kept_ref, edge_weight_ref, conv2_w_ref, proj_w_ref, framed_ref, weight_ref, sem):
+    copies = started(((conv2_w_hbm, conv2_w_ref), (proj_w_hbm, proj_w_ref)), sem)
     position = lax.axis_index("tm")
-    copies[0].wait()
     wave = wave_ref[...].astype(jnp.float32)
     width = wave.shape[1]
     rolled = {}
@@ -123,12 +124,10 @@
             rolled[shift] = wave if shift == 0 else pltpu.roll(wave, width - shift, 1)
         framed_ref[MICS * frame : MICS * (frame + 1), :] = rolled[shift][:, base : base + NFFT]
     framed_ref[MICS * (frames - HALO) :, :] = jnp.zeros((MICS * HALO, NFFT), jnp.float32)
-    copies[1].wait()
     spec = jnp.dot(framed_ref[...].astype(jnp.bfloat16), table_ref[...], preferred_element_type=jnp.float32)
     for tile in range(2 * TILES):
         spec_ref[tile] = spec[:, tile * LANES : (tile + 1) * LANES]
 
-    copies[2].wait()
     row = lax.broadcasted_iota(jnp.int32, (frames, 1), 0)
     live = jnp.where(position * frames + row < valid_ref[0], 1.0 / 255.0, 0.0)
     weight_ref[TILES - 1] = jnp.zeros((2, frames, LANES), jnp.float32)
@@ -153,17 +152,17 @@
 
         zero = jnp.zeros((MICS, LANES), jnp.float32)
         kept_ref[slot] = kept_sums(lax.fori_loop(0, frames // MICS, add_frames, (zero,) * 18))
-
-
-def edges_kernel(devices, own0_ref, own1_ref, got0_ref, got1_ref, table_ref, edge_weight_ref, kept_ref, spec_ref, mine_ref, theirs_ref, framed_ref):
+    for copy in copies:
+        copy.wait()
+
+
+def edges_kernel(own0_ref, own1_ref, got0_ref, got1_ref, table_ref, edge_weight_ref, kept_ref, spec_ref, mine_ref, theirs_ref, framed_ref):
     position = lax.axis_index("tm")
     even = position % 2 == 0
     own = [own0_ref[...].astype(jnp.float32), own1_ref[...].astype(jnp.float32)]
     got = [got0_ref[...].astype(jnp.float32), got1_ref[...].astype(jnp.float32)]
     head, tail = jnp.where(even, own[1], own[0]), jnp.where(even, own[0], own[1])
     prev, after = jnp.where(even, got[1], got[0]), jnp.where(even, got[0], got[1])
-    prev = jnp.where(position > 0, prev, 0.0)
-    after = jnp.where(position < devices - 1, after, 0.0)
     joined = jnp.concatenate(
         [jnp.concatenate([prev, head[:, :TAIL]], axis=1), jnp.concatenate([tail, after[:, :TAIL]], axis=1)], axis=0
     )
@@ -262,13 +261,37 @@
         out_ref[MICS:, :] = beam_im
 
 
-def stem_kernel(frames, mine_ref, theirs_ref, last_ref, spec_ref, edge_spec_ref, valid_ref, bank_ref, conv1_w_ref, conv1_b_ref, conv2_w_hbm, conv2_b_ref, proj_w_hbm, proj_b_ref, out_ref, power_ref, logmel_ref, conv1_ref, conv2_w_ref, proj_w_ref, sem):
-    copies = [
-        pltpu.make_async_copy(source, target, sem.at[i])
-        for i, (source, target) in enumerate(((conv2_w_hbm, conv2_w_ref), (proj_w_hbm, proj_w_ref)))
-    ]
-    for copy in copies:
-        copy.start()
+def power_of(beam_ref, tile, spec_ref, edge_spec_ref):
+    beam_re, beam_im = beam_ref[:MICS, :], beam_ref[MICS:, :]
+    groups = spec_ref.shape[1] // (MICS * MICS)
+    power = []
+    for group in range(groups + 1):
+        from_ref, first = (spec_ref, group * MICS * MICS) if group < groups else (edge_spec_ref, 0)
+        sum_re = sum_im = None
+        for m in range(MICS):
+            rows = pl.ds(first + m, MICS, stride=MICS)
+            x_re, x_im = from_ref[tile, rows, :], from_ref[TILES + tile, rows, :]
+            b_re, b_im = beam_re[m : m + 1], beam_im[m : m + 1]
+            part_re = b_re * x_re + b_im * x_im
+            part_im = b_re * x_im - b_im * x_re
+            sum_re = part_re if sum_re is None else sum_re + part_re
+            sum_im = part_im if sum_im is None else sum_im + part_im
+        power.append(sum_re * sum_re + sum_im * sum_im)
+    return jnp.concatenate(power, axis=0)
+
+
+def mel_of(power, bank):
+    return jnp.dot(power, bank, precision=lax.Precision.HIGHEST, preferred_element_type=jnp.float32)
+
+
+def power_kernel(mine_ref, last_ref, spec_ref, edge_spec_ref, bank_ref, mel_ref):
+    mine, _, last = slot_tiles(lax.axis_index("tm"))
+    power = [power_of(beam_ref, tile, spec_ref, edge_spec_ref) for beam_ref, tile in ((mine_ref, mine), (last_ref, last))]
+    bank = jnp.concatenate([bank_ref[mine], bank_ref[last]], axis=0)
+    mel_ref[...] = mel_of(jnp.concatenate(power, axis=1), bank)
+
+
+def stem_kernel(frames, theirs_ref, mel_ref, spec_ref, edge_spec_ref, valid_ref, bank_ref, conv1_w_ref, conv1_b_ref, conv2_w_ref, conv2_b_ref, proj_w_ref, proj_b_ref, out_ref, logmel_ref, conv1_ref):
     position = lax.axis_index("tm")
     valid = valid_ref[0]
     quarter = frames // 4
@@ -278,23 +301,8 @@
         conv1_ref[SPAN * shift_t : SPAN * shift_t + 3, :] = conv1_w_ref[3 * shift_t : 3 * shift_t + 3, :].astype(jnp.float32)
     conv1 = conv1_ref[...].astype(jnp.bfloat16)
 
-    groups = frames // MICS
-    for beam_ref, tile in zip((mine_ref, theirs_ref, last_ref), slot_tiles(position)):
-        beam_re, beam_im = beam_ref[:MICS, :], beam_ref[MICS:, :]
-        for group in range(groups + 1):
-            from_ref, first = (spec_ref, group * MICS * MICS) if group < groups else (edge_spec_ref, 0)
-            sum_re = sum_im = None
-            for m in range(MICS):
-                rows = pl.ds(first + m, MICS, stride=MICS)
-                x_re, x_im = from_ref[tile, rows, :], from_ref[TILES + tile, rows, :]
-                b_re, b_im = beam_re[m : m + 1], beam_im[m : m + 1]
-                part_re = b_re * x_re + b_im * x_im
-                part_im = b_re * x_im - b_im * x_re
-                sum_re = part_re if sum_re is None else sum_re + part_re
-                sum_im = part_im if sum_im is None else sum_im + part_im
-            power_ref[tile, group * MICS : (group + 1) * MICS, :] = sum_re * sum_re + sum_im * sum_im
-    power = jnp.concatenate([power_ref[tile] for tile in range(TILES)], axis=1)
-    mel = jnp.dot(power, bank_ref[...], precision=lax.Precision.HIGHEST, preferred_element_type=jnp.float32)
+    theirs = slot_tiles(position)[1]
+    mel = mel_ref[...] + mel_of(power_of(theirs_ref, theirs, spec_ref, edge_spec_ref), bank_ref[theirs])
     row = lax.broadcasted_iota(jnp.int32, (frames + MICS, 1), 0)
     edge = (row - frames) // 2 + jnp.where((row - frames) % 2 == 0, -HALO, frames - HALO)
     time = position * frames + jnp.where(row < frames, row, edge)
@@ -335,11 +343,9 @@
         windows.append(layer[:count])
         windows.append(layer[quarter * evens : quarter * evens + count])
         windows.append(layer[quarter : quarter + count])
-    copies[0].wait()
     second = jnp.dot(jnp.concatenate(windows, axis=1), conv2_w_ref[...], preferred_element_type=jnp.float32)
     second = jnp.maximum(second + conv2_b_ref[...], 0.0).astype(jnp.bfloat16)
     flat = jnp.concatenate([second[quarter * r : quarter * (r + 1)] for r in range(q_second)], axis=1)
-    copies[1].wait()
     features = jnp.dot(flat, proj_w_ref[...], preferred_element_type=jnp.float32) + proj_b_ref[...]
     features = jnp.where(position * frames + 4 * row < valid, features, 0.0)
     out_ref[0] = features.astype(jnp.bfloat16)
@@ -362,10 +368,8 @@
 
 
 def paired(block, axis, first):
-    size = lax.axis_size(axis)
-    lower = range(first, size, 2)
-    route = [(i, (i + 1) % size) for i in lower] + [((i + 1) % size, i) for i in lower]
-    return lax.ppermute(block, axis, route)
+    lower = range(first, lax.axis_size(axis) - 1, 2)
+    return lax.ppermute(block, axis, [(i, i + 1) for i in lower] + [(i + 1, i) for i in lower])
 
 
 def per_device(waveform, masks, valid, ref_mic, conv1_w, conv1_b, conv2_w, conv2_b, proj_w, proj_b):
@@ -375,43 +379,44 @@
     vmem = pl.BlockSpec(memory_space=pltpu.VMEM)
     smem = pl.BlockSpec(memory_space=pltpu.SMEM)
     hbm = pl.BlockSpec(memory_space=pltpu.HBM)
-    params = pltpu.CompilerParams(vmem_limit_bytes=20 * 1024 * 1024)
+    in_hbm = functools.partial(pltpu.with_memory_space_constraint, memory_space=pltpu.HBM)
+    params = pltpu.CompilerParams(vmem_limit_bytes=16 * 1024 * 1024)
     rim = jax.ShapeDtypeStruct((MICS, LEAD), waveform.dtype)
-    beside, across = pl.pallas_call(
+    table = dft_table()
+    conv2_w = conv2_w.reshape(-1, channels)
+    beside, across, waves, levels, table = pl.pallas_call(
         rims_kernel,
-        out_shape=(rim, rim),
-        in_specs=[hbm],
-        out_specs=(vmem, vmem),
-        scratch_shapes=[pltpu.SemaphoreType.DMA((2,))],
+        out_shape=(rim, rim) + tuple(jax.ShapeDtypeStruct(x.shape, x.dtype) for x in (waveform, masks, table)),
+        in_specs=[hbm] * 3,
+        out_specs=(vmem,) * 5,
+        scratch_shapes=[pltpu.SemaphoreType.DMA((3,))],
         compiler_params=params,
         name="rims",
-    )(waveform)
+    )(in_hbm(waveform), in_hbm(masks), in_hbm(table))
     got_across = paired(across, "tm", 1)
     got_beside = paired(beside, "tm", 0)
-    table = dft_table()
     stat_block = jax.ShapeDtypeStruct((STATS + MICS, LANES), jnp.float32)
-    spec, kept, edge_weight, table = pl.pallas_call(
+    spec, kept, edge_weight, conv2_w, proj_w = pl.pallas_call(
         functools.partial(stats_kernel, frames),
         out_shape=(
             jax.ShapeDtypeStruct((2 * TILES, frames * MICS, LANES), jnp.float32),
             jax.ShapeDtypeStruct((TILES, STATS, LANES), jnp.float32),
             jax.ShapeDtypeStruct((TILES, 2, MICS, LANES), jnp.float32),
-            jax.ShapeDtypeStruct(table.shape, table.dtype),
+            jax.ShapeDtypeStruct(conv2_w.shape, conv2_w.dtype),
+            jax.ShapeDtypeStruct(proj_w.shape, proj_w.dtype),
         ),
-        in_specs=[hbm, hbm, hbm, smem],
-        out_specs=(vmem,) * 4,
+        in_specs=[vmem] * 3 + [hbm] * 2 + [smem],
+        out_specs=(vmem,) * 5,
         scratch_shapes=[
-            pltpu.VMEM(waveform.shape, waveform.dtype),
-            pltpu.VMEM(masks.shape, masks.dtype),
             pltpu.VMEM((frames * MICS, NFFT), jnp.float32),
             pltpu.VMEM((TILES, 2, frames, LANES), jnp.float32),
-            pltpu.SemaphoreType.DMA((3,)),
+            pltpu.SemaphoreType.DMA((2,)),
         ],
         compiler_params=params,
         name="stats",
-    )(waveform, masks, table, valid)
+    )(waves, levels, table, in_hbm(conv2_w), in_hbm(proj_w), valid)
     edge_spec, mine, theirs = pl.pallas_call(
-        functools.partial(edges_kernel, lax.axis_size("tm")),
+        edges_kernel,
         out_shape=(jax.ShapeDtypeStruct((2 * TILES, MICS * MICS, LANES), jnp.float32), stat_block, stat_block),
         in_specs=[vmem] * 7,
         out_specs=(vmem,) * 3,
@@ -431,32 +436,33 @@
     )(stats, ref_mic)
     beam_theirs = flipped(beam_mine, "tm", 1)
     rows = frames + MICS
+    bank = packed_mel_bank()
+    mel = pl.pallas_call(
+        power_kernel,
+        out_shape=jax.ShapeDtypeStruct((rows, 2 * LANES), jnp.float32),
+        in_specs=[vmem] * 5,
+        out_specs=vmem,
+        compiler_params=params,
+        name="power",
+    )(beam_mine, beam_last, spec, edge_spec, bank)
     return pl.pallas_call(
         functools.partial(stem_kernel, frames),
         out_shape=jax.ShapeDtypeStruct((1, frames // 4, width), jnp.bfloat16),
-        in_specs=[vmem] * 5 + [smem] + [vmem] * 3 + [hbm, vmem, hbm, vmem],
+        in_specs=[vmem] * 4 + [smem] + [vmem] * 7,
         out_specs=vmem,
-        scratch_shapes=[
-            pltpu.VMEM((TILES, rows, LANES), jnp.float32),
-            pltpu.VMEM((2, rows, LANES), jnp.float32),
-            pltpu.VMEM((LANES, channels), jnp.float32),
-            pltpu.VMEM((9 * channels, channels), conv2_w.dtype),
-            pltpu.VMEM(proj_w.shape, proj_w.dtype),
-            pltpu.SemaphoreType.DMA((2,)),
-        ],
+        scratch_shapes=[pltpu.VMEM((2, rows, LANES), jnp.float32), pltpu.VMEM((LANES, channels), jnp.float32)],
         compiler_params=params,
         name="stem",
     )(
-        beam_mine,
         beam_theirs,
-        beam_last,
+        mel,
         spec,
         edge_spec,
         valid,
-        packed_mel_bank(),
+        bank,
         conv1_w,
         conv1_b[None],
-        conv2_w.reshape(-1, channels),
+        conv2_w,
         conv2_b[None],
         proj_w,
         proj_b[None],

time: 36.7 us -> 30 us (0.82)
  waiting for transfers between devices: 15.7 us -> 9.05 us
  starting transfers between devices: 6.51 us -> 11.2 us
  local copies, waits for them, and re-layouts: 4.26 us -> 0.02 us
    ppermute x5, starting transfers between devices: 0.33 us -> 10.1 us  [flipped(): return lax.ppermute(block, axis, [(i, i ^ step) for i in range(size)])]
    ppermute x5, waiting for transfers between devices: 15.7 us -> 9.05 us  [flipped(): return lax.ppermute(block, axis, [(i, i ^ step) for i in range(size)])]
    ppermute x2, starting transfers between devices: 6.18 us -> 1.17 us  [paired(): lax.ppermute(block, axis, [(i, i + 1) for i in lower] + [(i + 1, i) for i...]
    unnamed x20 -> x10, local copies, waits for them, and re-layouts: 4.26 us -> 0.02 us
    pallas_call x2 -> x3, Pallas kernels: 0.5 us -> 2.17 us  [the longest x1 1.27 us: per_device(): pl.pallas_call(rims_kernel, out_shape=(rim, rim) + tuple((jax.ShapeDtypeS...]
    pallas_call x1, Pallas kernels: 4.06 us -> 2.69 us  [per_device(): pl.pallas_call(functools.partial(stem_kernel, frames), out_shape=jax.Shap...]
    pallas_call x1, Pallas kernels: 3.26 us -> 2.59 us  [per_device(): pl.pallas_call(functools.partial(stats_kernel, frames), out_shape=(jax.Sh...]
  transfers between devices with their start and end apart: 7 -> 7, of which waited for: 5 -> 5; matrix products, arithmetic and copies ran while one was open for 0% -> 0% of each run, Pallas kernels for 9% -> 10%
where the time goes in v4:
time: 30 us; the launch traced here: 29.8 us
  starting transfers between devices  11.2 us (37%)
  waiting for transfers between devices  9.05 us (30%)
  Pallas kernels  8.05 us (27%)
  between operations  1.41 us (5%)
    ppermute x5, starting transfers between devices, flipped(): return lax.ppermute(block, axis, [(i, i ^ step) for i in range(size)])  10.1 us
    ppermute x5, waiting for transfers between devices, flipped(): return lax.ppermute(block, axis, [(i, i ^ step) for i in range(size)])  9.05 us
    pallas_call x1, Pallas kernels, per_device(): pl.pallas_call(functools.partial(stem_kernel, frames), out_shape=jax.Shap...  2.69 us
    pallas_call x1, Pallas kernels, per_device(): pl.pallas_call(functools.partial(stats_kernel, frames), out_shape=(jax.Sh...  2.59 us
    pallas_call x1, Pallas kernels, per_device(): pl.pallas_call(rims_kernel, out_shape=(rim, rim) + tuple((jax.ShapeDtypeS...  1.27 us
    ppermute x2, starting transfers between devices, paired(): lax.ppermute(block, axis, [(i, i + 1) for i in lower] + [(i + 1, i) for i...  1.17 us
  transfers between devices with their start and end apart: 7, of which 5 were waited for; matrix products, arithmetic and copies ran while one was open for 0% of the time, Pallas kernels for 10%

profile of v4, /device:TPU:0, one launch (start us, length us, event | category | flops | bytes accessed | tf_op | source)
XLA Modules:
  0.0 29.8 jit_solution(1916065824030762316)
XLA Ops:
  0.0 1.3 %rims.1 = (bf16[8,512]{1,0:T(8,128)(2,1)S(1)}, bf16[8,512]{1,0:T(8,128)(2,1)S(1)}, bf16[8,10240]{1,0:T(8,128)(2,1)S(1)}, s32[2,64,257]{2,1,0:T(8,128)S(1)}, bf16[512,768]{1,0:T(8,128)(2,1)S(1)}) custom-call(bf16[8,10240]{1,0:T(8,128)(2,1)} %wave_hbm.1, s32[2,64,257]{2,1,0:T(8,128)} %masks_hbm.1, bf16[512,768]{1,0:T(8,128)(2,1)} %constant.8.table_hbm), custom_call_target="tpu_custom_call" | custom-call | tf_op jit(solution)/shard_map/rims/pallas_call | solution.py:387
  1.3 0.5 %collective-permute-start = (bf16[8,512]{1,0:T(8,128)(2,1)S(1)}, bf16[8,512]{1,0:T(8,128)(2,1)S(1)}, u32[]{:S(2)}, u32[]{:S(2)}) collective-permute-start(bf16[8,512]{1,0:T(8,128)(2,1)S(1)} %get-tuple-element.20.own0_ref), channel_id=1, source_target_pairs={{0,1},{2,3},{4,5},{6,7},{8,9},{10,11},{12,13},{14,15},{1,0},{3,2},... | collective-permute-start | bytes 24584 | tf_op jit(solution)/shard_map/ppermute | solution.py:372
  1.8 0.6 %collective-permute-start.1 = (bf16[8,512]{1,0:T(8,128)(2,1)S(1)}, bf16[8,512]{1,0:T(8,128)(2,1)S(1)}, u32[]{:S(2)}, u32[]{:S(2)}) collective-permute-start(bf16[8,512]{1,0:T(8,128)(2,1)S(1)} %get-tuple-element.21.own1_ref), channel_id=1, source_target_pairs={{1,2},{3,4},{5,6},{7,8},{9,10},{11,12},{13,14},{2,1},{4,3},{6,5},{... | collective-permute-start | bytes 24584 | tf_op jit(solution)/shard_map/ppermute | solution.py:372
  3.1 2.6 %stats.1 = (f32[6,512,128]{2,1,0:T(8,128)S(1)}, f32[3,128,128]{2,1,0:T(8,128)S(1)}, f32[3,2,8,128]{3,2,1,0:T(8,128)S(1)}, bf16[2304,256]{1,0:T(8,128)(2,1)S(1)}, bf16[4864,256]{1,0:T(8,128)(2,1)S(1)}) custom-call(bf16[8,10240]{1,0:T(8,128)(2,1)S(1)} %get-tuple-element.23.wave_ref, s32[2,64,257]{2,1,0:T(8,128)S(1)} %get-tuple-element.24.masks_ref, ...), custom_call_target="tpu_custom_call" | custom-call | tf_op jit(solution)/shard_map/stats/pallas_call | solution.py:399
  5.7 0.0 copy-start
  5.7 0.0 collective-permute-done.got0_ref
  5.7 0.0 collective-permute-done.1.got1_ref
  5.7 0.4 %edges.1 = (f32[6,64,128]{2,1,0:T(8,128)S(1)}, f32[136,128]{1,0:T(8,128)S(1)}, f32[136,128]{1,0:T(8,128)S(1)}) custom-call(bf16[8,512]{1,0:T(8,128)(2,1)S(1)} %get-tuple-element.20.own0_ref, bf16[8,512]{1,0:T(8,128)(2,1)S(1)} %get-tuple-element.21.own1_ref, bf16[8,512]{1,0:T(8,128)(2,1)S(1)} %collective-permute-done.got0_ref, ...), custom_call_target="tpu_custom_call" | custom-call | tf_op jit(solution)/shard_map/edges/pallas_call | solution.py:418
  6.2 3.9 %collective-permute-start.2 = (f32[136,128]{1,0:T(8,128)S(1)}, f32[136,128]{1,0:T(8,128)S(1)}, u32[]{:S(2)}, u32[]{:S(2)}) collective-permute-start(f32[136,128]{1,0:T(8,128)S(1)} %get-tuple-element.28), channel_id=1, source_target_pairs={{0,1},{1,0},{2,3},{3,2},{4,5},{5,4},{6,7},{7,6},{8,9},{9,8},{10,11... | collective-permute-start | bytes 208904 | tf_op jit(solution)/shard_map/ppermute | solution.py:356
  10.1 0.9 %collective-permute-done.2 = f32[136,128]{1,0:T(8,128)S(1)} collective-permute-done((f32[136,128]{1,0:T(8,128)S(1)}, f32[136,128]{1,0:T(8,128)S(1)}, u32[]{:S(2)}, u32[]{:S(2)}) %collective-permute-start.2) | collective-permute-done | bytes 69664 | tf_op jit(solution)/shard_map/ppermute | solution.py:356
  11.0 0.0 copy-start.1
  11.0 0.0 copy-start.2
  11.0 0.0 copy-start.3
  11.0 0.0 copy-start.4
  11.1 1.6 %collective-permute-start.3 = (f32[136,128]{1,0:T(8,128)S(1)}, f32[136,128]{1,0:T(8,128)S(1)}, u32[]{:S(2)}, u32[]{:S(2)}) collective-permute-start(f32[136,128]{1,0:T(8,128)S(1)} %add.12), channel_id=1, source_target_pairs={{0,2},{1,3},{2,0},{3,1},{4,6},{5,7},{6,4},{7,5},{8,10},{9,11},{10,... | collective-permute-start | bytes 208904 | tf_op jit(solution)/shard_map/ppermute | solution.py:356
  12.6 2.9 %collective-permute-done.3 = f32[136,128]{1,0:T(8,128)S(1)} collective-permute-done((f32[136,128]{1,0:T(8,128)S(1)}, f32[136,128]{1,0:T(8,128)S(1)}, u32[]{:S(2)}, u32[]{:S(2)}) %collective-permute-start.3) | collective-permute-done | bytes 69664 | tf_op jit(solution)/shard_map/ppermute | solution.py:356
  15.6 1.7 %collective-permute-start.4 = (f32[136,128]{1,0:T(8,128)S(1)}, f32[136,128]{1,0:T(8,128)S(1)}, u32[]{:S(2)}, u32[]{:S(2)}) collective-permute-start(f32[136,128]{1,0:T(8,128)S(1)} %add.13), channel_id=1, source_target_pairs={{0,4},{1,5},{2,6},{3,7},{4,0},{5,1},{6,2},{7,3},{8,12},{9,13},{10,... | collective-permute-start | bytes 208904 | tf_op jit(solution)/shard_map/ppermute | solution.py:356
  17.3 2.7 %collective-permute-done.4 = f32[136,128]{1,0:T(8,128)S(1)} collective-permute-done((f32[136,128]{1,0:T(8,128)S(1)}, f32[136,128]{1,0:T(8,128)S(1)}, u32[]{:S(2)}, u32[]{:S(2)}) %collective-permute-start.4) | collective-permute-done | bytes 69664 | tf_op jit(solution)/shard_map/ppermute | solution.py:356
  20.0 2.7 %collective-permute-start.5 = (f32[136,128]{1,0:T(8,128)S(1)}, f32[136,128]{1,0:T(8,128)S(1)}, u32[]{:S(2)}, u32[]{:S(2)}) collective-permute-start(f32[136,128]{1,0:T(8,128)S(1)} %add.14), channel_id=1, source_target_pairs={{0,8},{1,9},{2,10},{3,11},{4,12},{5,13},{6,14},{7,15},{8,0},{9,1},... | collective-permute-start | bytes 208904 | tf_op jit(solution)/shard_map/ppermute | solution.py:356
  23.3 1.9 %collective-permute-done.5 = f32[136,128]{1,0:T(8,128)S(1)} collective-permute-done((f32[136,128]{1,0:T(8,128)S(1)}, f32[136,128]{1,0:T(8,128)S(1)}, u32[]{:S(2)}, u32[]{:S(2)}) %collective-permute-start.5) | collective-permute-done | bytes 69664 | tf_op jit(solution)/shard_map/ppermute | solution.py:356
  25.2 0.6 %solve.1 = (f32[16,128]{1,0:T(8,128)S(1)}, f32[16,128]{1,0:T(8,128)S(1)}) custom-call(f32[136,128]{1,0:T(8,128)S(1)} %add.15.stats_ref, s32[1]{0:T(128)S(6)} %copy.14.ref_mic_ref), custom_call_target="tpu_custom_call" | custom-call | tf_op jit(solution)/shard_map/solve/pallas_call | solution.py:429
  25.8 0.1 collective-permute-start.6
  25.9 0.0 copy-done
  25.9 0.5 %power.1.mel_ref = f32[72,256]{1,0:T(8,128)S(1)} custom-call(f32[16,128]{1,0:T(8,128)S(1)} %get-tuple-element.29.mine_ref, f32[16,128]{1,0:T(8,128)S(1)} %get-tuple-element.30.last_ref, f32[6,512,128]{2,1,0:T(8,128)S(1)} %get-tuple-element.31.spec_ref, f32[6,64,128]{2,1,0:T(8,128)S(1)} %get-tuple-element.32.edge_spec_ref, f32[3,128,256]{2,1,0:T(8,128)S(1)} %copy-done), custom_call_target="tpu_custom_call" | custom-call | tf_op jit(solution)/shard_map/power/pallas_call | solution.py:440
  26.4 0.7 %collective-permute-done.6.theirs_ref = f32[16,128]{1,0:T(8,128)S(1)} collective-permute-done((f32[16,128]{1,0:T(8,128)S(1)}, f32[16,128]{1,0:T(8,128)S(1)}, u32[]{:S(2)}, u32[]{:S(2)}) %collective-permute-start.6) | collective-permute-done | bytes 8224 | tf_op jit(solution)/shard_map/ppermute | solution.py:356
  27.1 0.0 copy-done.1
  27.1 0.0 copy-done.2
  27.1 0.0 copy-done.3
  27.1 0.0 copy-done.4
  27.1 2.7 %stem.1 = bf16[1,16,256]{2,1,0:T(8,128)(2,1)} custom-call(f32[16,128]{1,0:T(8,128)S(1)} %collective-permute-done.6.theirs_ref, f32[72,256]{1,0:T(8,128)S(1)} %power.1.mel_ref, f32[6,512,128]{2,1,0:T(8,128)S(1)} %get-tuple-element.31.spec_ref, f32[6,64,128]{2,1,0:T(8,128)S(1)} %get-tuple-element.32.edge_spec_ref, s32[1]{0:T(128)S(6)} %copy.13.valid_ref, ...), custom_call_target="tpu_custom_call" | custom-call | tf_op jit(solution)/shard_map/stem/pallas_call | solution.py:448
  (4 shorter events, 0.0 us)
Async XLA Ops:
  1.3 4.4 %collective-permute-start = (bf16[8,512]{1,0:T(8,128)(2,1)S(1)}, bf16[8,512]{1,0:T(8,128)(2,1)S(1)}, u32[]{:S(2)}, u32[]{:S(2)}) collective-permute-start(bf16[8,512]{1,0:T(8,128)(2,1)S(1)} %get-tuple-element.20.own0_ref), channel_id=1, source_target_pairs={{0,1},{2,3},{4,5},{6,7},{8,9},{10,11},{12,13},{14,15},{1,0},{3,2},... | collective-permute-start | bytes 24584 | tf_op jit(solution)/shard_map/ppermute | solution.py:372
  1.8 3.9 %collective-permute-start.1 = (bf16[8,512]{1,0:T(8,128)(2,1)S(1)}, bf16[8,512]{1,0:T(8,128)(2,1)S(1)}, u32[]{:S(2)}, u32[]{:S(2)}) collective-permute-start(bf16[8,512]{1,0:T(8,128)(2,1)S(1)} %get-tuple-element.21.own1_ref), channel_id=1, source_target_pairs={{1,2},{3,4},{5,6},{7,8},{9,10},{11,12},{13,14},{2,1},{4,3},{6,5},{... | collective-permute-start | bytes 24584 | tf_op jit(solution)/shard_map/ppermute | solution.py:372
  5.7 20.2 %copy-start = (f32[3,128,256]{2,1,0:T(8,128)S(1)}, f32[3,128,256]{2,1,0:T(8,128)}, u32[]{:S(2)}) copy-start(f32[3,128,256]{2,1,0:T(8,128)} %constant.5.clone.bank_ref) | copy-start | bytes 1179652
  6.2 4.8 %collective-permute-start.2 = (f32[136,128]{1,0:T(8,128)S(1)}, f32[136,128]{1,0:T(8,128)S(1)}, u32[]{:S(2)}, u32[]{:S(2)}) collective-permute-start(f32[136,128]{1,0:T(8,128)S(1)} %get-tuple-element.28), channel_id=1, source_target_pairs={{0,1},{1,0},{2,3},{3,2},{4,5},{5,4},{6,7},{7,6},{8,9},{9,8},{10,11... | collective-permute-start | bytes 208904 | tf_op jit(solution)/shard_map/ppermute | solution.py:356
  11.0 16.1 %copy-start.1 = (bf16[9,256]{1,0:T(8,128)(2,1)S(1)}, bf16[9,256]{1,0:T(8,128)(2,1)}, u32[]{:S(2)}) copy-start(bf16[9,256]{1,0:T(8,128)(2,1)} %conv1_w_ref.1) | copy-start | bytes 13828
  11.0 16.1 %copy-start.2 = (f32[256]{0:T(256)S(1)}, f32[256]{0:T(256)}, u32[]{:S(2)}) copy-start(f32[256]{0:T(256)} %param.17) | copy-start | bytes 3076
  11.0 16.1 %copy-start.3 = (f32[256]{0:T(256)S(1)}, f32[256]{0:T(256)}, u32[]{:S(2)}) copy-start(f32[256]{0:T(256)} %param.19) | copy-start | bytes 3076
  11.0 16.1 %copy-start.4 = (f32[256]{0:T(256)S(1)}, f32[256]{0:T(256)}, u32[]{:S(2)}) copy-start(f32[256]{0:T(256)} %param.21) | copy-start | bytes 3076
  11.1 4.5 %collective-permute-start.3 = (f32[136,128]{1,0:T(8,128)S(1)}, f32[136,128]{1,0:T(8,128)S(1)}, u32[]{:S(2)}, u32[]{:S(2)}) collective-permute-start(f32[136,128]{1,0:T(8,128)S(1)} %add.12), channel_id=1, source_target_pairs={{0,2},{1,3},{2,0},{3,1},{4,6},{5,7},{6,4},{7,5},{8,10},{9,11},{10,... | collective-permute-start | bytes 208904 | tf_op jit(solution)/shard_map/ppermute | solution.py:356
  15.6 4.4 %collective-permute-start.4 = (f32[136,128]{1,0:T(8,128)S(1)}, f32[136,128]{1,0:T(8,128)S(1)}, u32[]{:S(2)}, u32[]{:S(2)}) collective-permute-start(f32[136,128]{1,0:T(8,128)S(1)} %add.13), channel_id=1, source_target_pairs={{0,4},{1,5},{2,6},{3,7},{4,0},{5,1},{6,2},{7,3},{8,12},{9,13},{10,... | collective-permute-start | bytes 208904 | tf_op jit(solution)/shard_map/ppermute | solution.py:356
  20.0 5.3 %collective-permute-start.5 = (f32[136,128]{1,0:T(8,128)S(1)}, f32[136,128]{1,0:T(8,128)S(1)}, u32[]{:S(2)}, u32[]{:S(2)}) collective-permute-start(f32[136,128]{1,0:T(8,128)S(1)} %add.14), channel_id=1, source_target_pairs={{0,8},{1,9},{2,10},{3,11},{4,12},{5,13},{6,14},{7,15},{8,0},{9,1},... | collective-permute-start | bytes 208904 | tf_op jit(solution)/shard_map/ppermute | solution.py:356
  25.8 1.2 %collective-permute-start.6 = (f32[16,128]{1,0:T(8,128)S(1)}, f32[16,128]{1,0:T(8,128)S(1)}, u32[]{:S(2)}, u32[]{:S(2)}) collective-permute-start(f32[16,128]{1,0:T(8,128)S(1)} %get-tuple-element.29.mine_ref), channel_id=1, source_target_pairs={{0,1},{1,0},{2,3},{3,2},{4,5},{5,4},{6,7},{7,6},{8,9},{9,8},{10,11... | collective-permute-start | bytes 24584 | tf_op jit(solution)/shard_map/ppermute | solution.py:356

commit v5 on v4

--- a/solution.py
+++ b/solution.py
@@ -156,13 +156,15 @@
         copy.wait()
 
 
-def edges_kernel(own0_ref, own1_ref, got0_ref, got1_ref, table_ref, edge_weight_ref, kept_ref, spec_ref, mine_ref, theirs_ref, framed_ref):
+def edges_kernel(devices, own0_ref, own1_ref, got0_ref, got1_ref, table_ref, edge_weight_ref, kept_ref, spec_ref, mine_ref, theirs_ref, framed_ref):
     position = lax.axis_index("tm")
     even = position % 2 == 0
     own = [own0_ref[...].astype(jnp.float32), own1_ref[...].astype(jnp.float32)]
     got = [got0_ref[...].astype(jnp.float32), got1_ref[...].astype(jnp.float32)]
     head, tail = jnp.where(even, own[1], own[0]), jnp.where(even, own[0], own[1])
     prev, after = jnp.where(even, got[1], got[0]), jnp.where(even, got[0], got[1])
+    prev = jnp.where(position > 0, prev, 0.0)
+    after = jnp.where(position < devices - 1, after, 0.0)
     joined = jnp.concatenate(
         [jnp.concatenate([prev, head[:, :TAIL]], axis=1), jnp.concatenate([tail, after[:, :TAIL]], axis=1)], axis=0
     )
@@ -362,14 +364,16 @@
         return lax.psum(block, axis, axis_index_groups=[list(range(c, size, 2)) for c in range(2)])
     step = 2
     while step < size:
-        block = block + flipped(block, axis, step)
-        step *= 2
+        others = [step] if 2 * step >= size else [step, 2 * step, 3 * step]
+        block = sum([flipped(block, axis, other) for other in others], block)
+        step *= 4
     return block
 
 
 def paired(block, axis, first):
-    lower = range(first, lax.axis_size(axis) - 1, 2)
-    return lax.ppermute(block, axis, [(i, i + 1) for i in lower] + [(i + 1, i) for i in lower])
+    size = lax.axis_size(axis)
+    lower = range(first, size, 2)
+    return lax.ppermute(block, axis, [(i, (i + 1) % size) for i in lower] + [((i + 1) % size, i) for i in lower])
 
 
 def per_device(waveform, masks, valid, ref_mic, conv1_w, conv1_b, conv2_w, conv2_b, proj_w, proj_b):
@@ -416,7 +420,7 @@
         name="stats",
     )(waves, levels, table, in_hbm(conv2_w), in_hbm(proj_w), valid)
     edge_spec, mine, theirs = pl.pallas_call(
-        edges_kernel,
+        functools.partial(edges_kernel, lax.axis_size("tm")),
         out_shape=(jax.ShapeDtypeStruct((2 * TILES, MICS * MICS, LANES), jnp.float32), stat_block, stat_block),
         in_specs=[vmem] * 7,
         out_specs=(vmem,) * 3,

time: 30 us -> 30.1 us (level)
  starting transfers between devices: 11.2 us -> 11.9 us
  waiting for transfers between devices: 9.05 us -> 8.55 us
    ppermute x2, starting transfers between devices: 1.17 us -> 6.18 us  [paired(): lax.ppermute(block, axis, [(i, (i + 1) % size) for i in lower] + [((i + 1...]
    ppermute x5 -> x6, starting transfers between devices: 10.1 us -> 5.69 us  [flipped(): return lax.ppermute(block, axis, [(i, i ^ step) for i in range(size)])]
    ppermute x5 -> x6, waiting for transfers between devices: 9.05 us -> 8.54 us  [flipped(): return lax.ppermute(block, axis, [(i, i ^ step) for i in range(size)])]
  transfers between devices with their start and end apart: 7 -> 8, of which waited for: 5 -> 6; matrix products, arithmetic and copies ran while one was open for 0% -> 0% of each run, Pallas kernels for 10% -> 10%
where the time goes in v5:
time: 30.1 us; the launch traced here: 30 us
  starting transfers between devices  11.9 us (40%)
  waiting for transfers between devices  8.55 us (28%)
  Pallas kernels  8.05 us (27%)
  between operations  1.43 us (5%)
    ppermute x6, waiting for transfers between devices, flipped(): return lax.ppermute(block, axis, [(i, i ^ step) for i in range(size)])  8.54 us
    ppermute x2, starting transfers between devices, paired(): lax.ppermute(block, axis, [(i, (i + 1) % size) for i in lower] + [((i + 1...  6.18 us
    ppermute x6, starting transfers between devices, flipped(): return lax.ppermute(block, axis, [(i, i ^ step) for i in range(size)])  5.69 us
    pallas_call x1, Pallas kernels, per_device(): pl.pallas_call(functools.partial(stem_kernel, frames), out_shape=jax.Shap...  2.7 us
    pallas_call x1, Pallas kernels, per_device(): pl.pallas_call(functools.partial(stats_kernel, frames), out_shape=(jax.Sh...  2.59 us
    pallas_call x1, Pallas kernels, per_device(): pl.pallas_call(rims_kernel, out_shape=(rim, rim) + tuple((jax.ShapeDtypeS...  1.27 us
  transfers between devices with their start and end apart: 8, of which 6 were waited for; matrix products, arithmetic and copies ran while one was open for 0% of the time, Pallas kernels for 10%

profile of v5, /device:TPU:0, one launch (start us, length us, event | category | flops | bytes accessed | tf_op | source)
XLA Modules:
  0.0 30.0 jit_solution(7683647742164505864)
XLA Ops:
  0.0 1.3 %rims.1 = (bf16[8,512]{1,0:T(8,128)(2,1)S(1)}, bf16[8,512]{1,0:T(8,128)(2,1)S(1)}, bf16[8,10240]{1,0:T(8,128)(2,1)S(1)}, s32[2,64,257]{2,1,0:T(8,128)S(1)}, bf16[512,768]{1,0:T(8,128)(2,1)S(1)}) custom-call(bf16[8,10240]{1,0:T(8,128)(2,1)} %wave_hbm.1, s32[2,64,257]{2,1,0:T(8,128)} %masks_hbm.1, bf16[512,768]{1,0:T(8,128)(2,1)} %constant.8.table_hbm), custom_call_target="tpu_custom_call" | custom-call | tf_op jit(solution)/shard_map/rims/pallas_call | solution.py:391
  1.3 0.5 %collective-permute-start = (bf16[8,512]{1,0:T(8,128)(2,1)S(1)}, bf16[8,512]{1,0:T(8,128)(2,1)S(1)}, u32[]{:S(2)}, u32[]{:S(2)}) collective-permute-start(bf16[8,512]{1,0:T(8,128)(2,1)S(1)} %get-tuple-element.20.own0_ref), channel_id=1, source_target_pairs={{0,1},{2,3},{4,5},{6,7},{8,9},{10,11},{12,13},{14,15},{1,0},{3,2},... | collective-permute-start | bytes 24584 | tf_op jit(solution)/shard_map/ppermute | solution.py:376
  1.8 5.7 %collective-permute-start.1 = (bf16[8,512]{1,0:T(8,128)(2,1)S(1)}, bf16[8,512]{1,0:T(8,128)(2,1)S(1)}, u32[]{:S(2)}, u32[]{:S(2)}) collective-permute-start(bf16[8,512]{1,0:T(8,128)(2,1)S(1)} %get-tuple-element.21.own1_ref), channel_id=1, source_target_pairs={{1,2},{3,4},{5,6},{7,8},{9,10},{11,12},{13,14},{15,0},{2,1},{4,3},... | collective-permute-start | bytes 24584 | tf_op jit(solution)/shard_map/ppermute | solution.py:376
  8.1 2.6 %stats.1 = (f32[6,512,128]{2,1,0:T(8,128)S(1)}, f32[3,128,128]{2,1,0:T(8,128)S(1)}, f32[3,2,8,128]{3,2,1,0:T(8,128)S(1)}, bf16[2304,256]{1,0:T(8,128)(2,1)S(1)}, bf16[4864,256]{1,0:T(8,128)(2,1)S(1)}) custom-call(bf16[8,10240]{1,0:T(8,128)(2,1)S(1)} %get-tuple-element.23.wave_ref, s32[2,64,257]{2,1,0:T(8,128)S(1)} %get-tuple-element.24.masks_ref, ...), custom_call_target="tpu_custom_call" | custom-call | tf_op jit(solution)/shard_map/stats/pallas_call | solution.py:403
  10.7 0.0 copy-start
  10.7 0.0 collective-permute-done.got0_ref
  10.7 0.0 collective-permute-done.1.got1_ref
  10.8 0.4 %edges.1 = (f32[6,64,128]{2,1,0:T(8,128)S(1)}, f32[136,128]{1,0:T(8,128)S(1)}, f32[136,128]{1,0:T(8,128)S(1)}) custom-call(bf16[8,512]{1,0:T(8,128)(2,1)S(1)} %get-tuple-element.20.own0_ref, bf16[8,512]{1,0:T(8,128)(2,1)S(1)} %get-tuple-element.21.own1_ref, bf16[8,512]{1,0:T(8,128)(2,1)S(1)} %collective-permute-done.got0_ref, ...), custom_call_target="tpu_custom_call" | custom-call | tf_op jit(solution)/shard_map/edges/pallas_call | solution.py:422
  11.2 0.0 copy-start.1
  11.2 0.0 copy-start.2
  11.2 0.0 copy-start.3
  11.2 0.0 copy-start.4
  11.2 0.1 collective-permute-start.2
  11.3 1.2 %collective-permute-done.2 = f32[136,128]{1,0:T(8,128)S(1)} collective-permute-done((f32[136,128]{1,0:T(8,128)S(1)}, f32[136,128]{1,0:T(8,128)S(1)}, u32[]{:S(2)}, u32[]{:S(2)}) %collective-permute-start.2) | collective-permute-done | bytes 69664 | tf_op jit(solution)/shard_map/ppermute | solution.py:358
  12.5 0.1 collective-permute-start.3
  12.6 0.1 collective-permute-start.4
  12.7 3.4 %collective-permute-start.5 = (f32[136,128]{1,0:T(8,128)S(1)}, f32[136,128]{1,0:T(8,128)S(1)}, u32[]{:S(2)}, u32[]{:S(2)}) collective-permute-start(f32[136,128]{1,0:T(8,128)S(1)} %add.15), channel_id=1, source_target_pairs={{0,6},{1,7},{2,4},{3,5},{4,2},{5,3},{6,0},{7,1},{8,14},{9,15},{10,... | collective-permute-start | bytes 208904 | tf_op jit(solution)/shard_map/ppermute | solution.py:358
  16.1 0.8 %collective-permute-done.3 = f32[136,128]{1,0:T(8,128)S(1)} collective-permute-done((f32[136,128]{1,0:T(8,128)S(1)}, f32[136,128]{1,0:T(8,128)S(1)}, u32[]{:S(2)}, u32[]{:S(2)}) %collective-permute-start.3) | collective-permute-done | bytes 69664 | tf_op jit(solution)/shard_map/ppermute | solution.py:358
  16.9 0.5 %collective-permute-done.4 = f32[136,128]{1,0:T(8,128)S(1)} collective-permute-done((f32[136,128]{1,0:T(8,128)S(1)}, f32[136,128]{1,0:T(8,128)S(1)}, u32[]{:S(2)}, u32[]{:S(2)}) %collective-permute-start.4) | collective-permute-done | bytes 69664 | tf_op jit(solution)/shard_map/ppermute | solution.py:358
  17.5 2.1 %collective-permute-done.5 = f32[136,128]{1,0:T(8,128)S(1)} collective-permute-done((f32[136,128]{1,0:T(8,128)S(1)}, f32[136,128]{1,0:T(8,128)S(1)}, u32[]{:S(2)}, u32[]{:S(2)}) %collective-permute-start.5) | collective-permute-done | bytes 69664 | tf_op jit(solution)/shard_map/ppermute | solution.py:358
  19.6 2.0 %collective-permute-start.6 = (f32[136,128]{1,0:T(8,128)S(1)}, f32[136,128]{1,0:T(8,128)S(1)}, u32[]{:S(2)}, u32[]{:S(2)}) collective-permute-start(f32[136,128]{1,0:T(8,128)S(1)} %add_add_fusion), channel_id=1, source_target_pairs={{0,8},{1,9},{2,10},{3,11},{4,12},{5,13},{6,14},{7,15},{8,0},{9,1},... | collective-permute-start | bytes 208904 | tf_op jit(solution)/shard_map/ppermute | solution.py:358
  22.2 3.2 %collective-permute-done.6 = f32[136,128]{1,0:T(8,128)S(1)} collective-permute-done((f32[136,128]{1,0:T(8,128)S(1)}, f32[136,128]{1,0:T(8,128)S(1)}, u32[]{:S(2)}, u32[]{:S(2)}) %collective-permute-start.6) | collective-permute-done | bytes 69664 | tf_op jit(solution)/shard_map/ppermute | solution.py:358
  25.4 0.6 %solve.1 = (f32[16,128]{1,0:T(8,128)S(1)}, f32[16,128]{1,0:T(8,128)S(1)}) custom-call(f32[136,128]{1,0:T(8,128)S(1)} %add.19.stats_ref, s32[1]{0:T(128)S(6)} %copy.14.ref_mic_ref), custom_call_target="tpu_custom_call" | custom-call | tf_op jit(solution)/shard_map/solve/pallas_call | solution.py:433
  26.0 0.1 collective-permute-start.7
  26.1 0.0 copy-done
  26.1 0.5 %power.1.mel_ref = f32[72,256]{1,0:T(8,128)S(1)} custom-call(f32[16,128]{1,0:T(8,128)S(1)} %get-tuple-element.29.mine_ref, f32[16,128]{1,0:T(8,128)S(1)} %get-tuple-element.30.last_ref, f32[6,512,128]{2,1,0:T(8,128)S(1)} %get-tuple-element.31.spec_ref, f32[6,64,128]{2,1,0:T(8,128)S(1)} %get-tuple-element.32.edge_spec_ref, f32[3,128,256]{2,1,0:T(8,128)S(1)} %copy-done), custom_call_target="tpu_custom_call" | custom-call | tf_op jit(solution)/shard_map/power/pallas_call | solution.py:444
  26.6 0.7 %collective-permute-done.7.theirs_ref = f32[16,128]{1,0:T(8,128)S(1)} collective-permute-done((f32[16,128]{1,0:T(8,128)S(1)}, f32[16,128]{1,0:T(8,128)S(1)}, u32[]{:S(2)}, u32[]{:S(2)}) %collective-permute-start.7) | collective-permute-done | bytes 8224 | tf_op jit(solution)/shard_map/ppermute | solution.py:358
  27.3 0.0 copy-done.1
  27.3 0.0 copy-done.2
  27.3 0.0 copy-done.3
  27.3 0.0 copy-done.4
  27.3 2.7 %stem.1 = bf16[1,16,256]{2,1,0:T(8,128)(2,1)} custom-call(f32[16,128]{1,0:T(8,128)S(1)} %collective-permute-done.7.theirs_ref, f32[72,256]{1,0:T(8,128)S(1)} %power.1.mel_ref, f32[6,512,128]{2,1,0:T(8,128)S(1)} %get-tuple-element.31.spec_ref, f32[6,64,128]{2,1,0:T(8,128)S(1)} %get-tuple-element.32.edge_spec_ref, s32[1]{0:T(128)S(6)} %copy.13.valid_ref, ...), custom_call_target="tpu_custom_call" | custom-call | tf_op jit(solution)/shard_map/stem/pallas_call | solution.py:452
  (3 shorter events, 0.0 us)
Async XLA Ops:
  1.3 9.4 %collective-permute-start = (bf16[8,512]{1,0:T(8,128)(2,1)S(1)}, bf16[8,512]{1,0:T(8,128)(2,1)S(1)}, u32[]{:S(2)}, u32[]{:S(2)}) collective-permute-start(bf16[8,512]{1,0:T(8,128)(2,1)S(1)} %get-tuple-element.20.own0_ref), channel_id=1, source_target_pairs={{0,1},{2,3},{4,5},{6,7},{8,9},{10,11},{12,13},{14,15},{1,0},{3,2},... | collective-permute-start | bytes 24584 | tf_op jit(solution)/shard_map/ppermute | solution.py:376
  1.8 8.9 %collective-permute-start.1 = (bf16[8,512]{1,0:T(8,128)(2,1)S(1)}, bf16[8,512]{1,0:T(8,128)(2,1)S(1)}, u32[]{:S(2)}, u32[]{:S(2)}) collective-permute-start(bf16[8,512]{1,0:T(8,128)(2,1)S(1)} %get-tuple-element.21.own1_ref), channel_id=1, source_target_pairs={{1,2},{3,4},{5,6},{7,8},{9,10},{11,12},{13,14},{15,0},{2,1},{4,3},... | collective-permute-start | bytes 24584 | tf_op jit(solution)/shard_map/ppermute | solution.py:376
  10.7 15.4 %copy-start = (f32[3,128,256]{2,1,0:T(8,128)S(1)}, f32[3,128,256]{2,1,0:T(8,128)}, u32[]{:S(2)}) copy-start(f32[3,128,256]{2,1,0:T(8,128)} %constant.5.clone.bank_ref) | copy-start | bytes 1179652
  11.2 16.1 %copy-start.1 = (bf16[9,256]{1,0:T(8,128)(2,1)S(1)}, bf16[9,256]{1,0:T(8,128)(2,1)}, u32[]{:S(2)}) copy-start(bf16[9,256]{1,0:T(8,128)(2,1)} %conv1_w_ref.1) | copy-start | bytes 13828
  11.2 16.1 %copy-start.2 = (f32[256]{0:T(256)S(1)}, f32[256]{0:T(256)}, u32[]{:S(2)}) copy-start(f32[256]{0:T(256)} %param.17) | copy-start | bytes 3076
  11.2 16.1 %copy-start.3 = (f32[256]{0:T(256)S(1)}, f32[256]{0:T(256)}, u32[]{:S(2)}) copy-start(f32[256]{0:T(256)} %param.19) | copy-start | bytes 3076
  11.2 16.1 %copy-start.4 = (f32[256]{0:T(256)S(1)}, f32[256]{0:T(256)}, u32[]{:S(2)}) copy-start(f32[256]{0:T(256)} %param.21) | copy-start | bytes 3076
  11.2 1.3 %collective-permute-start.2 = (f32[136,128]{1,0:T(8,128)S(1)}, f32[136,128]{1,0:T(8,128)S(1)}, u32[]{:S(2)}, u32[]{:S(2)}) collective-permute-start(f32[136,128]{1,0:T(8,128)S(1)} %get-tuple-element.28), channel_id=1, source_target_pairs={{0,1},{1,0},{2,3},{3,2},{4,5},{5,4},{6,7},{7,6},{8,9},{9,8},{10,11... | collective-permute-start | bytes 208904 | tf_op jit(solution)/shard_map/ppermute | solution.py:358
  12.5 4.4 %collective-permute-start.3 = (f32[136,128]{1,0:T(8,128)S(1)}, f32[136,128]{1,0:T(8,128)S(1)}, u32[]{:S(2)}, u32[]{:S(2)}) collective-permute-start(f32[136,128]{1,0:T(8,128)S(1)} %add.15), channel_id=1, source_target_pairs={{0,2},{1,3},{2,0},{3,1},{4,6},{5,7},{6,4},{7,5},{8,10},{9,11},{10,... | collective-permute-start | bytes 208904 | tf_op jit(solution)/shard_map/ppermute | solution.py:358
  12.6 4.8 %collective-permute-start.4 = (f32[136,128]{1,0:T(8,128)S(1)}, f32[136,128]{1,0:T(8,128)S(1)}, u32[]{:S(2)}, u32[]{:S(2)}) collective-permute-start(f32[136,128]{1,0:T(8,128)S(1)} %add.15), channel_id=1, source_target_pairs={{0,4},{1,5},{2,6},{3,7},{4,0},{5,1},{6,2},{7,3},{8,12},{9,13},{10,... | collective-permute-start | bytes 208904 | tf_op jit(solution)/shard_map/ppermute | solution.py:358
  12.7 6.8 %collective-permute-start.5 = (f32[136,128]{1,0:T(8,128)S(1)}, f32[136,128]{1,0:T(8,128)S(1)}, u32[]{:S(2)}, u32[]{:S(2)}) collective-permute-start(f32[136,128]{1,0:T(8,128)S(1)} %add.15), channel_id=1, source_target_pairs={{0,6},{1,7},{2,4},{3,5},{4,2},{5,3},{6,0},{7,1},{8,14},{9,15},{10,... | collective-permute-start | bytes 208904 | tf_op jit(solution)/shard_map/ppermute | solution.py:358
  19.6 5.8 %collective-permute-start.6 = (f32[136,128]{1,0:T(8,128)S(1)}, f32[136,128]{1,0:T(8,128)S(1)}, u32[]{:S(2)}, u32[]{:S(2)}) collective-permute-start(f32[136,128]{1,0:T(8,128)S(1)} %add_add_fusion), channel_id=1, source_target_pairs={{0,8},{1,9},{2,10},{3,11},{4,12},{5,13},{6,14},{7,15},{8,0},{9,1},... | collective-permute-start | bytes 208904 | tf_op jit(solution)/shard_map/ppermute | solution.py:358
  26.0 1.2 %collective-permute-start.7 = (f32[16,128]{1,0:T(8,128)S(1)}, f32[16,128]{1,0:T(8,128)S(1)}, u32[]{:S(2)}, u32[]{:S(2)}) collective-permute-start(f32[16,128]{1,0:T(8,128)S(1)} %get-tuple-element.29.mine_ref), channel_id=1, source_target_pairs={{0,1},{1,0},{2,3},{3,2},{4,5},{5,4},{6,7},{7,6},{8,9},{9,8},{10,11... | collective-permute-start | bytes 24584 | tf_op jit(solution)/shard_map/ppermute | solution.py:358

commit v6 on v5

--- a/solution.py
+++ b/solution.py
@@ -370,10 +370,17 @@
     return block
 
 
-def paired(block, axis, first):
-    size = lax.axis_size(axis)
-    lower = range(first, size, 2)
-    return lax.ppermute(block, axis, [(i, (i + 1) % size) for i in lower] + [((i + 1) % size, i) for i in lower])
+def paired(block, first):
+    size, meets = lax.axis_size("tm"), lax.axis_size("meet")
+    pairs = []
+    for meet in range(meets):
+        at = meet * size
+        pairs += [(at + i, at + i + 1) for i in range(first, size - 1, 2)]
+        if first and meets % 2:
+            pairs.append((at, at + size - 1))
+        elif first and meet % 2 == 0:
+            pairs += [(at + end, at + size + end) for end in (0, size - 1)]
+    return lax.ppermute(block, ("meet", "tm"), pairs + [(j, i) for i, j in pairs])
 
 
 def per_device(waveform, masks, valid, ref_mic, conv1_w, conv1_b, conv2_w, conv2_b, proj_w, proj_b):
@@ -397,8 +404,8 @@
         compiler_params=params,
         name="rims",
     )(in_hbm(waveform), in_hbm(masks), in_hbm(table))
-    got_across = paired(across, "tm", 1)
-    got_beside = paired(beside, "tm", 0)
+    got_across = paired(across, 1)
+    got_beside = paired(beside, 0)
     stat_block = jax.ShapeDtypeStruct((STATS + MICS, LANES), jnp.float32)
     spec, kept, edge_weight, conv2_w, proj_w = pl.pallas_call(
         functools.partial(stats_kernel, frames),

time: 30.1 us -> 28.4 us (0.944)
  starting transfers between devices: 11.9 us -> 9.57 us
  waiting for transfers between devices: 8.55 us -> 9.11 us
    ppermute x2, starting transfers between devices: 6.18 us -> 3.08 us  [paired(): lax.ppermute(block, ('meet', 'tm'), pairs + [(j, i) for i, j in pairs])]
    ppermute x6, starting transfers between devices: 5.69 us -> 6.49 us  [flipped(): return lax.ppermute(block, axis, [(i, i ^ step) for i in range(size)])]
    ppermute x6, waiting for transfers between devices: 8.54 us -> 9.11 us  [flipped(): return lax.ppermute(block, axis, [(i, i ^ step) for i in range(size)])]
  transfers between devices with their start and end apart: 8 -> 8, of which waited for: 6 -> 6; matrix products, arithmetic and copies ran while one was open for 0% -> 0% of each run, Pallas kernels for 10% -> 11%
where the time goes in v6:
time: 28.4 us; the launch traced here: 28.2 us
  starting transfers between devices  9.57 us (34%)
  waiting for transfers between devices  9.11 us (32%)
  Pallas kernels  8.05 us (28%)
  between operations  1.41 us (5%)
    ppermute x6, waiting for transfers between devices, flipped(): return lax.ppermute(block, axis, [(i, i ^ step) for i in range(size)])  9.11 us
    ppermute x6, starting transfers between devices, flipped(): return lax.ppermute(block, axis, [(i, i ^ step) for i in range(size)])  6.49 us
    ppermute x2, starting transfers between devices, paired(): lax.ppermute(block, ('meet', 'tm'), pairs + [(j, i) for i, j in pairs])  3.08 us
    pallas_call x1, Pallas kernels, per_device(): pl.pallas_call(functools.partial(stem_kernel, frames), out_shape=jax.Shap...  2.7 us
    pallas_call x1, Pallas kernels, per_device(): pl.pallas_call(functools.partial(stats_kernel, frames), out_shape=(jax.Sh...  2.59 us
    pallas_call x1, Pallas kernels, per_device(): pl.pallas_call(rims_kernel, out_shape=(rim, rim) + tuple((jax.ShapeDtypeS...  1.27 us
    pallas_call x1, Pallas kernels, per_device(): pl.pallas_call(solve_kernel, out_shape=(beam, beam), in_specs=[vmem, smem...  0.59 us
  transfers between devices with their start and end apart: 8, of which 6 were waited for; matrix products, arithmetic and copies ran while one was open for 0% of the time, Pallas kernels for 11%

profile of v6, /device:TPU:0, one launch (start us, length us, event | category | flops | bytes accessed | tf_op | source)
XLA Modules:
  0.0 28.2 jit_solution(8296489398081471255)
XLA Ops:
  0.0 1.3 %rims.1 = (bf16[8,512]{1,0:T(8,128)(2,1)S(1)}, bf16[8,512]{1,0:T(8,128)(2,1)S(1)}, bf16[8,10240]{1,0:T(8,128)(2,1)S(1)}, s32[2,64,257]{2,1,0:T(8,128)S(1)}, bf16[512,768]{1,0:T(8,128)(2,1)S(1)}) custom-call(bf16[8,10240]{1,0:T(8,128)(2,1)} %wave_hbm.1, s32[2,64,257]{2,1,0:T(8,128)} %masks_hbm.1, bf16[512,768]{1,0:T(8,128)(2,1)} %constant.8.table_hbm), custom_call_target="tpu_custom_call" | custom-call | tf_op jit(solution)/shard_map/rims/pallas_call | solution.py:398
  1.3 0.5 %collective-permute-start = (bf16[8,512]{1,0:T(8,128)(2,1)S(1)}, bf16[8,512]{1,0:T(8,128)(2,1)S(1)}, u32[]{:S(2)}, u32[]{:S(2)}) collective-permute-start(bf16[8,512]{1,0:T(8,128)(2,1)S(1)} %get-tuple-element.20.own0_ref), channel_id=1, source_target_pairs={{0,1},{2,3},{4,5},{6,7},{8,9},{10,11},{12,13},{14,15},{16,17},{18,... | collective-permute-start | bytes 24584 | tf_op jit(solution)/shard_map/ppermute | solution.py:383
  1.8 2.6 %collective-permute-start.1 = (bf16[8,512]{1,0:T(8,128)(2,1)S(1)}, bf16[8,512]{1,0:T(8,128)(2,1)S(1)}, u32[]{:S(2)}, u32[]{:S(2)}) collective-permute-start(bf16[8,512]{1,0:T(8,128)(2,1)S(1)} %get-tuple-element.21.own1_ref), channel_id=1, source_target_pairs={{1,2},{3,4},{5,6},{7,8},{9,10},{11,12},{13,14},{0,16},{15,31},{17,... | collective-permute-start | bytes 24584 | tf_op jit(solution)/shard_map/ppermute | solution.py:383
  5.0 2.6 %stats.1 = (f32[6,512,128]{2,1,0:T(8,128)S(1)}, f32[3,128,128]{2,1,0:T(8,128)S(1)}, f32[3,2,8,128]{3,2,1,0:T(8,128)S(1)}, bf16[2304,256]{1,0:T(8,128)(2,1)S(1)}, bf16[4864,256]{1,0:T(8,128)(2,1)S(1)}) custom-call(bf16[8,10240]{1,0:T(8,128)(2,1)S(1)} %get-tuple-element.23.wave_ref, s32[2,64,257]{2,1,0:T(8,128)S(1)} %get-tuple-element.24.masks_ref, ...), custom_call_target="tpu_custom_call" | custom-call | tf_op jit(solution)/shard_map/stats/pallas_call | solution.py:410
  7.6 0.0 copy-start
  7.6 0.0 collective-permute-done.got0_ref
  7.6 0.0 collective-permute-done.1.got1_ref
  7.7 0.4 %edges.1 = (f32[6,64,128]{2,1,0:T(8,128)S(1)}, f32[136,128]{1,0:T(8,128)S(1)}, f32[136,128]{1,0:T(8,128)S(1)}) custom-call(bf16[8,512]{1,0:T(8,128)(2,1)S(1)} %get-tuple-element.20.own0_ref, bf16[8,512]{1,0:T(8,128)(2,1)S(1)} %get-tuple-element.21.own1_ref, bf16[8,512]{1,0:T(8,128)(2,1)S(1)} %collective-permute-done.got0_ref, ...), custom_call_target="tpu_custom_call" | custom-call | tf_op jit(solution)/shard_map/edges/pallas_call | solution.py:429
  8.1 0.0 copy-start.1
  8.1 0.0 copy-start.2
  8.1 0.0 copy-start.3
  8.1 0.0 copy-start.4
  8.1 0.2 collective-permute-start.2
  8.3 1.1 %collective-permute-done.2 = f32[136,128]{1,0:T(8,128)S(1)} collective-permute-done((f32[136,128]{1,0:T(8,128)S(1)}, f32[136,128]{1,0:T(8,128)S(1)}, u32[]{:S(2)}, u32[]{:S(2)}) %collective-permute-start.2) | collective-permute-done | bytes 69664 | tf_op jit(solution)/shard_map/ppermute | solution.py:358
  9.4 1.4 %collective-permute-start.3 = (f32[136,128]{1,0:T(8,128)S(1)}, f32[136,128]{1,0:T(8,128)S(1)}, u32[]{:S(2)}, u32[]{:S(2)}) collective-permute-start(f32[136,128]{1,0:T(8,128)S(1)} %add.15), channel_id=1, source_target_pairs={{0,2},{1,3},{2,0},{3,1},{4,6},{5,7},{6,4},{7,5},{8,10},{9,11},{10,... | collective-permute-start | bytes 208904 | tf_op jit(solution)/shard_map/ppermute | solution.py:358
  10.8 1.6 %collective-permute-start.4 = (f32[136,128]{1,0:T(8,128)S(1)}, f32[136,128]{1,0:T(8,128)S(1)}, u32[]{:S(2)}, u32[]{:S(2)}) collective-permute-start(f32[136,128]{1,0:T(8,128)S(1)} %add.15), channel_id=1, source_target_pairs={{0,4},{1,5},{2,6},{3,7},{4,0},{5,1},{6,2},{7,3},{8,12},{9,13},{10,... | collective-permute-start | bytes 208904 | tf_op jit(solution)/shard_map/ppermute | solution.py:358
  12.4 0.6 %collective-permute-start.5 = (f32[136,128]{1,0:T(8,128)S(1)}, f32[136,128]{1,0:T(8,128)S(1)}, u32[]{:S(2)}, u32[]{:S(2)}) collective-permute-start(f32[136,128]{1,0:T(8,128)S(1)} %add.15), channel_id=1, source_target_pairs={{0,6},{1,7},{2,4},{3,5},{4,2},{5,3},{6,0},{7,1},{8,14},{9,15},{10,... | collective-permute-start | bytes 208904 | tf_op jit(solution)/shard_map/ppermute | solution.py:358
  13.0 0.8 %collective-permute-done.3 = f32[136,128]{1,0:T(8,128)S(1)} collective-permute-done((f32[136,128]{1,0:T(8,128)S(1)}, f32[136,128]{1,0:T(8,128)S(1)}, u32[]{:S(2)}, u32[]{:S(2)}) %collective-permute-start.3) | collective-permute-done | bytes 69664 | tf_op jit(solution)/shard_map/ppermute | solution.py:358
  13.8 1.7 %collective-permute-done.4 = f32[136,128]{1,0:T(8,128)S(1)} collective-permute-done((f32[136,128]{1,0:T(8,128)S(1)}, f32[136,128]{1,0:T(8,128)S(1)}, u32[]{:S(2)}, u32[]{:S(2)}) %collective-permute-start.4) | collective-permute-done | bytes 69664 | tf_op jit(solution)/shard_map/ppermute | solution.py:358
  15.5 2.1 %collective-permute-done.5 = f32[136,128]{1,0:T(8,128)S(1)} collective-permute-done((f32[136,128]{1,0:T(8,128)S(1)}, f32[136,128]{1,0:T(8,128)S(1)}, u32[]{:S(2)}, u32[]{:S(2)}) %collective-permute-start.5) | collective-permute-done | bytes 69664 | tf_op jit(solution)/shard_map/ppermute | solution.py:358
  17.6 2.7 %collective-permute-start.6 = (f32[136,128]{1,0:T(8,128)S(1)}, f32[136,128]{1,0:T(8,128)S(1)}, u32[]{:S(2)}, u32[]{:S(2)}) collective-permute-start(f32[136,128]{1,0:T(8,128)S(1)} %add_add_fusion), channel_id=1, source_target_pairs={{0,8},{1,9},{2,10},{3,11},{4,12},{5,13},{6,14},{7,15},{8,0},{9,1},... | collective-permute-start | bytes 208904 | tf_op jit(solution)/shard_map/ppermute | solution.py:358
  20.9 2.7 %collective-permute-done.6 = f32[136,128]{1,0:T(8,128)S(1)} collective-permute-done((f32[136,128]{1,0:T(8,128)S(1)}, f32[136,128]{1,0:T(8,128)S(1)}, u32[]{:S(2)}, u32[]{:S(2)}) %collective-permute-start.6) | collective-permute-done | bytes 69664 | tf_op jit(solution)/shard_map/ppermute | solution.py:358
  23.7 0.6 %solve.1 = (f32[16,128]{1,0:T(8,128)S(1)}, f32[16,128]{1,0:T(8,128)S(1)}) custom-call(f32[136,128]{1,0:T(8,128)S(1)} %add.19.stats_ref, s32[1]{0:T(128)S(6)} %copy.14.ref_mic_ref), custom_call_target="tpu_custom_call" | custom-call | tf_op jit(solution)/shard_map/solve/pallas_call | solution.py:440
  24.3 0.1 collective-permute-start.7
  24.3 0.0 copy-done
  24.4 0.5 %power.1.mel_ref = f32[72,256]{1,0:T(8,128)S(1)} custom-call(f32[16,128]{1,0:T(8,128)S(1)} %get-tuple-element.29.mine_ref, f32[16,128]{1,0:T(8,128)S(1)} %get-tuple-element.30.last_ref, f32[6,512,128]{2,1,0:T(8,128)S(1)} %get-tuple-element.31.spec_ref, f32[6,64,128]{2,1,0:T(8,128)S(1)} %get-tuple-element.32.edge_spec_ref, f32[3,128,256]{2,1,0:T(8,128)S(1)} %copy-done), custom_call_target="tpu_custom_call" | custom-call | tf_op jit(solution)/shard_map/power/pallas_call | solution.py:451
  24.8 0.7 %collective-permute-done.7.theirs_ref = f32[16,128]{1,0:T(8,128)S(1)} collective-permute-done((f32[16,128]{1,0:T(8,128)S(1)}, f32[16,128]{1,0:T(8,128)S(1)}, u32[]{:S(2)}, u32[]{:S(2)}) %collective-permute-start.7) | collective-permute-done | bytes 8224 | tf_op jit(solution)/shard_map/ppermute | solution.py:358
  25.5 0.0 copy-done.1
  25.5 0.0 copy-done.2
  25.5 0.0 copy-done.3
  25.5 0.0 copy-done.4
  25.5 2.7 %stem.1 = bf16[1,16,256]{2,1,0:T(8,128)(2,1)} custom-call(f32[16,128]{1,0:T(8,128)S(1)} %collective-permute-done.7.theirs_ref, f32[72,256]{1,0:T(8,128)S(1)} %power.1.mel_ref, f32[6,512,128]{2,1,0:T(8,128)S(1)} %get-tuple-element.31.spec_ref, f32[6,64,128]{2,1,0:T(8,128)S(1)} %get-tuple-element.32.edge_spec_ref, s32[1]{0:T(128)S(6)} %copy.13.valid_ref, ...), custom_call_target="tpu_custom_call" | custom-call | tf_op jit(solution)/shard_map/stem/pallas_call | solution.py:459
  (3 shorter events, 0.0 us)
Async XLA Ops:
  1.3 6.4 %collective-permute-start = (bf16[8,512]{1,0:T(8,128)(2,1)S(1)}, bf16[8,512]{1,0:T(8,128)(2,1)S(1)}, u32[]{:S(2)}, u32[]{:S(2)}) collective-permute-start(bf16[8,512]{1,0:T(8,128)(2,1)S(1)} %get-tuple-element.20.own0_ref), channel_id=1, source_target_pairs={{0,1},{2,3},{4,5},{6,7},{8,9},{10,11},{12,13},{14,15},{16,17},{18,... | collective-permute-start | bytes 24584 | tf_op jit(solution)/shard_map/ppermute | solution.py:383
  1.8 5.8 %collective-permute-start.1 = (bf16[8,512]{1,0:T(8,128)(2,1)S(1)}, bf16[8,512]{1,0:T(8,128)(2,1)S(1)}, u32[]{:S(2)}, u32[]{:S(2)}) collective-permute-start(bf16[8,512]{1,0:T(8,128)(2,1)S(1)} %get-tuple-element.21.own1_ref), channel_id=1, source_target_pairs={{1,2},{3,4},{5,6},{7,8},{9,10},{11,12},{13,14},{0,16},{15,31},{17,... | collective-permute-start | bytes 24584 | tf_op jit(solution)/shard_map/ppermute | solution.py:383
  7.6 16.7 %copy-start = (f32[3,128,256]{2,1,0:T(8,128)S(1)}, f32[3,128,256]{2,1,0:T(8,128)}, u32[]{:S(2)}) copy-start(f32[3,128,256]{2,1,0:T(8,128)} %constant.5.clone.bank_ref) | copy-start | bytes 1179652
  8.1 17.4 %copy-start.1 = (bf16[9,256]{1,0:T(8,128)(2,1)S(1)}, bf16[9,256]{1,0:T(8,128)(2,1)}, u32[]{:S(2)}) copy-start(bf16[9,256]{1,0:T(8,128)(2,1)} %conv1_w_ref.1) | copy-start | bytes 13828
  8.1 17.4 %copy-start.2 = (f32[256]{0:T(256)S(1)}, f32[256]{0:T(256)}, u32[]{:S(2)}) copy-start(f32[256]{0:T(256)} %param.17) | copy-start | bytes 3076
  8.1 17.4 %copy-start.3 = (f32[256]{0:T(256)S(1)}, f32[256]{0:T(256)}, u32[]{:S(2)}) copy-start(f32[256]{0:T(256)} %param.19) | copy-start | bytes 3076
  8.1 17.4 %copy-start.4 = (f32[256]{0:T(256)S(1)}, f32[256]{0:T(256)}, u32[]{:S(2)}) copy-start(f32[256]{0:T(256)} %param.21) | copy-start | bytes 3076
  8.1 1.3 %collective-permute-start.2 = (f32[136,128]{1,0:T(8,128)S(1)}, f32[136,128]{1,0:T(8,128)S(1)}, u32[]{:S(2)}, u32[]{:S(2)}) collective-permute-start(f32[136,128]{1,0:T(8,128)S(1)} %get-tuple-element.28), channel_id=1, source_target_pairs={{0,1},{1,0},{2,3},{3,2},{4,5},{5,4},{6,7},{7,6},{8,9},{9,8},{10,11... | collective-permute-start | bytes 208904 | tf_op jit(solution)/shard_map/ppermute | solution.py:358
  9.4 4.4 %collective-permute-start.3 = (f32[136,128]{1,0:T(8,128)S(1)}, f32[136,128]{1,0:T(8,128)S(1)}, u32[]{:S(2)}, u32[]{:S(2)}) collective-permute-start(f32[136,128]{1,0:T(8,128)S(1)} %add.15), channel_id=1, source_target_pairs={{0,2},{1,3},{2,0},{3,1},{4,6},{5,7},{6,4},{7,5},{8,10},{9,11},{10,... | collective-permute-start | bytes 208904 | tf_op jit(solution)/shard_map/ppermute | solution.py:358
  10.8 4.7 %collective-permute-start.4 = (f32[136,128]{1,0:T(8,128)S(1)}, f32[136,128]{1,0:T(8,128)S(1)}, u32[]{:S(2)}, u32[]{:S(2)}) collective-permute-start(f32[136,128]{1,0:T(8,128)S(1)} %add.15), channel_id=1, source_target_pairs={{0,4},{1,5},{2,6},{3,7},{4,0},{5,1},{6,2},{7,3},{8,12},{9,13},{10,... | collective-permute-start | bytes 208904 | tf_op jit(solution)/shard_map/ppermute | solution.py:358
  12.4 5.2 %collective-permute-start.5 = (f32[136,128]{1,0:T(8,128)S(1)}, f32[136,128]{1,0:T(8,128)S(1)}, u32[]{:S(2)}, u32[]{:S(2)}) collective-permute-start(f32[136,128]{1,0:T(8,128)S(1)} %add.15), channel_id=1, source_target_pairs={{0,6},{1,7},{2,4},{3,5},{4,2},{5,3},{6,0},{7,1},{8,14},{9,15},{10,... | collective-permute-start | bytes 208904 | tf_op jit(solution)/shard_map/ppermute | solution.py:358
  17.6 6.0 %collective-permute-start.6 = (f32[136,128]{1,0:T(8,128)S(1)}, f32[136,128]{1,0:T(8,128)S(1)}, u32[]{:S(2)}, u32[]{:S(2)}) collective-permute-start(f32[136,128]{1,0:T(8,128)S(1)} %add_add_fusion), channel_id=1, source_target_pairs={{0,8},{1,9},{2,10},{3,11},{4,12},{5,13},{6,14},{7,15},{8,0},{9,1},... | collective-permute-start | bytes 208904 | tf_op jit(solution)/shard_map/ppermute | solution.py:358
  24.3 1.2 %collective-permute-start.7 = (f32[16,128]{1,0:T(8,128)S(1)}, f32[16,128]{1,0:T(8,128)S(1)}, u32[]{:S(2)}, u32[]{:S(2)}) collective-permute-start(f32[16,128]{1,0:T(8,128)S(1)} %get-tuple-element.29.mine_ref), channel_id=1, source_target_pairs={{0,1},{1,0},{2,3},{3,2},{4,5},{5,4},{6,7},{7,6},{8,9},{9,8},{10,11... | collective-permute-start | bytes 24584 | tf_op jit(solution)/shard_map/ppermute | solution.py:358

commit v7 on v6

--- a/solution.py
+++ b/solution.py
@@ -100,7 +100,7 @@
     return copies
 
 
-def rims_kernel(wave_hbm, masks_hbm, table_hbm, beside_ref, across_ref, wave_ref, masks_ref, table_ref, sem):
+def rims_kernel(frames, wave_hbm, masks_hbm, table_hbm, beside_ref, across_ref, framed_ref, masks_ref, table_ref, wave_ref, sem):
     copies = started(((wave_hbm, wave_ref), (table_hbm, table_ref), (masks_hbm, masks_ref)), sem)
     even = lax.axis_index("tm") % 2 == 0
     copies[0].wait()
@@ -108,23 +108,48 @@
     tail = wave_ref[:, wave_ref.shape[1] - LEAD :].astype(jnp.float32)
     beside_ref[...] = jnp.where(even, tail, head).astype(beside_ref.dtype)
     across_ref[...] = jnp.where(even, head, tail).astype(across_ref.dtype)
-    copies[1].wait()
-    copies[2].wait()
-
-
-def stats_kernel(frames, wave_ref, masks_ref, table_ref, conv2_w_hbm, proj_w_hbm, valid_ref, spec_ref, kept_ref, edge_weight_ref, conv2_w_ref, proj_w_ref, framed_ref, weight_ref, sem):
-    copies = started(((conv2_w_hbm, conv2_w_ref), (proj_w_hbm, proj_w_ref)), sem)
-    position = lax.axis_index("tm")
     wave = wave_ref[...].astype(jnp.float32)
     width = wave.shape[1]
     rolled = {}
-    for frame in range(frames - HALO):
+
+    def frame_of(frame):
+        if frame >= frames - HALO:
+            return jnp.zeros((MICS, NFFT), jnp.float32)
         base, shift = frame * HOP // LANES * LANES, frame * HOP % LANES
         if shift not in rolled:
             rolled[shift] = wave if shift == 0 else pltpu.roll(wave, width - shift, 1)
-        framed_ref[MICS * frame : MICS * (frame + 1), :] = rolled[shift][:, base : base + NFFT]
-    framed_ref[MICS * (frames - HALO) :, :] = jnp.zeros((MICS * HALO, NFFT), jnp.float32)
-    spec = jnp.dot(framed_ref[...].astype(jnp.bfloat16), table_ref[...], preferred_element_type=jnp.float32)
+        return rolled[shift][:, base : base + NFFT]
+
+    for frame in range(0, frames, 2):
+        pair = jnp.concatenate([frame_of(frame), frame_of(frame + 1)], axis=0)
+        framed_ref[MICS * frame : MICS * (frame + 2), :] = pair.astype(framed_ref.dtype)
+    copies[1].wait()
+    copies[2].wait()
+
+
+def last_bin_sums(frames, spec_ref, weight_ref):
+    x_re = x_im = jnp.zeros((MICS, LANES), jnp.float32)
+    for frame in range(frames):
+        rows = slice(MICS * frame, MICS * (frame + 1))
+        part_re, part_im = spec_ref[TILES - 1, rows, :], spec_ref[2 * TILES - 1, rows, :]
+        x_re = x_re + (pltpu.roll(part_re, frame, 1) if frame else part_re)
+        x_im = x_im + (pltpu.roll(part_im, frame, 1) if frame else part_im)
+    frame = lax.broadcasted_iota(jnp.int32, (frames, LANES), 0)
+    lane = lax.broadcasted_iota(jnp.int32, (frames, LANES), 1)
+    sums = []
+    for k in range(2):
+        weight = weight_ref[TILES - 1, k][:, :1]
+        weight = jnp.sum(jnp.where(frame == lane, weight, 0.0), axis=0, keepdims=True)
+        for pair in cyclic_pairs(x_re, x_im):
+            total = jnp.sum(pair * weight, axis=1, keepdims=True)
+            sums.append(jnp.where(lane[:MICS] == 0, total, 0.0))
+    return kept_sums(sums)
+
+
+def stats_kernel(frames, framed_ref, masks_ref, table_ref, conv2_w_hbm, proj_w_hbm, valid_ref, spec_ref, kept_ref, edge_weight_ref, conv2_w_ref, proj_w_ref, weight_ref, sem):
+    copies = started(((conv2_w_hbm, conv2_w_ref), (proj_w_hbm, proj_w_ref)), sem)
+    position = lax.axis_index("tm")
+    spec = jnp.dot(framed_ref[...], table_ref[...], preferred_element_type=jnp.float32)
     for tile in range(2 * TILES):
         spec_ref[tile] = spec[:, tile * LANES : (tile + 1) * LANES]
 
@@ -138,7 +163,7 @@
             weight_ref[tile, k, :, :kept_lanes] = weight[:, tile * LANES : tile * LANES + kept_lanes]
     edge_weight_ref[...] = weight_ref[:, :, frames - MICS :, :]
 
-    for slot, tile in enumerate(slot_tiles(position)):
+    for slot, tile in enumerate(slot_tiles(position)[:2]):
 
         def add_frames(group, sums):
             first = pl.multiple_of(group * MICS, MICS)
@@ -152,6 +177,7 @@
 
         zero = jnp.zeros((MICS, LANES), jnp.float32)
         kept_ref[slot] = kept_sums(lax.fori_loop(0, frames // MICS, add_frames, (zero,) * 18))
+    kept_ref[2] = last_bin_sums(frames, spec_ref, weight_ref)
     for copy in copies:
         copy.wait()
 
@@ -395,12 +421,13 @@
     rim = jax.ShapeDtypeStruct((MICS, LEAD), waveform.dtype)
     table = dft_table()
     conv2_w = conv2_w.reshape(-1, channels)
-    beside, across, waves, levels, table = pl.pallas_call(
-        rims_kernel,
-        out_shape=(rim, rim) + tuple(jax.ShapeDtypeStruct(x.shape, x.dtype) for x in (waveform, masks, table)),
+    beside, across, framed, levels, table = pl.pallas_call(
+        functools.partial(rims_kernel, frames),
+        out_shape=(rim, rim, jax.ShapeDtypeStruct((frames * MICS, NFFT), waveform.dtype))
+        + tuple(jax.ShapeDtypeStruct(x.shape, x.dtype) for x in (masks, table)),
         in_specs=[hbm] * 3,
         out_specs=(vmem,) * 5,
-        scratch_shapes=[pltpu.SemaphoreType.DMA((3,))],
+        scratch_shapes=[pltpu.VMEM(waveform.shape, waveform.dtype), pltpu.SemaphoreType.DMA((3,))],
         compiler_params=params,
         name="rims",
     )(in_hbm(waveform), in_hbm(masks), in_hbm(table))
@@ -419,13 +446,12 @@
         in_specs=[vmem] * 3 + [hbm] * 2 + [smem],
         out_specs=(vmem,) * 5,
         scratch_shapes=[
-            pltpu.VMEM((frames * MICS, NFFT), jnp.float32),
             pltpu.VMEM((TILES, 2, frames, LANES), jnp.float32),
             pltpu.SemaphoreType.DMA((2,)),
         ],
         compiler_params=params,
         name="stats",
-    )(waves, levels, table, in_hbm(conv2_w), in_hbm(proj_w), valid)
+    )(framed, levels, table, in_hbm(conv2_w), in_hbm(proj_w), valid)
     edge_spec, mine, theirs = pl.pallas_call(
         functools.partial(edges_kernel, lax.axis_size("tm")),
         out_shape=(jax.ShapeDtypeStruct((2 * TILES, MICS * MICS, LANES), jnp.float32), stat_block, stat_block),

time: 28.4 us -> 28.3 us (level)
  no operation moved by 1% of the time
where the time goes in v7:
time: 28.3 us; the launch traced here: 28.2 us
  starting transfers between devices  9.58 us (34%)
  waiting for transfers between devices  9.12 us (32%)
  Pallas kernels  8.01 us (28%)
  between operations  1.41 us (5%)
    ppermute x6, waiting for transfers between devices, flipped(): return lax.ppermute(block, axis, [(i, i ^ step) for i in range(size)])  9.11 us
    ppermute x6, starting transfers between devices, flipped(): return lax.ppermute(block, axis, [(i, i ^ step) for i in range(size)])  6.49 us
    ppermute x2, starting transfers between devices, paired(): lax.ppermute(block, ('meet', 'tm'), pairs + [(j, i) for i, j in pairs])  3.08 us
    pallas_call x1, Pallas kernels, per_device(): pl.pallas_call(functools.partial(stem_kernel, frames), out_shape=jax.Shap...  2.69 us
    pallas_call x1, Pallas kernels, per_device(): pl.pallas_call(functools.partial(stats_kernel, frames), out_shape=(jax.Sh...  2.56 us
    pallas_call x1, Pallas kernels, per_device(): pl.pallas_call(functools.partial(rims_kernel, frames), out_shape=(rim, ri...  1.27 us
    pallas_call x1, Pallas kernels, per_device(): pl.pallas_call(solve_kernel, out_shape=(beam, beam), in_specs=[vmem, smem...  0.59 us
  transfers between devices with their start and end apart: 8, of which 6 were waited for; matrix products, arithmetic and copies ran while one was open for 0% of the time, Pallas kernels for 11%

profile of v7, /device:TPU:0, one launch (start us, length us, event | category | flops | bytes accessed | tf_op | source)
XLA Modules:
  0.0 28.2 jit_solution(8869207721921561393)
XLA Ops:
  0.0 1.3 %rims.1 = (bf16[8,512]{1,0:T(8,128)(2,1)S(1)}, bf16[8,512]{1,0:T(8,128)(2,1)S(1)}, bf16[512,512]{1,0:T(8,128)(2,1)S(1)}, s32[2,64,257]{2,1,0:T(8,128)S(1)}, bf16[512,768]{1,0:T(8,128)(2,1)S(1)}) custom-call(bf16[8,10240]{1,0:T(8,128)(2,1)} %wave_hbm.1, s32[2,64,257]{2,1,0:T(8,128)} %masks_hbm.1, bf16[512,768]{1,0:T(8,128)(2,1)} %constant.8.table_hbm), custom_call_target="tpu_custom_call" | custom-call | tf_op jit(solution)/shard_map/rims/pallas_call | solution.py:424
  1.3 0.5 %collective-permute-start = (bf16[8,512]{1,0:T(8,128)(2,1)S(1)}, bf16[8,512]{1,0:T(8,128)(2,1)S(1)}, u32[]{:S(2)}, u32[]{:S(2)}) collective-permute-start(bf16[8,512]{1,0:T(8,128)(2,1)S(1)} %get-tuple-element.20.own0_ref), channel_id=1, source_target_pairs={{0,1},{2,3},{4,5},{6,7},{8,9},{10,11},{12,13},{14,15},{16,17},{18,... | collective-permute-start | bytes 24584 | tf_op jit(solution)/shard_map/ppermute | solution.py:409
  1.8 2.6 %collective-permute-start.1 = (bf16[8,512]{1,0:T(8,128)(2,1)S(1)}, bf16[8,512]{1,0:T(8,128)(2,1)S(1)}, u32[]{:S(2)}, u32[]{:S(2)}) collective-permute-start(bf16[8,512]{1,0:T(8,128)(2,1)S(1)} %get-tuple-element.21.own1_ref), channel_id=1, source_target_pairs={{1,2},{3,4},{5,6},{7,8},{9,10},{11,12},{13,14},{0,16},{15,31},{17,... | collective-permute-start | bytes 24584 | tf_op jit(solution)/shard_map/ppermute | solution.py:409
  5.0 2.6 %stats.1 = (f32[6,512,128]{2,1,0:T(8,128)S(1)}, f32[3,128,128]{2,1,0:T(8,128)S(1)}, f32[3,2,8,128]{3,2,1,0:T(8,128)S(1)}, bf16[2304,256]{1,0:T(8,128)(2,1)S(1)}, bf16[4864,256]{1,0:T(8,128)(2,1)S(1)}) custom-call(bf16[512,512]{1,0:T(8,128)(2,1)S(1)} %get-tuple-element.23.framed_ref, s32[2,64,257]{2,1,0:T(8,128)S(1)} %get-tuple-element.24.masks_ref, ...), custom_call_target="tpu_custom_call" | custom-call | tf_op jit(solution)/shard_map/stats/pallas_call | solution.py:437
  7.6 0.0 copy-start
  7.6 0.0 collective-permute-done.got0_ref
  7.6 0.0 collective-permute-done.1.got1_ref
  7.6 0.4 %edges.1 = (f32[6,64,128]{2,1,0:T(8,128)S(1)}, f32[136,128]{1,0:T(8,128)S(1)}, f32[136,128]{1,0:T(8,128)S(1)}) custom-call(bf16[8,512]{1,0:T(8,128)(2,1)S(1)} %get-tuple-element.20.own0_ref, bf16[8,512]{1,0:T(8,128)(2,1)S(1)} %get-tuple-element.21.own1_ref, bf16[8,512]{1,0:T(8,128)(2,1)S(1)} %collective-permute-done.got0_ref, ...), custom_call_target="tpu_custom_call" | custom-call | tf_op jit(solution)/shard_map/edges/pallas_call | solution.py:455
  8.1 0.0 copy-start.1
  8.1 0.0 copy-start.2
  8.1 0.0 copy-start.3
  8.1 0.0 copy-start.4
  8.1 0.2 collective-permute-start.2
  8.3 1.1 %collective-permute-done.2 = f32[136,128]{1,0:T(8,128)S(1)} collective-permute-done((f32[136,128]{1,0:T(8,128)S(1)}, f32[136,128]{1,0:T(8,128)S(1)}, u32[]{:S(2)}, u32[]{:S(2)}) %collective-permute-start.2) | collective-permute-done | bytes 69664 | tf_op jit(solution)/shard_map/ppermute | solution.py:384
  9.4 1.4 %collective-permute-start.3 = (f32[136,128]{1,0:T(8,128)S(1)}, f32[136,128]{1,0:T(8,128)S(1)}, u32[]{:S(2)}, u32[]{:S(2)}) collective-permute-start(f32[136,128]{1,0:T(8,128)S(1)} %add.15), channel_id=1, source_target_pairs={{0,2},{1,3},{2,0},{3,1},{4,6},{5,7},{6,4},{7,5},{8,10},{9,11},{10,... | collective-permute-start | bytes 208904 | tf_op jit(solution)/shard_map/ppermute | solution.py:384
  10.8 1.6 %collective-permute-start.4 = (f32[136,128]{1,0:T(8,128)S(1)}, f32[136,128]{1,0:T(8,128)S(1)}, u32[]{:S(2)}, u32[]{:S(2)}) collective-permute-start(f32[136,128]{1,0:T(8,128)S(1)} %add.15), channel_id=1, source_target_pairs={{0,4},{1,5},{2,6},{3,7},{4,0},{5,1},{6,2},{7,3},{8,12},{9,13},{10,... | collective-permute-start | bytes 208904 | tf_op jit(solution)/shard_map/ppermute | solution.py:384
  12.4 0.6 %collective-permute-start.5 = (f32[136,128]{1,0:T(8,128)S(1)}, f32[136,128]{1,0:T(8,128)S(1)}, u32[]{:S(2)}, u32[]{:S(2)}) collective-permute-start(f32[136,128]{1,0:T(8,128)S(1)} %add.15), channel_id=1, source_target_pairs={{0,6},{1,7},{2,4},{3,5},{4,2},{5,3},{6,0},{7,1},{8,14},{9,15},{10,... | collective-permute-start | bytes 208904 | tf_op jit(solution)/shard_map/ppermute | solution.py:384
  13.0 0.8 %collective-permute-done.3 = f32[136,128]{1,0:T(8,128)S(1)} collective-permute-done((f32[136,128]{1,0:T(8,128)S(1)}, f32[136,128]{1,0:T(8,128)S(1)}, u32[]{:S(2)}, u32[]{:S(2)}) %collective-permute-start.3) | collective-permute-done | bytes 69664 | tf_op jit(solution)/shard_map/ppermute | solution.py:384
  13.8 1.7 %collective-permute-done.4 = f32[136,128]{1,0:T(8,128)S(1)} collective-permute-done((f32[136,128]{1,0:T(8,128)S(1)}, f32[136,128]{1,0:T(8,128)S(1)}, u32[]{:S(2)}, u32[]{:S(2)}) %collective-permute-start.4) | collective-permute-done | bytes 69664 | tf_op jit(solution)/shard_map/ppermute | solution.py:384
  15.5 2.1 %collective-permute-done.5 = f32[136,128]{1,0:T(8,128)S(1)} collective-permute-done((f32[136,128]{1,0:T(8,128)S(1)}, f32[136,128]{1,0:T(8,128)S(1)}, u32[]{:S(2)}, u32[]{:S(2)}) %collective-permute-start.5) | collective-permute-done | bytes 69664 | tf_op jit(solution)/shard_map/ppermute | solution.py:384
  17.6 2.7 %collective-permute-start.6 = (f32[136,128]{1,0:T(8,128)S(1)}, f32[136,128]{1,0:T(8,128)S(1)}, u32[]{:S(2)}, u32[]{:S(2)}) collective-permute-start(f32[136,128]{1,0:T(8,128)S(1)} %add_add_fusion), channel_id=1, source_target_pairs={{0,8},{1,9},{2,10},{3,11},{4,12},{5,13},{6,14},{7,15},{8,0},{9,1},... | collective-permute-start | bytes 208904 | tf_op jit(solution)/shard_map/ppermute | solution.py:384
  20.9 2.7 %collective-permute-done.6 = f32[136,128]{1,0:T(8,128)S(1)} collective-permute-done((f32[136,128]{1,0:T(8,128)S(1)}, f32[136,128]{1,0:T(8,128)S(1)}, u32[]{:S(2)}, u32[]{:S(2)}) %collective-permute-start.6) | collective-permute-done | bytes 69664 | tf_op jit(solution)/shard_map/ppermute | solution.py:384
  23.6 0.6 %solve.1 = (f32[16,128]{1,0:T(8,128)S(1)}, f32[16,128]{1,0:T(8,128)S(1)}) custom-call(f32[136,128]{1,0:T(8,128)S(1)} %add.19.stats_ref, s32[1]{0:T(128)S(6)} %copy.14.ref_mic_ref), custom_call_target="tpu_custom_call" | custom-call | tf_op jit(solution)/shard_map/solve/pallas_call | solution.py:466
  24.2 0.1 collective-permute-start.7
  24.3 0.0 copy-done
  24.3 0.5 %power.1.mel_ref = f32[72,256]{1,0:T(8,128)S(1)} custom-call(f32[16,128]{1,0:T(8,128)S(1)} %get-tuple-element.29.mine_ref, f32[16,128]{1,0:T(8,128)S(1)} %get-tuple-element.30.last_ref, f32[6,512,128]{2,1,0:T(8,128)S(1)} %get-tuple-element.31.spec_ref, f32[6,64,128]{2,1,0:T(8,128)S(1)} %get-tuple-element.32.edge_spec_ref, f32[3,128,256]{2,1,0:T(8,128)S(1)} %copy-done), custom_call_target="tpu_custom_call" | custom-call | tf_op jit(solution)/shard_map/power/pallas_call | solution.py:477
  24.8 0.7 %collective-permute-done.7.theirs_ref = f32[16,128]{1,0:T(8,128)S(1)} collective-permute-done((f32[16,128]{1,0:T(8,128)S(1)}, f32[16,128]{1,0:T(8,128)S(1)}, u32[]{:S(2)}, u32[]{:S(2)}) %collective-permute-start.7) | collective-permute-done | bytes 8224 | tf_op jit(solution)/shard_map/ppermute | solution.py:384
  25.5 0.0 copy-done.1
  25.5 0.0 copy-done.2
  25.5 0.0 copy-done.3
  25.5 0.0 copy-done.4
  25.5 2.7 %stem.1 = bf16[1,16,256]{2,1,0:T(8,128)(2,1)} custom-call(f32[16,128]{1,0:T(8,128)S(1)} %collective-permute-done.7.theirs_ref, f32[72,256]{1,0:T(8,128)S(1)} %power.1.mel_ref, f32[6,512,128]{2,1,0:T(8,128)S(1)} %get-tuple-element.31.spec_ref, f32[6,64,128]{2,1,0:T(8,128)S(1)} %get-tuple-element.32.edge_spec_ref, s32[1]{0:T(128)S(6)} %copy.13.valid_ref, ...), custom_call_target="tpu_custom_call" | custom-call | tf_op jit(solution)/shard_map/stem/pallas_call | solution.py:485
  (3 shorter events, 0.0 us)
Async XLA Ops:
  1.3 6.3 %collective-permute-start = (bf16[8,512]{1,0:T(8,128)(2,1)S(1)}, bf16[8,512]{1,0:T(8,128)(2,1)S(1)}, u32[]{:S(2)}, u32[]{:S(2)}) collective-permute-start(bf16[8,512]{1,0:T(8,128)(2,1)S(1)} %get-tuple-element.20.own0_ref), channel_id=1, source_target_pairs={{0,1},{2,3},{4,5},{6,7},{8,9},{10,11},{12,13},{14,15},{16,17},{18,... | collective-permute-start | bytes 24584 | tf_op jit(solution)/shard_map/ppermute | solution.py:409
  1.8 5.8 %collective-permute-start.1 = (bf16[8,512]{1,0:T(8,128)(2,1)S(1)}, bf16[8,512]{1,0:T(8,128)(2,1)S(1)}, u32[]{:S(2)}, u32[]{:S(2)}) collective-permute-start(bf16[8,512]{1,0:T(8,128)(2,1)S(1)} %get-tuple-element.21.own1_ref), channel_id=1, source_target_pairs={{1,2},{3,4},{5,6},{7,8},{9,10},{11,12},{13,14},{0,16},{15,31},{17,... | collective-permute-start | bytes 24584 | tf_op jit(solution)/shard_map/ppermute | solution.py:409
  7.6 16.7 %copy-start = (f32[3,128,256]{2,1,0:T(8,128)S(1)}, f32[3,128,256]{2,1,0:T(8,128)}, u32[]{:S(2)}) copy-start(f32[3,128,256]{2,1,0:T(8,128)} %constant.5.clone.bank_ref) | copy-start | bytes 1179652
  8.1 17.4 %copy-start.1 = (bf16[9,256]{1,0:T(8,128)(2,1)S(1)}, bf16[9,256]{1,0:T(8,128)(2,1)}, u32[]{:S(2)}) copy-start(bf16[9,256]{1,0:T(8,128)(2,1)} %conv1_w_ref.1) | copy-start | bytes 13828
  8.1 17.4 %copy-start.2 = (f32[256]{0:T(256)S(1)}, f32[256]{0:T(256)}, u32[]{:S(2)}) copy-start(f32[256]{0:T(256)} %param.17) | copy-start | bytes 3076
  8.1 17.4 %copy-start.3 = (f32[256]{0:T(256)S(1)}, f32[256]{0:T(256)}, u32[]{:S(2)}) copy-start(f32[256]{0:T(256)} %param.19) | copy-start | bytes 3076
  8.1 17.4 %copy-start.4 = (f32[256]{0:T(256)S(1)}, f32[256]{0:T(256)}, u32[]{:S(2)}) copy-start(f32[256]{0:T(256)} %param.21) | copy-start | bytes 3076
  8.1 1.3 %collective-permute-start.2 = (f32[136,128]{1,0:T(8,128)S(1)}, f32[136,128]{1,0:T(8,128)S(1)}, u32[]{:S(2)}, u32[]{:S(2)}) collective-permute-start(f32[136,128]{1,0:T(8,128)S(1)} %get-tuple-element.28), channel_id=1, source_target_pairs={{0,1},{1,0},{2,3},{3,2},{4,5},{5,4},{6,7},{7,6},{8,9},{9,8},{10,11... | collective-permute-start | bytes 208904 | tf_op jit(solution)/shard_map/ppermute | solution.py:384
  9.4 4.4 %collective-permute-start.3 = (f32[136,128]{1,0:T(8,128)S(1)}, f32[136,128]{1,0:T(8,128)S(1)}, u32[]{:S(2)}, u32[]{:S(2)}) collective-permute-start(f32[136,128]{1,0:T(8,128)S(1)} %add.15), channel_id=1, source_target_pairs={{0,2},{1,3},{2,0},{3,1},{4,6},{5,7},{6,4},{7,5},{8,10},{9,11},{10,... | collective-permute-start | bytes 208904 | tf_op jit(solution)/shard_map/ppermute | solution.py:384
  10.8 4.7 %collective-permute-start.4 = (f32[136,128]{1,0:T(8,128)S(1)}, f32[136,128]{1,0:T(8,128)S(1)}, u32[]{:S(2)}, u32[]{:S(2)}) collective-permute-start(f32[136,128]{1,0:T(8,128)S(1)} %add.15), channel_id=1, source_target_pairs={{0,4},{1,5},{2,6},{3,7},{4,0},{5,1},{6,2},{7,3},{8,12},{9,13},{10,... | collective-permute-start | bytes 208904 | tf_op jit(solution)/shard_map/ppermute | solution.py:384
  12.4 5.2 %collective-permute-start.5 = (f32[136,128]{1,0:T(8,128)S(1)}, f32[136,128]{1,0:T(8,128)S(1)}, u32[]{:S(2)}, u32[]{:S(2)}) collective-permute-start(f32[136,128]{1,0:T(8,128)S(1)} %add.15), channel_id=1, source_target_pairs={{0,6},{1,7},{2,4},{3,5},{4,2},{5,3},{6,0},{7,1},{8,14},{9,15},{10,... | collective-permute-start | bytes 208904 | tf_op jit(solution)/shard_map/ppermute | solution.py:384
  17.6 6.0 %collective-permute-start.6 = (f32[136,128]{1,0:T(8,128)S(1)}, f32[136,128]{1,0:T(8,128)S(1)}, u32[]{:S(2)}, u32[]{:S(2)}) collective-permute-start(f32[136,128]{1,0:T(8,128)S(1)} %add_add_fusion), channel_id=1, source_target_pairs={{0,8},{1,9},{2,10},{3,11},{4,12},{5,13},{6,14},{7,15},{8,0},{9,1},... | collective-permute-start | bytes 208904 | tf_op jit(solution)/shard_map/ppermute | solution.py:384
  24.2 1.2 %collective-permute-start.7 = (f32[16,128]{1,0:T(8,128)S(1)}, f32[16,128]{1,0:T(8,128)S(1)}, u32[]{:S(2)}, u32[]{:S(2)}) collective-permute-start(f32[16,128]{1,0:T(8,128)S(1)} %get-tuple-element.29.mine_ref), channel_id=1, source_target_pairs={{0,1},{1,0},{2,3},{3,2},{4,5},{5,4},{6,7},{7,6},{8,9},{9,8},{10,11... | collective-permute-start | bytes 24584 | tf_op jit(solution)/shard_map/ppermute | solution.py:384

commit v8 on v7

--- a/solution.py
+++ b/solution.py
@@ -146,8 +146,8 @@
     return kept_sums(sums)
 
 
-def stats_kernel(frames, framed_ref, masks_ref, table_ref, conv2_w_hbm, proj_w_hbm, valid_ref, spec_ref, kept_ref, edge_weight_ref, conv2_w_ref, proj_w_ref, weight_ref, sem):
-    copies = started(((conv2_w_hbm, conv2_w_ref), (proj_w_hbm, proj_w_ref)), sem)
+def stats_kernel(frames, framed_ref, masks_ref, table_ref, conv2_w_hbm, valid_ref, spec_ref, kept_ref, edge_weight_ref, conv2_w_ref, weight_ref, sem):
+    copies = started(((conv2_w_hbm, conv2_w_ref),), sem)
     position = lax.axis_index("tm")
     spec = jnp.dot(framed_ref[...], table_ref[...], preferred_element_type=jnp.float32)
     for tile in range(2 * TILES):
@@ -434,24 +434,23 @@
     got_across = paired(across, 1)
     got_beside = paired(beside, 0)
     stat_block = jax.ShapeDtypeStruct((STATS + MICS, LANES), jnp.float32)
-    spec, kept, edge_weight, conv2_w, proj_w = pl.pallas_call(
+    spec, kept, edge_weight, conv2_w = pl.pallas_call(
         functools.partial(stats_kernel, frames),
         out_shape=(
             jax.ShapeDtypeStruct((2 * TILES, frames * MICS, LANES), jnp.float32),
             jax.ShapeDtypeStruct((TILES, STATS, LANES), jnp.float32),
             jax.ShapeDtypeStruct((TILES, 2, MICS, LANES), jnp.float32),
             jax.ShapeDtypeStruct(conv2_w.shape, conv2_w.dtype),
-            jax.ShapeDtypeStruct(proj_w.shape, proj_w.dtype),
         ),
-        in_specs=[vmem] * 3 + [hbm] * 2 + [smem],
-        out_specs=(vmem,) * 5,
+        in_specs=[vmem] * 3 + [hbm, smem],
+        out_specs=(vmem,) * 4,
         scratch_shapes=[
             pltpu.VMEM((TILES, 2, frames, LANES), jnp.float32),
-            pltpu.SemaphoreType.DMA((2,)),
+            pltpu.SemaphoreType.DMA((1,)),
         ],
         compiler_params=params,
         name="stats",
-    )(framed, levels, table, in_hbm(conv2_w), in_hbm(proj_w), valid)
+    )(framed, levels, table, in_hbm(conv2_w), valid)
     edge_spec, mine, theirs = pl.pallas_call(
         functools.partial(edges_kernel, lax.axis_size("tm")),
         out_shape=(jax.ShapeDtypeStruct((2 * TILES, MICS * MICS, LANES), jnp.float32), stat_block, stat_block),

time: 28.3 us -> 28 us (0.989)
  Pallas kernels: 8.01 us -> 7.66 us
    pallas_call x1, Pallas kernels: 2.56 us -> 2.2 us  [per_device(): pl.pallas_call(functools.partial(stats_kernel, frames), out_shape=(jax.Sh...]
  transfers between devices with their start and end apart: 8 -> 8, of which waited for: 6 -> 6; matrix products, arithmetic and copies ran while one was open for 0% -> 0% of each run, Pallas kernels for 11% -> 10%
where the time goes in v8:
time: 28 us; the launch traced here: 27.8 us
  starting transfers between devices  9.58 us (34%)
  waiting for transfers between devices  9.11 us (33%)
  Pallas kernels  7.66 us (27%)
  between operations  1.43 us (5%)
    ppermute x6, waiting for transfers between devices, flipped(): return lax.ppermute(block, axis, [(i, i ^ step) for i in range(size)])  9.11 us
    ppermute x6, starting transfers between devices, flipped(): return lax.ppermute(block, axis, [(i, i ^ step) for i in range(size)])  6.49 us
    ppermute x2, starting transfers between devices, paired(): lax.ppermute(block, ('meet', 'tm'), pairs + [(j, i) for i, j in pairs])  3.08 us
    pallas_call x1, Pallas kernels, per_device(): pl.pallas_call(functools.partial(stem_kernel, frames), out_shape=jax.Shap...  2.69 us
    pallas_call x1, Pallas kernels, per_device(): pl.pallas_call(functools.partial(stats_kernel, frames), out_shape=(jax.Sh...  2.2 us
    pallas_call x1, Pallas kernels, per_device(): pl.pallas_call(functools.partial(rims_kernel, frames), out_shape=(rim, ri...  1.27 us
    pallas_call x1, Pallas kernels, per_device(): pl.pallas_call(solve_kernel, out_shape=(beam, beam), in_specs=[vmem, smem...  0.59 us
  transfers between devices with their start and end apart: 8, of which 6 were waited for; matrix products, arithmetic and copies ran while one was open for 0% of the time, Pallas kernels for 10%

profile of v8, /device:TPU:0, one launch (start us, length us, event | category | flops | bytes accessed | tf_op | source)
XLA Modules:
  0.0 27.8 jit_solution(10140351790568084705)
XLA Ops:
  0.0 1.3 %rims.1 = (bf16[8,512]{1,0:T(8,128)(2,1)S(1)}, bf16[8,512]{1,0:T(8,128)(2,1)S(1)}, bf16[512,512]{1,0:T(8,128)(2,1)S(1)}, s32[2,64,257]{2,1,0:T(8,128)S(1)}, bf16[512,768]{1,0:T(8,128)(2,1)S(1)}) custom-call(bf16[8,10240]{1,0:T(8,128)(2,1)} %wave_hbm.1, s32[2,64,257]{2,1,0:T(8,128)} %masks_hbm.1, bf16[512,768]{1,0:T(8,128)(2,1)} %constant.8.table_hbm), custom_call_target="tpu_custom_call" | custom-call | tf_op jit(solution)/shard_map/rims/pallas_call | solution.py:424
  1.3 0.5 %collective-permute-start = (bf16[8,512]{1,0:T(8,128)(2,1)S(1)}, bf16[8,512]{1,0:T(8,128)(2,1)S(1)}, u32[]{:S(2)}, u32[]{:S(2)}) collective-permute-start(bf16[8,512]{1,0:T(8,128)(2,1)S(1)} %get-tuple-element.19.own0_ref), channel_id=1, source_target_pairs={{0,1},{2,3},{4,5},{6,7},{8,9},{10,11},{12,13},{14,15},{16,17},{18,... | collective-permute-start | bytes 24584 | tf_op jit(solution)/shard_map/ppermute | solution.py:409
  1.8 2.6 %collective-permute-start.1 = (bf16[8,512]{1,0:T(8,128)(2,1)S(1)}, bf16[8,512]{1,0:T(8,128)(2,1)S(1)}, u32[]{:S(2)}, u32[]{:S(2)}) collective-permute-start(bf16[8,512]{1,0:T(8,128)(2,1)S(1)} %get-tuple-element.20.own1_ref), channel_id=1, source_target_pairs={{1,2},{3,4},{5,6},{7,8},{9,10},{11,12},{13,14},{0,16},{15,31},{17,... | collective-permute-start | bytes 24584 | tf_op jit(solution)/shard_map/ppermute | solution.py:409
  5.0 2.2 %stats.1 = (f32[6,512,128]{2,1,0:T(8,128)S(1)}, f32[3,128,128]{2,1,0:T(8,128)S(1)}, f32[3,2,8,128]{3,2,1,0:T(8,128)S(1)}, bf16[2304,256]{1,0:T(8,128)(2,1)S(1)}) custom-call(bf16[512,512]{1,0:T(8,128)(2,1)S(1)} %get-tuple-element.22.framed_ref, s32[2,64,257]{2,1,0:T(8,128)S(1)} %get-tuple-element.23.masks_ref, ...), custom_call_target="tpu_custom_call" | custom-call | tf_op jit(solution)/shard_map/stats/pallas_call | solution.py:437
  7.2 0.0 copy-start.1
  7.2 0.0 collective-permute-done.got0_ref
  7.2 0.0 collective-permute-done.1.got1_ref
  7.3 0.4 %edges.1 = (f32[6,64,128]{2,1,0:T(8,128)S(1)}, f32[136,128]{1,0:T(8,128)S(1)}, f32[136,128]{1,0:T(8,128)S(1)}) custom-call(bf16[8,512]{1,0:T(8,128)(2,1)S(1)} %get-tuple-element.19.own0_ref, bf16[8,512]{1,0:T(8,128)(2,1)S(1)} %get-tuple-element.20.own1_ref, bf16[8,512]{1,0:T(8,128)(2,1)S(1)} %collective-permute-done.got0_ref, ...), custom_call_target="tpu_custom_call" | custom-call | tf_op jit(solution)/shard_map/edges/pallas_call | solution.py:454
  7.7 0.0 copy-start
  7.7 0.0 copy-start.4
  7.7 0.0 copy-start.5
  7.7 0.2 collective-permute-start.2
  7.9 1.1 %collective-permute-done.2 = f32[136,128]{1,0:T(8,128)S(1)} collective-permute-done((f32[136,128]{1,0:T(8,128)S(1)}, f32[136,128]{1,0:T(8,128)S(1)}, u32[]{:S(2)}, u32[]{:S(2)}) %collective-permute-start.2) | collective-permute-done | bytes 69664 | tf_op jit(solution)/shard_map/ppermute | solution.py:384
  9.1 1.4 %collective-permute-start.3 = (f32[136,128]{1,0:T(8,128)S(1)}, f32[136,128]{1,0:T(8,128)S(1)}, u32[]{:S(2)}, u32[]{:S(2)}) collective-permute-start(f32[136,128]{1,0:T(8,128)S(1)} %add.15), channel_id=1, source_target_pairs={{0,2},{1,3},{2,0},{3,1},{4,6},{5,7},{6,4},{7,5},{8,10},{9,11},{10,... | collective-permute-start | bytes 208904 | tf_op jit(solution)/shard_map/ppermute | solution.py:384
  10.4 1.6 %collective-permute-start.4 = (f32[136,128]{1,0:T(8,128)S(1)}, f32[136,128]{1,0:T(8,128)S(1)}, u32[]{:S(2)}, u32[]{:S(2)}) collective-permute-start(f32[136,128]{1,0:T(8,128)S(1)} %add.15), channel_id=1, source_target_pairs={{0,4},{1,5},{2,6},{3,7},{4,0},{5,1},{6,2},{7,3},{8,12},{9,13},{10,... | collective-permute-start | bytes 208904 | tf_op jit(solution)/shard_map/ppermute | solution.py:384
  12.0 0.6 %collective-permute-start.5 = (f32[136,128]{1,0:T(8,128)S(1)}, f32[136,128]{1,0:T(8,128)S(1)}, u32[]{:S(2)}, u32[]{:S(2)}) collective-permute-start(f32[136,128]{1,0:T(8,128)S(1)} %add.15), channel_id=1, source_target_pairs={{0,6},{1,7},{2,4},{3,5},{4,2},{5,3},{6,0},{7,1},{8,14},{9,15},{10,... | collective-permute-start | bytes 208904 | tf_op jit(solution)/shard_map/ppermute | solution.py:384
  12.6 0.8 %collective-permute-done.3 = f32[136,128]{1,0:T(8,128)S(1)} collective-permute-done((f32[136,128]{1,0:T(8,128)S(1)}, f32[136,128]{1,0:T(8,128)S(1)}, u32[]{:S(2)}, u32[]{:S(2)}) %collective-permute-start.3) | collective-permute-done | bytes 69664 | tf_op jit(solution)/shard_map/ppermute | solution.py:384
  13.4 1.7 %collective-permute-done.4 = f32[136,128]{1,0:T(8,128)S(1)} collective-permute-done((f32[136,128]{1,0:T(8,128)S(1)}, f32[136,128]{1,0:T(8,128)S(1)}, u32[]{:S(2)}, u32[]{:S(2)}) %collective-permute-start.4) | collective-permute-done | bytes 69664 | tf_op jit(solution)/shard_map/ppermute | solution.py:384
  15.2 2.1 %collective-permute-done.5 = f32[136,128]{1,0:T(8,128)S(1)} collective-permute-done((f32[136,128]{1,0:T(8,128)S(1)}, f32[136,128]{1,0:T(8,128)S(1)}, u32[]{:S(2)}, u32[]{:S(2)}) %collective-permute-start.5) | collective-permute-done | bytes 69664 | tf_op jit(solution)/shard_map/ppermute | solution.py:384
  17.3 2.7 %collective-permute-start.6 = (f32[136,128]{1,0:T(8,128)S(1)}, f32[136,128]{1,0:T(8,128)S(1)}, u32[]{:S(2)}, u32[]{:S(2)}) collective-permute-start(f32[136,128]{1,0:T(8,128)S(1)} %add_add_fusion), channel_id=1, source_target_pairs={{0,8},{1,9},{2,10},{3,11},{4,12},{5,13},{6,14},{7,15},{8,0},{9,1},... | collective-permute-start | bytes 208904 | tf_op jit(solution)/shard_map/ppermute | solution.py:384
  20.6 2.7 %collective-permute-done.6 = f32[136,128]{1,0:T(8,128)S(1)} collective-permute-done((f32[136,128]{1,0:T(8,128)S(1)}, f32[136,128]{1,0:T(8,128)S(1)}, u32[]{:S(2)}, u32[]{:S(2)}) %collective-permute-start.6) | collective-permute-done | bytes 69664 | tf_op jit(solution)/shard_map/ppermute | solution.py:384
  23.3 0.6 %solve.1 = (f32[16,128]{1,0:T(8,128)S(1)}, f32[16,128]{1,0:T(8,128)S(1)}) custom-call(f32[136,128]{1,0:T(8,128)S(1)} %add.19.stats_ref, s32[1]{0:T(128)S(6)} %copy.14.ref_mic_ref), custom_call_target="tpu_custom_call" | custom-call | tf_op jit(solution)/shard_map/solve/pallas_call | solution.py:465
  23.9 0.1 collective-permute-start.7
  24.0 0.0 copy-done.1
  24.0 0.5 %power.1.mel_ref = f32[72,256]{1,0:T(8,128)S(1)} custom-call(f32[16,128]{1,0:T(8,128)S(1)} %get-tuple-element.28.mine_ref, f32[16,128]{1,0:T(8,128)S(1)} %get-tuple-element.29.last_ref, f32[6,512,128]{2,1,0:T(8,128)S(1)} %get-tuple-element.30.spec_ref, f32[6,64,128]{2,1,0:T(8,128)S(1)} %get-tuple-element.31.edge_spec_ref, f32[3,128,256]{2,1,0:T(8,128)S(1)} %copy-done.1), custom_call_target="tpu_custom_call" | custom-call | tf_op jit(solution)/shard_map/power/pallas_call | solution.py:476
  24.4 0.7 %collective-permute-done.7.theirs_ref = f32[16,128]{1,0:T(8,128)S(1)} collective-permute-done((f32[16,128]{1,0:T(8,128)S(1)}, f32[16,128]{1,0:T(8,128)S(1)}, u32[]{:S(2)}, u32[]{:S(2)}) %collective-permute-start.7) | collective-permute-done | bytes 8224 | tf_op jit(solution)/shard_map/ppermute | solution.py:384
  25.1 0.0 copy-done
  25.1 0.0 copy-done.2
  25.1 0.0 copy-done.3
  25.1 0.0 copy-done.4
  25.1 0.0 copy-done.5
  25.2 2.7 %stem.1 = bf16[1,16,256]{2,1,0:T(8,128)(2,1)} custom-call(f32[16,128]{1,0:T(8,128)S(1)} %collective-permute-done.7.theirs_ref, f32[72,256]{1,0:T(8,128)S(1)} %power.1.mel_ref, f32[6,512,128]{2,1,0:T(8,128)S(1)} %get-tuple-element.30.spec_ref, f32[6,64,128]{2,1,0:T(8,128)S(1)} %get-tuple-element.31.edge_spec_ref, s32[1]{0:T(128)S(6)} %copy.13.valid_ref, ...), custom_call_target="tpu_custom_call" | custom-call | tf_op jit(solution)/shard_map/stem/pallas_call | solution.py:484
  (5 shorter events, 0.0 us)
Async XLA Ops:
  1.3 6.0 %collective-permute-start = (bf16[8,512]{1,0:T(8,128)(2,1)S(1)}, bf16[8,512]{1,0:T(8,128)(2,1)S(1)}, u32[]{:S(2)}, u32[]{:S(2)}) collective-permute-start(bf16[8,512]{1,0:T(8,128)(2,1)S(1)} %get-tuple-element.19.own0_ref), channel_id=1, source_target_pairs={{0,1},{2,3},{4,5},{6,7},{8,9},{10,11},{12,13},{14,15},{16,17},{18,... | collective-permute-start | bytes 24584 | tf_op jit(solution)/shard_map/ppermute | solution.py:409
  1.8 5.5 %collective-permute-start.1 = (bf16[8,512]{1,0:T(8,128)(2,1)S(1)}, bf16[8,512]{1,0:T(8,128)(2,1)S(1)}, u32[]{:S(2)}, u32[]{:S(2)}) collective-permute-start(bf16[8,512]{1,0:T(8,128)(2,1)S(1)} %get-tuple-element.20.own1_ref), channel_id=1, source_target_pairs={{1,2},{3,4},{5,6},{7,8},{9,10},{11,12},{13,14},{0,16},{15,31},{17,... | collective-permute-start | bytes 24584 | tf_op jit(solution)/shard_map/ppermute | solution.py:409
  7.2 16.7 %copy-start.1 = (f32[3,128,256]{2,1,0:T(8,128)S(1)}, f32[3,128,256]{2,1,0:T(8,128)}, u32[]{:S(2)}) copy-start(f32[3,128,256]{2,1,0:T(8,128)} %constant.5.clone.bank_ref) | copy-start | bytes 1179652
  7.7 17.4 %copy-start = (bf16[4864,256]{1,0:T(8,128)(2,1)S(1)}, bf16[4864,256]{1,0:T(8,128)(2,1)}, u32[]{:S(2)}) copy-start(bf16[4864,256]{1,0:T(8,128)(2,1)} %proj_w_ref.1) | copy-start | bytes 7471108
  7.7 17.4 %copy-start.2 = (bf16[9,256]{1,0:T(8,128)(2,1)S(1)}, bf16[9,256]{1,0:T(8,128)(2,1)}, u32[]{:S(2)}) copy-start(bf16[9,256]{1,0:T(8,128)(2,1)} %conv1_w_ref.1) | copy-start | bytes 13828
  7.7 17.4 %copy-start.3 = (f32[256]{0:T(256)S(1)}, f32[256]{0:T(256)}, u32[]{:S(2)}) copy-start(f32[256]{0:T(256)} %param.17) | copy-start | bytes 3076
  7.7 17.4 %copy-start.4 = (f32[256]{0:T(256)S(1)}, f32[256]{0:T(256)}, u32[]{:S(2)}) copy-start(f32[256]{0:T(256)} %param.19) | copy-start | bytes 3076
  7.7 17.4 %copy-start.5 = (f32[256]{0:T(256)S(1)}, f32[256]{0:T(256)}, u32[]{:S(2)}) copy-start(f32[256]{0:T(256)} %param.21) | copy-start | bytes 3076
  7.7 1.3 %collective-permute-start.2 = (f32[136,128]{1,0:T(8,128)S(1)}, f32[136,128]{1,0:T(8,128)S(1)}, u32[]{:S(2)}, u32[]{:S(2)}) collective-permute-start(f32[136,128]{1,0:T(8,128)S(1)} %get-tuple-element.27), channel_id=1, source_target_pairs={{0,1},{1,0},{2,3},{3,2},{4,5},{5,4},{6,7},{7,6},{8,9},{9,8},{10,11... | collective-permute-start | bytes 208904 | tf_op jit(solution)/shard_map/ppermute | solution.py:384
  9.1 4.4 %collective-permute-start.3 = (f32[136,128]{1,0:T(8,128)S(1)}, f32[136,128]{1,0:T(8,128)S(1)}, u32[]{:S(2)}, u32[]{:S(2)}) collective-permute-start(f32[136,128]{1,0:T(8,128)S(1)} %add.15), channel_id=1, source_target_pairs={{0,2},{1,3},{2,0},{3,1},{4,6},{5,7},{6,4},{7,5},{8,10},{9,11},{10,... | collective-permute-start | bytes 208904 | tf_op jit(solution)/shard_map/ppermute | solution.py:384
  10.4 4.7 %collective-permute-start.4 = (f32[136,128]{1,0:T(8,128)S(1)}, f32[136,128]{1,0:T(8,128)S(1)}, u32[]{:S(2)}, u32[]{:S(2)}) collective-permute-start(f32[136,128]{1,0:T(8,128)S(1)} %add.15), channel_id=1, source_target_pairs={{0,4},{1,5},{2,6},{3,7},{4,0},{5,1},{6,2},{7,3},{8,12},{9,13},{10,... | collective-permute-start | bytes 208904 | tf_op jit(solution)/shard_map/ppermute | solution.py:384
  12.0 5.2 %collective-permute-start.5 = (f32[136,128]{1,0:T(8,128)S(1)}, f32[136,128]{1,0:T(8,128)S(1)}, u32[]{:S(2)}, u32[]{:S(2)}) collective-permute-start(f32[136,128]{1,0:T(8,128)S(1)} %add.15), channel_id=1, source_target_pairs={{0,6},{1,7},{2,4},{3,5},{4,2},{5,3},{6,0},{7,1},{8,14},{9,15},{10,... | collective-permute-start | bytes 208904 | tf_op jit(solution)/shard_map/ppermute | solution.py:384
  17.3 6.0 %collective-permute-start.6 = (f32[136,128]{1,0:T(8,128)S(1)}, f32[136,128]{1,0:T(8,128)S(1)}, u32[]{:S(2)}, u32[]{:S(2)}) collective-permute-start(f32[136,128]{1,0:T(8,128)S(1)} %add_add_fusion), channel_id=1, source_target_pairs={{0,8},{1,9},{2,10},{3,11},{4,12},{5,13},{6,14},{7,15},{8,0},{9,1},... | collective-permute-start | bytes 208904 | tf_op jit(solution)/shard_map/ppermute | solution.py:384
  23.9 1.2 %collective-permute-start.7 = (f32[16,128]{1,0:T(8,128)S(1)}, f32[16,128]{1,0:T(8,128)S(1)}, u32[]{:S(2)}, u32[]{:S(2)}) collective-permute-start(f32[16,128]{1,0:T(8,128)S(1)} %get-tuple-element.28.mine_ref), channel_id=1, source_target_pairs={{0,1},{1,0},{2,3},{3,2},{4,5},{5,4},{6,7},{7,6},{8,9},{9,8},{10,11... | collective-permute-start | bytes 24584 | tf_op jit(solution)/shard_map/ppermute | solution.py:384

commit v9 on v8

--- a/solution.py
+++ b/solution.py
@@ -182,36 +182,38 @@
         copy.wait()
 
 
-def edges_kernel(devices, own0_ref, own1_ref, got0_ref, got1_ref, table_ref, edge_weight_ref, kept_ref, spec_ref, mine_ref, theirs_ref, framed_ref):
-    position = lax.axis_index("tm")
-    even = position % 2 == 0
-    own = [own0_ref[...].astype(jnp.float32), own1_ref[...].astype(jnp.float32)]
-    got = [got0_ref[...].astype(jnp.float32), got1_ref[...].astype(jnp.float32)]
-    head, tail = jnp.where(even, own[1], own[0]), jnp.where(even, own[0], own[1])
-    prev, after = jnp.where(even, got[1], got[0]), jnp.where(even, got[0], got[1])
-    prev = jnp.where(position > 0, prev, 0.0)
-    after = jnp.where(position < devices - 1, after, 0.0)
-    joined = jnp.concatenate(
-        [jnp.concatenate([prev, head[:, :TAIL]], axis=1), jnp.concatenate([tail, after[:, :TAIL]], axis=1)], axis=0
-    )
+def edge_frames(tail, head, table, framed_ref):
+    joined = jnp.concatenate([tail, head[:, :TAIL]], axis=1)
     for i in range(HALO):
         start = LEAD - HALO * HOP + i * HOP
         base, shift = start // LANES * LANES, start % LANES
         turned = joined if shift == 0 else pltpu.roll(joined, joined.shape[1] - shift, 1)
-        framed_ref[2 * MICS * i : 2 * MICS * (i + 1), :] = turned[:, base : base + NFFT]
-    used = 2 * MICS * HALO
+        framed_ref[MICS * i : MICS * (i + 1), :] = turned[:, base : base + NFFT]
+    used = MICS * HALO
     framed_ref[used:, :] = jnp.zeros((framed_ref.shape[0] - used, NFFT), jnp.float32)
-    spec = jnp.dot(framed_ref[...].astype(jnp.bfloat16), table_ref[...], preferred_element_type=jnp.float32)
+    return jnp.dot(framed_ref[...].astype(jnp.bfloat16), table, preferred_element_type=jnp.float32)
+
+
+def edge_sums(spec_ref, first, tile, weights):
+    sums = (jnp.zeros((MICS, LANES), jnp.float32),) * 18
+    for i in range(HALO):
+        rows = slice(first + MICS * i, first + MICS * (i + 1))
+        at = MICS - HALO + i
+        sums = add_frame(sums, spec_ref[tile, rows, :], spec_ref[TILES + tile, rows, :], [w[at : at + 1] for w in weights])
+    return kept_sums(sums)
+
+
+def edges_kernel(devices, own_ref, got_ref, beside_ref, table_ref, edge_weight_ref, kept_ref, spec_ref, mine_ref, theirs_ref, framed_ref):
+    position = lax.axis_index("tm")
+    even = position % 2 == 0
+    own = own_ref[...].astype(jnp.float32)
+    got = jnp.where((position > 0) & (position < devices - 1), got_ref[...].astype(jnp.float32), 0.0)
+    spec = edge_frames(jnp.where(even, got, own), jnp.where(even, own, got), table_ref[...], framed_ref)
     for tile in range(2 * TILES):
         spec_ref[tile] = spec[:, tile * LANES : (tile + 1) * LANES]
     for slot, tile in enumerate(slot_tiles(position)):
-        sums = (jnp.zeros((MICS, LANES), jnp.float32),) * 18
-        for i in range(HALO):
-            rows = slice((2 * i + 1) * MICS, (2 * i + 2) * MICS)
-            at = MICS - HALO + i
-            weights = [edge_weight_ref[tile, k, at : at + 1, :] for k in range(2)]
-            sums = add_frame(sums, spec_ref[tile, rows, :], spec_ref[TILES + tile, rows, :], weights)
-        total = kept_ref[slot] + kept_sums(sums)
+        weights = [jnp.where(even, 0.0, edge_weight_ref[tile, k]) for k in range(2)]
+        total = kept_ref[slot] + edge_sums(spec_ref, 0, tile, weights)
         if slot == 0:
             mine_ref[:STATS, :] = total
         elif slot == 1:
@@ -219,7 +221,39 @@
         else:
             last_bin = jnp.transpose(total)[:MICS]
             mine_ref[STATS:, :] = last_bin
-            theirs_ref[STATS:, :] = last_bin
+            theirs_ref[STATS : STATS + MICS, :] = last_bin
+    first = STATS + MICS
+    beside = beside_ref[...].astype(jnp.float32)
+    sent = [beside[:, at : at + LANES] for at in range(0, LEAD, LANES)]
+    sent += [edge_weight_ref[tile, k] for tile in slot_tiles(position)[1:] for k in range(2)]
+    for i, rows in enumerate(sent):
+        theirs_ref[first + MICS * i : first + MICS * (i + 1), :] = rows
+
+
+def chip_kernel(mine_ref, got_ref, beside_ref, table_ref, edge_weight_ref, across_spec_ref, stats_ref, spec_ref, framed_ref):
+    position = lax.axis_index("tm")
+    even = position % 2 == 0
+    first = STATS + MICS
+    got = jnp.concatenate([got_ref[first + MICS * i : first + MICS * (i + 1), :] for i in range(LEAD // LANES)], axis=1)
+    own = beside_ref[...].astype(jnp.float32)
+    spec = edge_frames(jnp.where(even, own, got), jnp.where(even, got, own), table_ref[...], framed_ref)
+    used = MICS * HALO
+    for tile in range(2 * TILES):
+        spec_ref[tile, :used, :] = across_spec_ref[tile, :used, :]
+        spec_ref[tile, used : used + framed_ref.shape[0], :] = spec[:, tile * LANES : (tile + 1) * LANES]
+        spec_ref[tile, used + framed_ref.shape[0] :, :] = jnp.zeros((MICS, LANES), jnp.float32)
+    first += LEAD // LANES * MICS
+    for part, tile in enumerate((slot_tiles(position)[0], TILES - 1)):
+        weights = []
+        for k in range(2):
+            at = first + (2 * part + k) * MICS
+            weights.append(jnp.where(even, edge_weight_ref[tile, k], got_ref[at : at + MICS, :]))
+        total = edge_sums(spec_ref, used, tile, weights)
+        if part == 0:
+            stats_ref[:STATS, :] = mine_ref[:STATS, :] + got_ref[:STATS, :] + total
+        else:
+            last_bin = mine_ref[STATS:, :] + got_ref[STATS : STATS + MICS, :]
+            stats_ref[STATS:, :] = last_bin + jnp.transpose(total)[:MICS]
 
 
 def columns_of(kept, sub):
@@ -332,7 +366,10 @@
     theirs = slot_tiles(position)[1]
     mel = mel_ref[...] + mel_of(power_of(theirs_ref, theirs, spec_ref, edge_spec_ref), bank_ref[theirs])
     row = lax.broadcasted_iota(jnp.int32, (frames + MICS, 1), 0)
-    edge = (row - frames) // 2 + jnp.where((row - frames) % 2 == 0, -HALO, frames - HALO)
+    even = position % 2 == 0
+    slot = row - frames
+    before = (slot < HALO) == even
+    edge = slot - jnp.where(slot < HALO, 0, HALO) + jnp.where(before, -HALO, frames - HALO)
     time = position * frames + jnp.where(row < frames, row, edge)
     live = (time >= 0) & (time < valid)
     logmel = jnp.where(live, jnp.log(mel + epsilon), 0.0)
@@ -340,9 +377,9 @@
     for half in range(2):
         part = logmel[:, half * LANES : (half + 1) * LANES]
         logmel_ref[half, HALO : HALO + frames, :] = part[:frames]
-        for i in range(HALO):
-            logmel_ref[half, i : i + 1, :] = part[frames + 2 * i : frames + 2 * i + 1]
-            logmel_ref[half, frames + i : frames + i + 1, :] = part[frames + 2 * i + 1 : frames + 2 * i + 2]
+        across, within = part[frames : frames + HALO], part[frames + HALO : frames + 2 * HALO]
+        logmel_ref[half, :HALO, :] = jnp.where(even, across, within)
+        logmel_ref[half, HALO + frames - HALO : frames + HALO, :] = jnp.where(even, within, across)
 
     q_first = (MELS - 3) // 2 + 1
     q_second = (q_first - 3) // 2 + 1
@@ -432,8 +469,6 @@
         name="rims",
     )(in_hbm(waveform), in_hbm(masks), in_hbm(table))
     got_across = paired(across, 1)
-    got_beside = paired(beside, 0)
-    stat_block = jax.ShapeDtypeStruct((STATS + MICS, LANES), jnp.float32)
     spec, kept, edge_weight, conv2_w = pl.pallas_call(
         functools.partial(stats_kernel, frames),
         out_shape=(
@@ -451,16 +486,32 @@
         compiler_params=params,
         name="stats",
     )(framed, levels, table, in_hbm(conv2_w), valid)
-    edge_spec, mine, theirs = pl.pallas_call(
+    edge_rows = (HALO + 1) * MICS
+    sent_rows = STATS + MICS + LEAD // LANES * MICS + 4 * MICS
+    across_spec, mine, theirs = pl.pallas_call(
         functools.partial(edges_kernel, lax.axis_size("tm")),
-        out_shape=(jax.ShapeDtypeStruct((2 * TILES, MICS * MICS, LANES), jnp.float32), stat_block, stat_block),
-        in_specs=[vmem] * 7,
+        out_shape=tuple(
+            jax.ShapeDtypeStruct(shape, jnp.float32)
+            for shape in ((2 * TILES, edge_rows, LANES), (STATS + MICS, LANES), (sent_rows, LANES))
+        ),
+        in_specs=[vmem] * 6,
         out_specs=(vmem,) * 3,
-        scratch_shapes=[pltpu.VMEM((MICS * MICS, NFFT), jnp.float32)],
+        scratch_shapes=[pltpu.VMEM((edge_rows, NFFT), jnp.float32)],
         compiler_params=params,
         name="edges",
-    )(beside, across, got_beside, got_across, table, edge_weight, kept)
-    stats = summed_over_chips(mine + flipped(theirs, "tm", 1), "tm")
+    )(across, got_across, beside, table, edge_weight, kept)
+    stats, edge_spec = pl.pallas_call(
+        chip_kernel,
+        out_shape=tuple(
+            jax.ShapeDtypeStruct(shape, jnp.float32) for shape in ((STATS + MICS, LANES), (2 * TILES, MICS * MICS, LANES))
+        ),
+        in_specs=[vmem] * 6,
+        out_specs=(vmem,) * 2,
+        scratch_shapes=[pltpu.VMEM((edge_rows, NFFT), jnp.float32)],
+        compiler_params=params,
+        name="chip",
+    )(mine, flipped(theirs, "tm", 1), beside, table, edge_weight, across_spec)
+    stats = summed_over_chips(stats, "tm")
     beam = jax.ShapeDtypeStruct((2 * MICS, LANES), jnp.float32)
     beam_mine, beam_last = pl.pallas_call(
         solve_kernel,

time: 28 us -> 28.3 us (1.011)
  starting transfers between devices: 9.58 us -> 8.88 us
  waiting for transfers between devices: 9.11 us -> 9.74 us
  Pallas kernels: 7.66 us -> 8.04 us
    ppermute x6, waiting for transfers between devices: 9.11 us -> 9.73 us  [flipped(): return lax.ppermute(block, axis, [(i, i ^ step) for i in range(size)])]
    ppermute x6, starting transfers between devices: 6.49 us -> 5.87 us  [flipped(): return lax.ppermute(block, axis, [(i, i ^ step) for i in range(size)])]
    pallas_call x0 -> x1, Pallas kernels: none -> 0.39 us  [per_device(): pl.pallas_call(chip_kernel, out_shape=tuple((jax.ShapeDtypeStruct(shape,...]
    ppermute x2 -> x1, starting transfers between devices: 3.08 us -> 3 us  [paired(): lax.ppermute(block, ('meet', 'tm'), pairs + [(j, i) for i, j in pairs])]
  transfers between devices with their start and end apart: 8 -> 7, of which waited for: 6 -> 6; matrix products, arithmetic and copies ran while one was open for 0% -> 0% of each run, Pallas kernels for 10% -> 9%
where the time goes in v9:
time: 28.3 us; the launch traced here: 28.1 us
  waiting for transfers between devices  9.74 us (34%)
  starting transfers between devices  8.88 us (31%)
  Pallas kernels  8.04 us (28%)
  between operations  1.41 us (5%)
    ppermute x6, waiting for transfers between devices, flipped(): return lax.ppermute(block, axis, [(i, i ^ step) for i in range(size)])  9.73 us
    ppermute x6, starting transfers between devices, flipped(): return lax.ppermute(block, axis, [(i, i ^ step) for i in range(size)])  5.87 us
    ppermute x1, starting transfers between devices, paired(): lax.ppermute(block, ('meet', 'tm'), pairs + [(j, i) for i, j in pairs])  3 us
    pallas_call x1, Pallas kernels, per_device(): pl.pallas_call(functools.partial(stem_kernel, frames), out_shape=jax.Shap...  2.7 us
    pallas_call x1, Pallas kernels, per_device(): pl.pallas_call(functools.partial(stats_kernel, frames), out_shape=(jax.Sh...  2.2 us
    pallas_call x1, Pallas kernels, per_device(): pl.pallas_call(functools.partial(rims_kernel, frames), out_shape=(rim, ri...  1.27 us
    pallas_call x1, Pallas kernels, per_device(): pl.pallas_call(solve_kernel, out_shape=(beam, beam), in_specs=[vmem, smem...  0.59 us
  transfers between devices with their start and end apart: 7, of which 6 were waited for; matrix products, arithmetic and copies ran while one was open for 0% of the time, Pallas kernels for 9%

profile of v9, /device:TPU:0, one launch (start us, length us, event | category | flops | bytes accessed | tf_op | source)
XLA Modules:
  0.0 28.1 jit_solution(10535151884293744895)
XLA Ops:
  0.0 1.3 %rims.1 = (bf16[8,512]{1,0:T(8,128)(2,1)S(1)}, bf16[8,512]{1,0:T(8,128)(2,1)S(1)}, bf16[512,512]{1,0:T(8,128)(2,1)S(1)}, s32[2,64,257]{2,1,0:T(8,128)S(1)}, bf16[512,768]{1,0:T(8,128)(2,1)S(1)}) custom-call(bf16[8,10240]{1,0:T(8,128)(2,1)} %wave_hbm.1, s32[2,64,257]{2,1,0:T(8,128)} %masks_hbm.1, bf16[512,768]{1,0:T(8,128)(2,1)} %constant.8.table_hbm), custom_call_target="tpu_custom_call" | custom-call | tf_op jit(solution)/shard_map/rims/pallas_call | solution.py:461
  1.3 3.0 %collective-permute-start = (bf16[8,512]{1,0:T(8,128)(2,1)S(1)}, bf16[8,512]{1,0:T(8,128)(2,1)S(1)}, u32[]{:S(2)}, u32[]{:S(2)}) collective-permute-start(bf16[8,512]{1,0:T(8,128)(2,1)S(1)} %get-tuple-element.21.own_ref), channel_id=1, source_target_pairs={{1,2},{3,4},{5,6},{7,8},{9,10},{11,12},{13,14},{0,16},{15,31},{17,... | collective-permute-start | bytes 24584 | tf_op jit(solution)/shard_map/ppermute | solution.py:446
  4.9 2.2 %stats.1 = (f32[6,512,128]{2,1,0:T(8,128)S(1)}, f32[3,128,128]{2,1,0:T(8,128)S(1)}, f32[3,2,8,128]{3,2,1,0:T(8,128)S(1)}, bf16[2304,256]{1,0:T(8,128)(2,1)S(1)}) custom-call(bf16[512,512]{1,0:T(8,128)(2,1)S(1)} %get-tuple-element.24.framed_ref, s32[2,64,257]{2,1,0:T(8,128)S(1)} %get-tuple-element.25.masks_ref, ...), custom_call_target="tpu_custom_call" | custom-call | tf_op jit(solution)/shard_map/stats/pallas_call | solution.py:472
  7.1 0.0 copy-start.1
  7.2 0.0 collective-permute-done.got_ref
  7.2 0.4 %edges.1 = (f32[6,32,128]{2,1,0:T(8,128)S(1)}, f32[136,128]{1,0:T(8,128)S(1)}, f32[200,128]{1,0:T(8,128)S(1)}) custom-call(bf16[8,512]{1,0:T(8,128)(2,1)S(1)} %get-tuple-element.21.own_ref, bf16[8,512]{1,0:T(8,128)(2,1)S(1)} %collective-permute-done.got_ref, bf16[8,512]{1,0:T(8,128)(2,1)S(1)} %get-tuple-element.22.beside_ref, ...), custom_call_target="tpu_custom_call" | custom-call | tf_op jit(solution)/shard_map/edges/pallas_call | solution.py:491
  7.6 0.2 collective-permute-start.1
  7.8 1.2 %collective-permute-done.1.got_ref = f32[200,128]{1,0:T(8,128)S(1)} collective-permute-done((f32[200,128]{1,0:T(8,128)S(1)}, f32[200,128]{1,0:T(8,128)S(1)}, u32[]{:S(2)}, u32[]{:S(2)}) %collective-permute-start.1) | collective-permute-done | bytes 102432 | tf_op jit(solution)/shard_map/ppermute | solution.py:421
  8.9 0.4 %chip.1 = (f32[136,128]{1,0:T(8,128)S(1)}, f32[6,64,128]{2,1,0:T(8,128)S(1)}) custom-call(f32[136,128]{1,0:T(8,128)S(1)} %get-tuple-element.28.mine_ref, f32[200,128]{1,0:T(8,128)S(1)} %collective-permute-done.1.got_ref, bf16[8,512]{1,0:T(8,128)(2,1)S(1)} %get-tuple-element.22.beside_ref, bf16[512,768]{1,0:T(8,128)(2,1)S(1)} %get-tuple-element.23.table_ref, ...), custom_call_target="tpu_custom_call" | custom-call | tf_op jit(solution)/shard_map/chip/pallas_call | solution.py:503
  9.3 0.0 copy-start
  9.3 0.0 copy-start.2
  9.3 0.0 copy-start.4
  9.4 0.0 copy-start.5
  9.4 1.4 %collective-permute-start.2 = (f32[136,128]{1,0:T(8,128)S(1)}, f32[136,128]{1,0:T(8,128)S(1)}, u32[]{:S(2)}, u32[]{:S(2)}) collective-permute-start(f32[136,128]{1,0:T(8,128)S(1)} %get-tuple-element.31), channel_id=1, source_target_pairs={{0,2},{1,3},{2,0},{3,1},{4,6},{5,7},{6,4},{7,5},{8,10},{9,11},{10,... | collective-permute-start | bytes 208904 | tf_op jit(solution)/shard_map/ppermute | solution.py:421
  10.8 1.6 %collective-permute-start.3 = (f32[136,128]{1,0:T(8,128)S(1)}, f32[136,128]{1,0:T(8,128)S(1)}, u32[]{:S(2)}, u32[]{:S(2)}) collective-permute-start(f32[136,128]{1,0:T(8,128)S(1)} %get-tuple-element.31), channel_id=1, source_target_pairs={{0,4},{1,5},{2,6},{3,7},{4,0},{5,1},{6,2},{7,3},{8,12},{9,13},{10,... | collective-permute-start | bytes 208904 | tf_op jit(solution)/shard_map/ppermute | solution.py:421
  12.3 0.6 %collective-permute-start.4 = (f32[136,128]{1,0:T(8,128)S(1)}, f32[136,128]{1,0:T(8,128)S(1)}, u32[]{:S(2)}, u32[]{:S(2)}) collective-permute-start(f32[136,128]{1,0:T(8,128)S(1)} %get-tuple-element.31), channel_id=1, source_target_pairs={{0,6},{1,7},{2,4},{3,5},{4,2},{5,3},{6,0},{7,1},{8,14},{9,15},{10,... | collective-permute-start | bytes 208904 | tf_op jit(solution)/shard_map/ppermute | solution.py:421
  12.9 0.8 %collective-permute-done.2 = f32[136,128]{1,0:T(8,128)S(1)} collective-permute-done((f32[136,128]{1,0:T(8,128)S(1)}, f32[136,128]{1,0:T(8,128)S(1)}, u32[]{:S(2)}, u32[]{:S(2)}) %collective-permute-start.2) | collective-permute-done | bytes 69664 | tf_op jit(solution)/shard_map/ppermute | solution.py:421
  13.7 1.7 %collective-permute-done.3 = f32[136,128]{1,0:T(8,128)S(1)} collective-permute-done((f32[136,128]{1,0:T(8,128)S(1)}, f32[136,128]{1,0:T(8,128)S(1)}, u32[]{:S(2)}, u32[]{:S(2)}) %collective-permute-start.3) | collective-permute-done | bytes 69664 | tf_op jit(solution)/shard_map/ppermute | solution.py:421
  15.5 2.1 %collective-permute-done.4 = f32[136,128]{1,0:T(8,128)S(1)} collective-permute-done((f32[136,128]{1,0:T(8,128)S(1)}, f32[136,128]{1,0:T(8,128)S(1)}, u32[]{:S(2)}, u32[]{:S(2)}) %collective-permute-start.4) | collective-permute-done | bytes 69664 | tf_op jit(solution)/shard_map/ppermute | solution.py:421
  17.6 2.1 %collective-permute-start.5 = (f32[136,128]{1,0:T(8,128)S(1)}, f32[136,128]{1,0:T(8,128)S(1)}, u32[]{:S(2)}, u32[]{:S(2)}) collective-permute-start(f32[136,128]{1,0:T(8,128)S(1)} %add_add_fusion), channel_id=1, source_target_pairs={{0,8},{1,9},{2,10},{3,11},{4,12},{5,13},{6,14},{7,15},{8,0},{9,1},... | collective-permute-start | bytes 208904 | tf_op jit(solution)/shard_map/ppermute | solution.py:421
  20.3 3.3 %collective-permute-done.5 = f32[136,128]{1,0:T(8,128)S(1)} collective-permute-done((f32[136,128]{1,0:T(8,128)S(1)}, f32[136,128]{1,0:T(8,128)S(1)}, u32[]{:S(2)}, u32[]{:S(2)}) %collective-permute-start.5) | collective-permute-done | bytes 69664 | tf_op jit(solution)/shard_map/ppermute | solution.py:421
  23.6 0.6 %solve.1 = (f32[16,128]{1,0:T(8,128)S(1)}, f32[16,128]{1,0:T(8,128)S(1)}) custom-call(f32[136,128]{1,0:T(8,128)S(1)} %add.15.stats_ref, s32[1]{0:T(128)S(6)} %copy.14.ref_mic_ref), custom_call_target="tpu_custom_call" | custom-call | tf_op jit(solution)/shard_map/solve/pallas_call | solution.py:516
  24.2 0.1 collective-permute-start.6
  24.2 0.0 copy-done.1
  24.3 0.5 %power.1.mel_ref = f32[72,256]{1,0:T(8,128)S(1)} custom-call(f32[16,128]{1,0:T(8,128)S(1)} %get-tuple-element.32.mine_ref, f32[16,128]{1,0:T(8,128)S(1)} %get-tuple-element.33.last_ref, f32[6,512,128]{2,1,0:T(8,128)S(1)} %get-tuple-element.34.spec_ref, f32[6,64,128]{2,1,0:T(8,128)S(1)} %get-tuple-element.35.edge_spec_ref, f32[3,128,256]{2,1,0:T(8,128)S(1)} %copy-done.1), custom_call_target="tpu_custom_call" | custom-call | tf_op jit(solution)/shard_map/power/pallas_call | solution.py:527
  24.7 0.7 %collective-permute-done.6.theirs_ref = f32[16,128]{1,0:T(8,128)S(1)} collective-permute-done((f32[16,128]{1,0:T(8,128)S(1)}, f32[16,128]{1,0:T(8,128)S(1)}, u32[]{:S(2)}, u32[]{:S(2)}) %collective-permute-start.6) | collective-permute-done | bytes 8224 | tf_op jit(solution)/shard_map/ppermute | solution.py:421
  25.4 0.0 copy-done
  25.4 0.0 copy-done.2
  25.4 0.0 copy-done.3
  25.4 0.0 copy-done.4
  25.4 0.0 copy-done.5
  25.4 2.7 %stem.1 = bf16[1,16,256]{2,1,0:T(8,128)(2,1)} custom-call(f32[16,128]{1,0:T(8,128)S(1)} %collective-permute-done.6.theirs_ref, f32[72,256]{1,0:T(8,128)S(1)} %power.1.mel_ref, f32[6,512,128]{2,1,0:T(8,128)S(1)} %get-tuple-element.34.spec_ref, f32[6,64,128]{2,1,0:T(8,128)S(1)} %get-tuple-element.35.edge_spec_ref, s32[1]{0:T(128)S(6)} %copy.13.valid_ref, ...), custom_call_target="tpu_custom_call" | custom-call | tf_op jit(solution)/shard_map/stem/pallas_call | solution.py:535
  (3 shorter events, 0.0 us)
Async XLA Ops:
  1.3 5.9 %collective-permute-start = (bf16[8,512]{1,0:T(8,128)(2,1)S(1)}, bf16[8,512]{1,0:T(8,128)(2,1)S(1)}, u32[]{:S(2)}, u32[]{:S(2)}) collective-permute-start(bf16[8,512]{1,0:T(8,128)(2,1)S(1)} %get-tuple-element.21.own_ref), channel_id=1, source_target_pairs={{1,2},{3,4},{5,6},{7,8},{9,10},{11,12},{13,14},{0,16},{15,31},{17,... | collective-permute-start | bytes 24584 | tf_op jit(solution)/shard_map/ppermute | solution.py:446
  7.1 17.1 %copy-start.1 = (f32[3,128,256]{2,1,0:T(8,128)S(1)}, f32[3,128,256]{2,1,0:T(8,128)}, u32[]{:S(2)}) copy-start(f32[3,128,256]{2,1,0:T(8,128)} %constant.5.clone.bank_ref) | copy-start | bytes 1179652
  7.6 1.3 %collective-permute-start.1 = (f32[200,128]{1,0:T(8,128)S(1)}, f32[200,128]{1,0:T(8,128)S(1)}, u32[]{:S(2)}, u32[]{:S(2)}) collective-permute-start(f32[200,128]{1,0:T(8,128)S(1)} %get-tuple-element.29), channel_id=1, source_target_pairs={{0,1},{1,0},{2,3},{3,2},{4,5},{5,4},{6,7},{7,6},{8,9},{9,8},{10,11... | collective-permute-start | bytes 307208 | tf_op jit(solution)/shard_map/ppermute | solution.py:421
  9.3 16.1 %copy-start = (bf16[4864,256]{1,0:T(8,128)(2,1)S(1)}, bf16[4864,256]{1,0:T(8,128)(2,1)}, u32[]{:S(2)}) copy-start(bf16[4864,256]{1,0:T(8,128)(2,1)} %proj_w_ref.1) | copy-start | bytes 7471108
  9.3 16.1 %copy-start.2 = (bf16[9,256]{1,0:T(8,128)(2,1)S(1)}, bf16[9,256]{1,0:T(8,128)(2,1)}, u32[]{:S(2)}) copy-start(bf16[9,256]{1,0:T(8,128)(2,1)} %conv1_w_ref.1) | copy-start | bytes 13828
  9.3 16.1 %copy-start.3 = (f32[256]{0:T(256)S(1)}, f32[256]{0:T(256)}, u32[]{:S(2)}) copy-start(f32[256]{0:T(256)} %param.17) | copy-start | bytes 3076
  9.3 16.1 %copy-start.4 = (f32[256]{0:T(256)S(1)}, f32[256]{0:T(256)}, u32[]{:S(2)}) copy-start(f32[256]{0:T(256)} %param.19) | copy-start | bytes 3076
  9.4 16.1 %copy-start.5 = (f32[256]{0:T(256)S(1)}, f32[256]{0:T(256)}, u32[]{:S(2)}) copy-start(f32[256]{0:T(256)} %param.21) | copy-start | bytes 3076
  9.4 4.4 %collective-permute-start.2 = (f32[136,128]{1,0:T(8,128)S(1)}, f32[136,128]{1,0:T(8,128)S(1)}, u32[]{:S(2)}, u32[]{:S(2)}) collective-permute-start(f32[136,128]{1,0:T(8,128)S(1)} %get-tuple-element.31), channel_id=1, source_target_pairs={{0,2},{1,3},{2,0},{3,1},{4,6},{5,7},{6,4},{7,5},{8,10},{9,11},{10,... | collective-permute-start | bytes 208904 | tf_op jit(solution)/shard_map/ppermute | solution.py:421
  10.8 4.7 %collective-permute-start.3 = (f32[136,128]{1,0:T(8,128)S(1)}, f32[136,128]{1,0:T(8,128)S(1)}, u32[]{:S(2)}, u32[]{:S(2)}) collective-permute-start(f32[136,128]{1,0:T(8,128)S(1)} %get-tuple-element.31), channel_id=1, source_target_pairs={{0,4},{1,5},{2,6},{3,7},{4,0},{5,1},{6,2},{7,3},{8,12},{9,13},{10,... | collective-permute-start | bytes 208904 | tf_op jit(solution)/shard_map/ppermute | solution.py:421
  12.3 5.2 %collective-permute-start.4 = (f32[136,128]{1,0:T(8,128)S(1)}, f32[136,128]{1,0:T(8,128)S(1)}, u32[]{:S(2)}, u32[]{:S(2)}) collective-permute-start(f32[136,128]{1,0:T(8,128)S(1)} %get-tuple-element.31), channel_id=1, source_target_pairs={{0,6},{1,7},{2,4},{3,5},{4,2},{5,3},{6,0},{7,1},{8,14},{9,15},{10,... | collective-permute-start | bytes 208904 | tf_op jit(solution)/shard_map/ppermute | solution.py:421
  17.6 6.0 %collective-permute-start.5 = (f32[136,128]{1,0:T(8,128)S(1)}, f32[136,128]{1,0:T(8,128)S(1)}, u32[]{:S(2)}, u32[]{:S(2)}) collective-permute-start(f32[136,128]{1,0:T(8,128)S(1)} %add_add_fusion), channel_id=1, source_target_pairs={{0,8},{1,9},{2,10},{3,11},{4,12},{5,13},{6,14},{7,15},{8,0},{9,1},... | collective-permute-start | bytes 208904 | tf_op jit(solution)/shard_map/ppermute | solution.py:421
  24.2 1.2 %collective-permute-start.6 = (f32[16,128]{1,0:T(8,128)S(1)}, f32[16,128]{1,0:T(8,128)S(1)}, u32[]{:S(2)}, u32[]{:S(2)}) collective-permute-start(f32[16,128]{1,0:T(8,128)S(1)} %get-tuple-element.32.mine_ref), channel_id=1, source_target_pairs={{0,1},{1,0},{2,3},{3,2},{4,5},{5,4},{6,7},{7,6},{8,9},{9,8},{10,11... | collective-permute-start | bytes 24584 | tf_op jit(solution)/shard_map/ppermute | solution.py:421

commit v10 on v8

--- a/solution.py
+++ b/solution.py
@@ -62,11 +62,14 @@
 
 def cyclic_pairs(x_re, x_im):
     pairs = [x_re * x_re + x_im * x_im]
-    for shift in range(1, MICS // 2 + 1):
+    for shift in range(1, MICS // 2):
         y_re = pltpu.roll(x_re, MICS - shift, 0)
         y_im = pltpu.roll(x_im, MICS - shift, 0)
         pairs.append(x_re * y_re + x_im * y_im)
         pairs.append(x_im * y_re - x_re * y_im)
+    low = lax.broadcasted_iota(jnp.int32, x_re.shape, 0) < MICS // 2
+    y_re, y_im = pltpu.roll(x_re, MICS // 2, 0), pltpu.roll(x_im, MICS // 2, 0)
+    pairs.append(jnp.where(low, x_re, x_im) * y_re + jnp.where(low, x_im, -x_re) * y_im)
     return pairs
 
 
@@ -77,15 +80,6 @@
         w = jnp.broadcast_to(weights[k], (MICS, LANES))
         out.extend(sums[k * len(pairs) + i] + w * pair for i, pair in enumerate(pairs))
     return tuple(out)
-
-
-def kept_sums(sums):
-    low = lax.broadcasted_iota(jnp.int32, (MICS, LANES), 0) < MICS // 2
-    kept = []
-    for k in range(2):
-        own = sums[9 * k : 9 * k + 9]
-        kept.extend(list(own[:7]) + [jnp.where(low, own[7], own[8])])
-    return jnp.concatenate(kept, axis=0)
 
 
 def slot_tiles(position):
@@ -143,7 +137,7 @@
         for pair in cyclic_pairs(x_re, x_im):
             total = jnp.sum(pair * weight, axis=1, keepdims=True)
             sums.append(jnp.where(lane[:MICS] == 0, total, 0.0))
-    return kept_sums(sums)
+    return jnp.concatenate(sums, axis=0)
 
 
 def stats_kernel(frames, framed_ref, masks_ref, table_ref, conv2_w_hbm, valid_ref, spec_ref, kept_ref, edge_weight_ref, conv2_w_ref, weight_ref, sem):
@@ -176,7 +170,7 @@
             return sums
 
         zero = jnp.zeros((MICS, LANES), jnp.float32)
-        kept_ref[slot] = kept_sums(lax.fori_loop(0, frames // MICS, add_frames, (zero,) * 18))
+        kept_ref[slot] = jnp.concatenate(lax.fori_loop(0, frames // MICS, add_frames, (zero,) * 2 * MICS, unroll=2), axis=0)
     kept_ref[2] = last_bin_sums(frames, spec_ref, weight_ref)
     for copy in copies:
         copy.wait()
@@ -205,13 +199,13 @@
     for tile in range(2 * TILES):
         spec_ref[tile] = spec[:, tile * LANES : (tile + 1) * LANES]
     for slot, tile in enumerate(slot_tiles(position)):
-        sums = (jnp.zeros((MICS, LANES), jnp.float32),) * 18
+        sums = (jnp.zeros((MICS, LANES), jnp.float32),) * 2 * MICS
         for i in range(HALO):
             rows = slice((2 * i + 1) * MICS, (2 * i + 2) * MICS)
             at = MICS - HALO + i
             weights = [edge_weight_ref[tile, k, at : at + 1, :] for k in range(2)]
             sums = add_frame(sums, spec_ref[tile, rows, :], spec_ref[TILES + tile, rows, :], weights)
-        total = kept_ref[slot] + kept_sums(sums)
+        total = kept_ref[slot] + jnp.concatenate(sums, axis=0)
         if slot == 0:
             mine_ref[:STATS, :] = total
         elif slot == 1:

time: 28 us -> 27.9 us (level)
  transfers between devices with their start and end apart: 8 -> 8, of which waited for: 6 -> 6; matrix products, arithmetic and copies ran while one was open for 0% -> 0% of each run, Pallas kernels for 10% -> 9%
where the time goes in v10:
time: 27.9 us; the launch traced here: 27.7 us
  starting transfers between devices  9.58 us (34%)
  waiting for transfers between devices  9.11 us (33%)
  Pallas kernels  7.53 us (27%)
  between operations  1.43 us (5%)
    ppermute x6, waiting for transfers between devices, flipped(): return lax.ppermute(block, axis, [(i, i ^ step) for i in range(size)])  9.11 us
    ppermute x6, starting transfers between devices, flipped(): return lax.ppermute(block, axis, [(i, i ^ step) for i in range(size)])  6.49 us
    ppermute x2, starting transfers between devices, paired(): lax.ppermute(block, ('meet', 'tm'), pairs + [(j, i) for i, j in pairs])  3.08 us
    pallas_call x1, Pallas kernels, per_device(): pl.pallas_call(functools.partial(stem_kernel, frames), out_shape=jax.Shap...  2.69 us
    pallas_call x1, Pallas kernels, per_device(): pl.pallas_call(functools.partial(stats_kernel, frames), out_shape=(jax.Sh...  2.08 us
    pallas_call x1, Pallas kernels, per_device(): pl.pallas_call(functools.partial(rims_kernel, frames), out_shape=(rim, ri...  1.27 us
    pallas_call x1, Pallas kernels, per_device(): pl.pallas_call(solve_kernel, out_shape=(beam, beam), in_specs=[vmem, smem...  0.59 us
  transfers between devices with their start and end apart: 8, of which 6 were waited for; matrix products, arithmetic and copies ran while one was open for 0% of the time, Pallas kernels for 9%

profile of v10, /device:TPU:0, one launch (start us, length us, event | category | flops | bytes accessed | tf_op | source)
XLA Modules:
  0.0 27.7 jit_solution(15624598477895946674)
XLA Ops:
  0.0 1.3 %rims.1 = (bf16[8,512]{1,0:T(8,128)(2,1)S(1)}, bf16[8,512]{1,0:T(8,128)(2,1)S(1)}, bf16[512,512]{1,0:T(8,128)(2,1)S(1)}, s32[2,64,257]{2,1,0:T(8,128)S(1)}, bf16[512,768]{1,0:T(8,128)(2,1)S(1)}) custom-call(bf16[8,10240]{1,0:T(8,128)(2,1)} %wave_hbm.1, s32[2,64,257]{2,1,0:T(8,128)} %masks_hbm.1, bf16[512,768]{1,0:T(8,128)(2,1)} %constant.8.table_hbm), custom_call_target="tpu_custom_call" | custom-call | tf_op jit(solution)/shard_map/rims/pallas_call | solution.py:418
  1.3 0.5 %collective-permute-start = (bf16[8,512]{1,0:T(8,128)(2,1)S(1)}, bf16[8,512]{1,0:T(8,128)(2,1)S(1)}, u32[]{:S(2)}, u32[]{:S(2)}) collective-permute-start(bf16[8,512]{1,0:T(8,128)(2,1)S(1)} %get-tuple-element.19.own0_ref), channel_id=1, source_target_pairs={{0,1},{2,3},{4,5},{6,7},{8,9},{10,11},{12,13},{14,15},{16,17},{18,... | collective-permute-start | bytes 24584 | tf_op jit(solution)/shard_map/ppermute | solution.py:403
  1.8 2.6 %collective-permute-start.1 = (bf16[8,512]{1,0:T(8,128)(2,1)S(1)}, bf16[8,512]{1,0:T(8,128)(2,1)S(1)}, u32[]{:S(2)}, u32[]{:S(2)}) collective-permute-start(bf16[8,512]{1,0:T(8,128)(2,1)S(1)} %get-tuple-element.20.own1_ref), channel_id=1, source_target_pairs={{1,2},{3,4},{5,6},{7,8},{9,10},{11,12},{13,14},{0,16},{15,31},{17,... | collective-permute-start | bytes 24584 | tf_op jit(solution)/shard_map/ppermute | solution.py:403
  5.0 2.1 %stats.1 = (f32[6,512,128]{2,1,0:T(8,128)S(1)}, f32[3,128,128]{2,1,0:T(8,128)S(1)}, f32[3,2,8,128]{3,2,1,0:T(8,128)S(1)}, bf16[2304,256]{1,0:T(8,128)(2,1)S(1)}) custom-call(bf16[512,512]{1,0:T(8,128)(2,1)S(1)} %get-tuple-element.22.framed_ref, s32[2,64,257]{2,1,0:T(8,128)S(1)} %get-tuple-element.23.masks_ref, ...), custom_call_target="tpu_custom_call" | custom-call | tf_op jit(solution)/shard_map/stats/pallas_call | solution.py:431
  7.1 0.0 copy-start.1
  7.1 0.0 collective-permute-done.got0_ref
  7.1 0.0 collective-permute-done.1.got1_ref
  7.1 0.4 %edges.1 = (f32[6,64,128]{2,1,0:T(8,128)S(1)}, f32[136,128]{1,0:T(8,128)S(1)}, f32[136,128]{1,0:T(8,128)S(1)}) custom-call(bf16[8,512]{1,0:T(8,128)(2,1)S(1)} %get-tuple-element.19.own0_ref, bf16[8,512]{1,0:T(8,128)(2,1)S(1)} %get-tuple-element.20.own1_ref, bf16[8,512]{1,0:T(8,128)(2,1)S(1)} %collective-permute-done.got0_ref, ...), custom_call_target="tpu_custom_call" | custom-call | tf_op jit(solution)/shard_map/edges/pallas_call | solution.py:448
  7.6 0.0 copy-start
  7.6 0.0 copy-start.4
  7.6 0.0 copy-start.5
  7.6 0.2 collective-permute-start.2
  7.8 1.1 %collective-permute-done.2 = f32[136,128]{1,0:T(8,128)S(1)} collective-permute-done((f32[136,128]{1,0:T(8,128)S(1)}, f32[136,128]{1,0:T(8,128)S(1)}, u32[]{:S(2)}, u32[]{:S(2)}) %collective-permute-start.2) | collective-permute-done | bytes 69664 | tf_op jit(solution)/shard_map/ppermute | solution.py:378
  8.9 1.4 %collective-permute-start.3 = (f32[136,128]{1,0:T(8,128)S(1)}, f32[136,128]{1,0:T(8,128)S(1)}, u32[]{:S(2)}, u32[]{:S(2)}) collective-permute-start(f32[136,128]{1,0:T(8,128)S(1)} %add.15), channel_id=1, source_target_pairs={{0,2},{1,3},{2,0},{3,1},{4,6},{5,7},{6,4},{7,5},{8,10},{9,11},{10,... | collective-permute-start | bytes 208904 | tf_op jit(solution)/shard_map/ppermute | solution.py:378
  10.3 1.6 %collective-permute-start.4 = (f32[136,128]{1,0:T(8,128)S(1)}, f32[136,128]{1,0:T(8,128)S(1)}, u32[]{:S(2)}, u32[]{:S(2)}) collective-permute-start(f32[136,128]{1,0:T(8,128)S(1)} %add.15), channel_id=1, source_target_pairs={{0,4},{1,5},{2,6},{3,7},{4,0},{5,1},{6,2},{7,3},{8,12},{9,13},{10,... | collective-permute-start | bytes 208904 | tf_op jit(solution)/shard_map/ppermute | solution.py:378
  11.9 0.6 %collective-permute-start.5 = (f32[136,128]{1,0:T(8,128)S(1)}, f32[136,128]{1,0:T(8,128)S(1)}, u32[]{:S(2)}, u32[]{:S(2)}) collective-permute-start(f32[136,128]{1,0:T(8,128)S(1)} %add.15), channel_id=1, source_target_pairs={{0,6},{1,7},{2,4},{3,5},{4,2},{5,3},{6,0},{7,1},{8,14},{9,15},{10,... | collective-permute-start | bytes 208904 | tf_op jit(solution)/shard_map/ppermute | solution.py:378
  12.5 0.8 %collective-permute-done.3 = f32[136,128]{1,0:T(8,128)S(1)} collective-permute-done((f32[136,128]{1,0:T(8,128)S(1)}, f32[136,128]{1,0:T(8,128)S(1)}, u32[]{:S(2)}, u32[]{:S(2)}) %collective-permute-start.3) | collective-permute-done | bytes 69664 | tf_op jit(solution)/shard_map/ppermute | solution.py:378
  13.3 1.7 %collective-permute-done.4 = f32[136,128]{1,0:T(8,128)S(1)} collective-permute-done((f32[136,128]{1,0:T(8,128)S(1)}, f32[136,128]{1,0:T(8,128)S(1)}, u32[]{:S(2)}, u32[]{:S(2)}) %collective-permute-start.4) | collective-permute-done | bytes 69664 | tf_op jit(solution)/shard_map/ppermute | solution.py:378
  15.0 2.1 %collective-permute-done.5 = f32[136,128]{1,0:T(8,128)S(1)} collective-permute-done((f32[136,128]{1,0:T(8,128)S(1)}, f32[136,128]{1,0:T(8,128)S(1)}, u32[]{:S(2)}, u32[]{:S(2)}) %collective-permute-start.5) | collective-permute-done | bytes 69664 | tf_op jit(solution)/shard_map/ppermute | solution.py:378
  17.1 2.7 %collective-permute-start.6 = (f32[136,128]{1,0:T(8,128)S(1)}, f32[136,128]{1,0:T(8,128)S(1)}, u32[]{:S(2)}, u32[]{:S(2)}) collective-permute-start(f32[136,128]{1,0:T(8,128)S(1)} %add_add_fusion), channel_id=1, source_target_pairs={{0,8},{1,9},{2,10},{3,11},{4,12},{5,13},{6,14},{7,15},{8,0},{9,1},... | collective-permute-start | bytes 208904 | tf_op jit(solution)/shard_map/ppermute | solution.py:378
  20.4 2.7 %collective-permute-done.6 = f32[136,128]{1,0:T(8,128)S(1)} collective-permute-done((f32[136,128]{1,0:T(8,128)S(1)}, f32[136,128]{1,0:T(8,128)S(1)}, u32[]{:S(2)}, u32[]{:S(2)}) %collective-permute-start.6) | collective-permute-done | bytes 69664 | tf_op jit(solution)/shard_map/ppermute | solution.py:378
  23.2 0.6 %solve.1 = (f32[16,128]{1,0:T(8,128)S(1)}, f32[16,128]{1,0:T(8,128)S(1)}) custom-call(f32[136,128]{1,0:T(8,128)S(1)} %add.19.stats_ref, s32[1]{0:T(128)S(6)} %copy.14.ref_mic_ref), custom_call_target="tpu_custom_call" | custom-call | tf_op jit(solution)/shard_map/solve/pallas_call | solution.py:459
  23.8 0.1 collective-permute-start.7
  23.8 0.0 copy-done.1
  23.8 0.5 %power.1.mel_ref = f32[72,256]{1,0:T(8,128)S(1)} custom-call(f32[16,128]{1,0:T(8,128)S(1)} %get-tuple-element.28.mine_ref, f32[16,128]{1,0:T(8,128)S(1)} %get-tuple-element.29.last_ref, f32[6,512,128]{2,1,0:T(8,128)S(1)} %get-tuple-element.30.spec_ref, f32[6,64,128]{2,1,0:T(8,128)S(1)} %get-tuple-element.31.edge_spec_ref, f32[3,128,256]{2,1,0:T(8,128)S(1)} %copy-done.1), custom_call_target="tpu_custom_call" | custom-call | tf_op jit(solution)/shard_map/power/pallas_call | solution.py:470
  24.3 0.7 %collective-permute-done.7.theirs_ref = f32[16,128]{1,0:T(8,128)S(1)} collective-permute-done((f32[16,128]{1,0:T(8,128)S(1)}, f32[16,128]{1,0:T(8,128)S(1)}, u32[]{:S(2)}, u32[]{:S(2)}) %collective-permute-start.7) | collective-permute-done | bytes 8224 | tf_op jit(solution)/shard_map/ppermute | solution.py:378
  25.0 0.0 copy-done
  25.0 0.0 copy-done.2
  25.0 0.0 copy-done.3
  25.0 0.0 copy-done.4
  25.0 0.0 copy-done.5
  25.0 2.7 %stem.1 = bf16[1,16,256]{2,1,0:T(8,128)(2,1)} custom-call(f32[16,128]{1,0:T(8,128)S(1)} %collective-permute-done.7.theirs_ref, f32[72,256]{1,0:T(8,128)S(1)} %power.1.mel_ref, f32[6,512,128]{2,1,0:T(8,128)S(1)} %get-tuple-element.30.spec_ref, f32[6,64,128]{2,1,0:T(8,128)S(1)} %get-tuple-element.31.edge_spec_ref, s32[1]{0:T(128)S(6)} %copy.13.valid_ref, ...), custom_call_target="tpu_custom_call" | custom-call | tf_op jit(solution)/shard_map/stem/pallas_call | solution.py:478
  (5 shorter events, 0.0 us)
Async XLA Ops:
  1.3 5.8 %collective-permute-start = (bf16[8,512]{1,0:T(8,128)(2,1)S(1)}, bf16[8,512]{1,0:T(8,128)(2,1)S(1)}, u32[]{:S(2)}, u32[]{:S(2)}) collective-permute-start(bf16[8,512]{1,0:T(8,128)(2,1)S(1)} %get-tuple-element.19.own0_ref), channel_id=1, source_target_pairs={{0,1},{2,3},{4,5},{6,7},{8,9},{10,11},{12,13},{14,15},{16,17},{18,... | collective-permute-start | bytes 24584 | tf_op jit(solution)/shard_map/ppermute | solution.py:403
  1.8 5.3 %collective-permute-start.1 = (bf16[8,512]{1,0:T(8,128)(2,1)S(1)}, bf16[8,512]{1,0:T(8,128)(2,1)S(1)}, u32[]{:S(2)}, u32[]{:S(2)}) collective-permute-start(bf16[8,512]{1,0:T(8,128)(2,1)S(1)} %get-tuple-element.20.own1_ref), channel_id=1, source_target_pairs={{1,2},{3,4},{5,6},{7,8},{9,10},{11,12},{13,14},{0,16},{15,31},{17,... | collective-permute-start | bytes 24584 | tf_op jit(solution)/shard_map/ppermute | solution.py:403
  7.1 16.7 %copy-start.1 = (f32[3,128,256]{2,1,0:T(8,128)S(1)}, f32[3,128,256]{2,1,0:T(8,128)}, u32[]{:S(2)}) copy-start(f32[3,128,256]{2,1,0:T(8,128)} %constant.5.clone.bank_ref) | copy-start | bytes 1179652
  7.6 17.4 %copy-start = (bf16[4864,256]{1,0:T(8,128)(2,1)S(1)}, bf16[4864,256]{1,0:T(8,128)(2,1)}, u32[]{:S(2)}) copy-start(bf16[4864,256]{1,0:T(8,128)(2,1)} %proj_w_ref.1) | copy-start | bytes 7471108
  7.6 17.4 %copy-start.2 = (bf16[9,256]{1,0:T(8,128)(2,1)S(1)}, bf16[9,256]{1,0:T(8,128)(2,1)}, u32[]{:S(2)}) copy-start(bf16[9,256]{1,0:T(8,128)(2,1)} %conv1_w_ref.1) | copy-start | bytes 13828
  7.6 17.4 %copy-start.3 = (f32[256]{0:T(256)S(1)}, f32[256]{0:T(256)}, u32[]{:S(2)}) copy-start(f32[256]{0:T(256)} %param.17) | copy-start | bytes 3076
  7.6 17.4 %copy-start.4 = (f32[256]{0:T(256)S(1)}, f32[256]{0:T(256)}, u32[]{:S(2)}) copy-start(f32[256]{0:T(256)} %param.19) | copy-start | bytes 3076
  7.6 17.4 %copy-start.5 = (f32[256]{0:T(256)S(1)}, f32[256]{0:T(256)}, u32[]{:S(2)}) copy-start(f32[256]{0:T(256)} %param.21) | copy-start | bytes 3076
  7.6 1.3 %collective-permute-start.2 = (f32[136,128]{1,0:T(8,128)S(1)}, f32[136,128]{1,0:T(8,128)S(1)}, u32[]{:S(2)}, u32[]{:S(2)}) collective-permute-start(f32[136,128]{1,0:T(8,128)S(1)} %get-tuple-element.27), channel_id=1, source_target_pairs={{0,1},{1,0},{2,3},{3,2},{4,5},{5,4},{6,7},{7,6},{8,9},{9,8},{10,11... | collective-permute-start | bytes 208904 | tf_op jit(solution)/shard_map/ppermute | solution.py:378
  8.9 4.4 %collective-permute-start.3 = (f32[136,128]{1,0:T(8,128)S(1)}, f32[136,128]{1,0:T(8,128)S(1)}, u32[]{:S(2)}, u32[]{:S(2)}) collective-permute-start(f32[136,128]{1,0:T(8,128)S(1)} %add.15), channel_id=1, source_target_pairs={{0,2},{1,3},{2,0},{3,1},{4,6},{5,7},{6,4},{7,5},{8,10},{9,11},{10,... | collective-permute-start | bytes 208904 | tf_op jit(solution)/shard_map/ppermute | solution.py:378
  10.3 4.7 %collective-permute-start.4 = (f32[136,128]{1,0:T(8,128)S(1)}, f32[136,128]{1,0:T(8,128)S(1)}, u32[]{:S(2)}, u32[]{:S(2)}) collective-permute-start(f32[136,128]{1,0:T(8,128)S(1)} %add.15), channel_id=1, source_target_pairs={{0,4},{1,5},{2,6},{3,7},{4,0},{5,1},{6,2},{7,3},{8,12},{9,13},{10,... | collective-permute-start | bytes 208904 | tf_op jit(solution)/shard_map/ppermute | solution.py:378
  11.9 5.2 %collective-permute-start.5 = (f32[136,128]{1,0:T(8,128)S(1)}, f32[136,128]{1,0:T(8,128)S(1)}, u32[]{:S(2)}, u32[]{:S(2)}) collective-permute-start(f32[136,128]{1,0:T(8,128)S(1)} %add.15), channel_id=1, source_target_pairs={{0,6},{1,7},{2,4},{3,5},{4,2},{5,3},{6,0},{7,1},{8,14},{9,15},{10,... | collective-permute-start | bytes 208904 | tf_op jit(solution)/shard_map/ppermute | solution.py:378
  17.1 6.0 %collective-permute-start.6 = (f32[136,128]{1,0:T(8,128)S(1)}, f32[136,128]{1,0:T(8,128)S(1)}, u32[]{:S(2)}, u32[]{:S(2)}) collective-permute-start(f32[136,128]{1,0:T(8,128)S(1)} %add_add_fusion), channel_id=1, source_target_pairs={{0,8},{1,9},{2,10},{3,11},{4,12},{5,13},{6,14},{7,15},{8,0},{9,1},... | collective-permute-start | bytes 208904 | tf_op jit(solution)/shard_map/ppermute | solution.py:378
  23.8 1.2 %collective-permute-start.7 = (f32[16,128]{1,0:T(8,128)S(1)}, f32[16,128]{1,0:T(8,128)S(1)}, u32[]{:S(2)}, u32[]{:S(2)}) collective-permute-start(f32[16,128]{1,0:T(8,128)S(1)} %get-tuple-element.28.mine_ref), channel_id=1, source_target_pairs={{0,1},{1,0},{2,3},{3,2},{4,5},{5,4},{6,7},{7,6},{8,9},{9,8},{10,11... | collective-permute-start | bytes 24584 | tf_op jit(solution)/shard_map/ppermute | solution.py:378

commit v11 on v10

--- a/solution.py
+++ b/solution.py
@@ -306,23 +306,21 @@
     return jnp.dot(power, bank, precision=lax.Precision.HIGHEST, preferred_element_type=jnp.float32)
 
 
-def power_kernel(mine_ref, last_ref, spec_ref, edge_spec_ref, bank_ref, mel_ref):
+def power_kernel(mine_ref, last_ref, spec_ref, edge_spec_ref, bank_ref, conv1_w_ref, mel_ref, taps_ref, padded_ref):
+    padded_ref[...] = jnp.zeros(padded_ref.shape, jnp.float32)
+    for shift_t in range(3):
+        padded_ref[SPAN * shift_t : SPAN * shift_t + 3, :] = conv1_w_ref[3 * shift_t : 3 * shift_t + 3, :].astype(jnp.float32)
+    taps_ref[...] = padded_ref[...].astype(taps_ref.dtype)
     mine, _, last = slot_tiles(lax.axis_index("tm"))
     power = [power_of(beam_ref, tile, spec_ref, edge_spec_ref) for beam_ref, tile in ((mine_ref, mine), (last_ref, last))]
     bank = jnp.concatenate([bank_ref[mine], bank_ref[last]], axis=0)
     mel_ref[...] = mel_of(jnp.concatenate(power, axis=1), bank)
 
 
-def stem_kernel(frames, theirs_ref, mel_ref, spec_ref, edge_spec_ref, valid_ref, bank_ref, conv1_w_ref, conv1_b_ref, conv2_w_ref, conv2_b_ref, proj_w_ref, proj_b_ref, out_ref, logmel_ref, conv1_ref):
+def stem_kernel(frames, theirs_ref, mel_ref, spec_ref, edge_spec_ref, valid_ref, bank_ref, taps_ref, conv1_b_ref, conv2_w_ref, conv2_b_ref, proj_w_ref, proj_b_ref, out_ref, logmel_ref):
     position = lax.axis_index("tm")
     valid = valid_ref[0]
     quarter = frames // 4
-    channels = conv1_w_ref.shape[1]
-    conv1_ref[...] = jnp.zeros((LANES, channels), jnp.float32)
-    for shift_t in range(3):
-        conv1_ref[SPAN * shift_t : SPAN * shift_t + 3, :] = conv1_w_ref[3 * shift_t : 3 * shift_t + 3, :].astype(jnp.float32)
-    conv1 = conv1_ref[...].astype(jnp.bfloat16)
-
     theirs = slot_tiles(position)[1]
     mel = mel_ref[...] + mel_of(power_of(theirs_ref, theirs, spec_ref, edge_spec_ref), bank_ref[theirs])
     row = lax.broadcasted_iota(jnp.int32, (frames + MICS, 1), 0)
@@ -355,7 +353,7 @@
             half, shift = (0, 2 * q) if q < 20 else (1, 2 * q - 40)
             patches.append(packs[half] if shift == 0 else pltpu.roll(packs[half], LANES - shift, 1))
         patches = jnp.concatenate(patches, axis=0).astype(jnp.bfloat16)
-        layer = jnp.dot(patches, conv1, preferred_element_type=jnp.float32) + conv1_b_ref[...]
+        layer = jnp.dot(patches, taps_ref[...], preferred_element_type=jnp.float32) + conv1_b_ref[...]
         layer = jnp.maximum(layer, 0.0)
         if tap == 0:
             keep = jnp.concatenate([row + 2 * quarter * position >= 1] * q_first, axis=0)
@@ -467,20 +465,24 @@
     beam_theirs = flipped(beam_mine, "tm", 1)
     rows = frames + MICS
     bank = packed_mel_bank()
-    mel = pl.pallas_call(
+    mel, taps = pl.pallas_call(
         power_kernel,
-        out_shape=jax.ShapeDtypeStruct((rows, 2 * LANES), jnp.float32),
-        in_specs=[vmem] * 5,
-        out_specs=vmem,
+        out_shape=(
+            jax.ShapeDtypeStruct((rows, 2 * LANES), jnp.float32),
+            jax.ShapeDtypeStruct((LANES, channels), conv1_w.dtype),
+        ),
+        in_specs=[vmem] * 6,
+        out_specs=(vmem,) * 2,
+        scratch_shapes=[pltpu.VMEM((LANES, channels), jnp.float32)],
         compiler_params=params,
         name="power",
-    )(beam_mine, beam_last, spec, edge_spec, bank)
+    )(beam_mine, beam_last, spec, edge_spec, bank, conv1_w)
     return pl.pallas_call(
         functools.partial(stem_kernel, frames),
         out_shape=jax.ShapeDtypeStruct((1, frames // 4, width), jnp.bfloat16),
         in_specs=[vmem] * 4 + [smem] + [vmem] * 7,
         out_specs=vmem,
-        scratch_shapes=[pltpu.VMEM((2, rows, LANES), jnp.float32), pltpu.VMEM((LANES, channels), jnp.float32)],
+        scratch_shapes=[pltpu.VMEM((2, rows, LANES), jnp.float32)],
         compiler_params=params,
         name="stem",
     )(
@@ -490,7 +492,7 @@
         edge_spec,
         valid,
         bank,
-        conv1_w,
+        taps,
         conv1_b[None],
         conv2_w,
         conv2_b[None],

time: 27.9 us -> 27.9 us (level)
  no operation moved by 1% of the time
where the time goes in v11:
time: 27.9 us; the launch traced here: 27.7 us
  starting transfers between devices  9.57 us (34%)
  waiting for transfers between devices  9.1 us (33%)
  Pallas kernels  7.53 us (27%)
  between operations  1.43 us (5%)
    ppermute x6, waiting for transfers between devices, flipped(): return lax.ppermute(block, axis, [(i, i ^ step) for i in range(size)])  9.1 us
    ppermute x6, starting transfers between devices, flipped(): return lax.ppermute(block, axis, [(i, i ^ step) for i in range(size)])  6.49 us
    ppermute x2, starting transfers between devices, paired(): lax.ppermute(block, ('meet', 'tm'), pairs + [(j, i) for i, j in pairs])  3.08 us
    pallas_call x1, Pallas kernels, per_device(): pl.pallas_call(functools.partial(stem_kernel, frames), out_shape=jax.Shap...  2.69 us
    pallas_call x1, Pallas kernels, per_device(): pl.pallas_call(functools.partial(stats_kernel, frames), out_shape=(jax.Sh...  2.08 us
    pallas_call x1, Pallas kernels, per_device(): pl.pallas_call(functools.partial(rims_kernel, frames), out_shape=(rim, ri...  1.27 us
    pallas_call x1, Pallas kernels, per_device(): pl.pallas_call(solve_kernel, out_shape=(beam, beam), in_specs=[vmem, smem...  0.59 us
  transfers between devices with their start and end apart: 8, of which 6 were waited for; matrix products, arithmetic and copies ran while one was open for 0% of the time, Pallas kernels for 9%

profile of v11, /device:TPU:0, one launch (start us, length us, event | category | flops | bytes accessed | tf_op | source)
XLA Modules:
  0.0 27.7 jit_solution(16289933389530417941)
XLA Ops:
  0.0 1.3 %rims.1 = (bf16[8,512]{1,0:T(8,128)(2,1)S(1)}, bf16[8,512]{1,0:T(8,128)(2,1)S(1)}, bf16[512,512]{1,0:T(8,128)(2,1)S(1)}, s32[2,64,257]{2,1,0:T(8,128)S(1)}, bf16[512,768]{1,0:T(8,128)(2,1)S(1)}) custom-call(bf16[8,10240]{1,0:T(8,128)(2,1)} %wave_hbm.1, s32[2,64,257]{2,1,0:T(8,128)} %masks_hbm.1, bf16[512,768]{1,0:T(8,128)(2,1)} %constant.8.table_hbm), custom_call_target="tpu_custom_call" | custom-call | tf_op jit(solution)/shard_map/rims/pallas_call | solution.py:416
  1.3 0.5 %collective-permute-start = (bf16[8,512]{1,0:T(8,128)(2,1)S(1)}, bf16[8,512]{1,0:T(8,128)(2,1)S(1)}, u32[]{:S(2)}, u32[]{:S(2)}) collective-permute-start(bf16[8,512]{1,0:T(8,128)(2,1)S(1)} %get-tuple-element.21.own0_ref), channel_id=1, source_target_pairs={{0,1},{2,3},{4,5},{6,7},{8,9},{10,11},{12,13},{14,15},{16,17},{18,... | collective-permute-start | bytes 24584 | tf_op jit(solution)/shard_map/ppermute | solution.py:401
  1.8 2.6 %collective-permute-start.1 = (bf16[8,512]{1,0:T(8,128)(2,1)S(1)}, bf16[8,512]{1,0:T(8,128)(2,1)S(1)}, u32[]{:S(2)}, u32[]{:S(2)}) collective-permute-start(bf16[8,512]{1,0:T(8,128)(2,1)S(1)} %get-tuple-element.22.own1_ref), channel_id=1, source_target_pairs={{1,2},{3,4},{5,6},{7,8},{9,10},{11,12},{13,14},{0,16},{15,31},{17,... | collective-permute-start | bytes 24584 | tf_op jit(solution)/shard_map/ppermute | solution.py:401
  5.0 2.1 %stats.1 = (f32[6,512,128]{2,1,0:T(8,128)S(1)}, f32[3,128,128]{2,1,0:T(8,128)S(1)}, f32[3,2,8,128]{3,2,1,0:T(8,128)S(1)}, bf16[2304,256]{1,0:T(8,128)(2,1)S(1)}) custom-call(bf16[512,512]{1,0:T(8,128)(2,1)S(1)} %get-tuple-element.24.framed_ref, s32[2,64,257]{2,1,0:T(8,128)S(1)} %get-tuple-element.25.masks_ref, ...), custom_call_target="tpu_custom_call" | custom-call | tf_op jit(solution)/shard_map/stats/pallas_call | solution.py:429
  7.1 0.0 copy-start.1
  7.1 0.0 copy-start.2
  7.1 0.0 collective-permute-done.got0_ref
  7.1 0.0 collective-permute-done.1.got1_ref
  7.1 0.4 %edges.1 = (f32[6,64,128]{2,1,0:T(8,128)S(1)}, f32[136,128]{1,0:T(8,128)S(1)}, f32[136,128]{1,0:T(8,128)S(1)}) custom-call(bf16[8,512]{1,0:T(8,128)(2,1)S(1)} %get-tuple-element.21.own0_ref, bf16[8,512]{1,0:T(8,128)(2,1)S(1)} %get-tuple-element.22.own1_ref, bf16[8,512]{1,0:T(8,128)(2,1)S(1)} %collective-permute-done.got0_ref, ...), custom_call_target="tpu_custom_call" | custom-call | tf_op jit(solution)/shard_map/edges/pallas_call | solution.py:446
  7.6 0.0 copy-start
  7.6 0.0 copy-start.5
  7.6 0.2 collective-permute-start.2
  7.8 1.1 %collective-permute-done.2 = f32[136,128]{1,0:T(8,128)S(1)} collective-permute-done((f32[136,128]{1,0:T(8,128)S(1)}, f32[136,128]{1,0:T(8,128)S(1)}, u32[]{:S(2)}, u32[]{:S(2)}) %collective-permute-start.2) | collective-permute-done | bytes 69664 | tf_op jit(solution)/shard_map/ppermute | solution.py:376
  8.9 1.4 %collective-permute-start.3 = (f32[136,128]{1,0:T(8,128)S(1)}, f32[136,128]{1,0:T(8,128)S(1)}, u32[]{:S(2)}, u32[]{:S(2)}) collective-permute-start(f32[136,128]{1,0:T(8,128)S(1)} %add.15), channel_id=1, source_target_pairs={{0,2},{1,3},{2,0},{3,1},{4,6},{5,7},{6,4},{7,5},{8,10},{9,11},{10,... | collective-permute-start | bytes 208904 | tf_op jit(solution)/shard_map/ppermute | solution.py:376
  10.3 1.6 %collective-permute-start.4 = (f32[136,128]{1,0:T(8,128)S(1)}, f32[136,128]{1,0:T(8,128)S(1)}, u32[]{:S(2)}, u32[]{:S(2)}) collective-permute-start(f32[136,128]{1,0:T(8,128)S(1)} %add.15), channel_id=1, source_target_pairs={{0,4},{1,5},{2,6},{3,7},{4,0},{5,1},{6,2},{7,3},{8,12},{9,13},{10,... | collective-permute-start | bytes 208904 | tf_op jit(solution)/shard_map/ppermute | solution.py:376
  11.9 0.6 %collective-permute-start.5 = (f32[136,128]{1,0:T(8,128)S(1)}, f32[136,128]{1,0:T(8,128)S(1)}, u32[]{:S(2)}, u32[]{:S(2)}) collective-permute-start(f32[136,128]{1,0:T(8,128)S(1)} %add.15), channel_id=1, source_target_pairs={{0,6},{1,7},{2,4},{3,5},{4,2},{5,3},{6,0},{7,1},{8,14},{9,15},{10,... | collective-permute-start | bytes 208904 | tf_op jit(solution)/shard_map/ppermute | solution.py:376
  12.5 0.8 %collective-permute-done.3 = f32[136,128]{1,0:T(8,128)S(1)} collective-permute-done((f32[136,128]{1,0:T(8,128)S(1)}, f32[136,128]{1,0:T(8,128)S(1)}, u32[]{:S(2)}, u32[]{:S(2)}) %collective-permute-start.3) | collective-permute-done | bytes 69664 | tf_op jit(solution)/shard_map/ppermute | solution.py:376
  13.3 1.7 %collective-permute-done.4 = f32[136,128]{1,0:T(8,128)S(1)} collective-permute-done((f32[136,128]{1,0:T(8,128)S(1)}, f32[136,128]{1,0:T(8,128)S(1)}, u32[]{:S(2)}, u32[]{:S(2)}) %collective-permute-start.4) | collective-permute-done | bytes 69664 | tf_op jit(solution)/shard_map/ppermute | solution.py:376
  15.0 2.1 %collective-permute-done.5 = f32[136,128]{1,0:T(8,128)S(1)} collective-permute-done((f32[136,128]{1,0:T(8,128)S(1)}, f32[136,128]{1,0:T(8,128)S(1)}, u32[]{:S(2)}, u32[]{:S(2)}) %collective-permute-start.5) | collective-permute-done | bytes 69664 | tf_op jit(solution)/shard_map/ppermute | solution.py:376
  17.1 2.7 %collective-permute-start.6 = (f32[136,128]{1,0:T(8,128)S(1)}, f32[136,128]{1,0:T(8,128)S(1)}, u32[]{:S(2)}, u32[]{:S(2)}) collective-permute-start(f32[136,128]{1,0:T(8,128)S(1)} %add_add_fusion), channel_id=1, source_target_pairs={{0,8},{1,9},{2,10},{3,11},{4,12},{5,13},{6,14},{7,15},{8,0},{9,1},... | collective-permute-start | bytes 208904 | tf_op jit(solution)/shard_map/ppermute | solution.py:376
  20.4 2.7 %collective-permute-done.6 = f32[136,128]{1,0:T(8,128)S(1)} collective-permute-done((f32[136,128]{1,0:T(8,128)S(1)}, f32[136,128]{1,0:T(8,128)S(1)}, u32[]{:S(2)}, u32[]{:S(2)}) %collective-permute-start.6) | collective-permute-done | bytes 69664 | tf_op jit(solution)/shard_map/ppermute | solution.py:376
  23.2 0.6 %solve.1 = (f32[16,128]{1,0:T(8,128)S(1)}, f32[16,128]{1,0:T(8,128)S(1)}) custom-call(f32[136,128]{1,0:T(8,128)S(1)} %add.19.stats_ref, s32[1]{0:T(128)S(6)} %copy.14.ref_mic_ref), custom_call_target="tpu_custom_call" | custom-call | tf_op jit(solution)/shard_map/solve/pallas_call | solution.py:457
  23.8 0.1 collective-permute-start.7
  23.8 0.0 copy-done.1
  23.8 0.0 copy-done.2
  23.9 0.5 %power.1 = (f32[72,256]{1,0:T(8,128)S(1)}, bf16[128,256]{1,0:T(8,128)(2,1)S(1)}) custom-call(f32[16,128]{1,0:T(8,128)S(1)} %get-tuple-element.30.mine_ref, f32[16,128]{1,0:T(8,128)S(1)} %get-tuple-element.31.last_ref, f32[6,512,128]{2,1,0:T(8,128)S(1)} %get-tuple-element.32.spec_ref, f32[6,64,128]{2,1,0:T(8,128)S(1)} %get-tuple-element.33.edge_spec_ref, ...), custom_call_target="tpu_custom_call" | custom-call | tf_op jit(solution)/shard_map/power/pallas_call | solution.py:468
  24.3 0.7 %collective-permute-done.7.theirs_ref = f32[16,128]{1,0:T(8,128)S(1)} collective-permute-done((f32[16,128]{1,0:T(8,128)S(1)}, f32[16,128]{1,0:T(8,128)S(1)}, u32[]{:S(2)}, u32[]{:S(2)}) %collective-permute-start.7) | collective-permute-done | bytes 8224 | tf_op jit(solution)/shard_map/ppermute | solution.py:376
  25.0 0.0 copy-done
  25.0 0.0 copy-done.3
  25.0 0.0 copy-done.4
  25.0 0.0 copy-done.5
  25.0 2.7 %stem.1 = bf16[1,16,256]{2,1,0:T(8,128)(2,1)} custom-call(f32[16,128]{1,0:T(8,128)S(1)} %collective-permute-done.7.theirs_ref, f32[72,256]{1,0:T(8,128)S(1)} %get-tuple-element.34.mel_ref, f32[6,512,128]{2,1,0:T(8,128)S(1)} %get-tuple-element.32.spec_ref, f32[6,64,128]{2,1,0:T(8,128)S(1)} %get-tuple-element.33.edge_spec_ref, s32[1]{0:T(128)S(6)} %copy.13.valid_ref, ...), custom_call_target="tpu_custom_call" | custom-call | tf_op jit(solution)/shard_map/stem/pallas_call | solution.py:480
  (5 shorter events, 0.0 us)
Async XLA Ops:
  1.3 5.8 %collective-permute-start = (bf16[8,512]{1,0:T(8,128)(2,1)S(1)}, bf16[8,512]{1,0:T(8,128)(2,1)S(1)}, u32[]{:S(2)}, u32[]{:S(2)}) collective-permute-start(bf16[8,512]{1,0:T(8,128)(2,1)S(1)} %get-tuple-element.21.own0_ref), channel_id=1, source_target_pairs={{0,1},{2,3},{4,5},{6,7},{8,9},{10,11},{12,13},{14,15},{16,17},{18,... | collective-permute-start | bytes 24584 | tf_op jit(solution)/shard_map/ppermute | solution.py:401
  1.8 5.3 %collective-permute-start.1 = (bf16[8,512]{1,0:T(8,128)(2,1)S(1)}, bf16[8,512]{1,0:T(8,128)(2,1)S(1)}, u32[]{:S(2)}, u32[]{:S(2)}) collective-permute-start(bf16[8,512]{1,0:T(8,128)(2,1)S(1)} %get-tuple-element.22.own1_ref), channel_id=1, source_target_pairs={{1,2},{3,4},{5,6},{7,8},{9,10},{11,12},{13,14},{0,16},{15,31},{17,... | collective-permute-start | bytes 24584 | tf_op jit(solution)/shard_map/ppermute | solution.py:401
  7.1 16.7 %copy-start.1 = (f32[3,128,256]{2,1,0:T(8,128)S(1)}, f32[3,128,256]{2,1,0:T(8,128)}, u32[]{:S(2)}) copy-start(f32[3,128,256]{2,1,0:T(8,128)} %constant.5.clone.bank_ref) | copy-start | bytes 1179652
  7.1 16.7 %copy-start.2 = (bf16[9,256]{1,0:T(8,128)(2,1)S(1)}, bf16[9,256]{1,0:T(8,128)(2,1)}, u32[]{:S(2)}) copy-start(bf16[9,256]{1,0:T(8,128)(2,1)} %conv1_w_ref.1) | copy-start | bytes 13828
  7.6 17.4 %copy-start = (bf16[4864,256]{1,0:T(8,128)(2,1)S(1)}, bf16[4864,256]{1,0:T(8,128)(2,1)}, u32[]{:S(2)}) copy-start(bf16[4864,256]{1,0:T(8,128)(2,1)} %proj_w_ref.1) | copy-start | bytes 7471108
  7.6 17.4 %copy-start.3 = (f32[256]{0:T(256)S(1)}, f32[256]{0:T(256)}, u32[]{:S(2)}) copy-start(f32[256]{0:T(256)} %param.17) | copy-start | bytes 3076
  7.6 17.4 %copy-start.4 = (f32[256]{0:T(256)S(1)}, f32[256]{0:T(256)}, u32[]{:S(2)}) copy-start(f32[256]{0:T(256)} %param.19) | copy-start | bytes 3076
  7.6 17.4 %copy-start.5 = (f32[256]{0:T(256)S(1)}, f32[256]{0:T(256)}, u32[]{:S(2)}) copy-start(f32[256]{0:T(256)} %param.21) | copy-start | bytes 3076
  7.6 1.3 %collective-permute-start.2 = (f32[136,128]{1,0:T(8,128)S(1)}, f32[136,128]{1,0:T(8,128)S(1)}, u32[]{:S(2)}, u32[]{:S(2)}) collective-permute-start(f32[136,128]{1,0:T(8,128)S(1)} %get-tuple-element.29), channel_id=1, source_target_pairs={{0,1},{1,0},{2,3},{3,2},{4,5},{5,4},{6,7},{7,6},{8,9},{9,8},{10,11... | collective-permute-start | bytes 208904 | tf_op jit(solution)/shard_map/ppermute | solution.py:376
  8.9 4.4 %collective-permute-start.3 = (f32[136,128]{1,0:T(8,128)S(1)}, f32[136,128]{1,0:T(8,128)S(1)}, u32[]{:S(2)}, u32[]{:S(2)}) collective-permute-start(f32[136,128]{1,0:T(8,128)S(1)} %add.15), channel_id=1, source_target_pairs={{0,2},{1,3},{2,0},{3,1},{4,6},{5,7},{6,4},{7,5},{8,10},{9,11},{10,... | collective-permute-start | bytes 208904 | tf_op jit(solution)/shard_map/ppermute | solution.py:376
  10.3 4.7 %collective-permute-start.4 = (f32[136,128]{1,0:T(8,128)S(1)}, f32[136,128]{1,0:T(8,128)S(1)}, u32[]{:S(2)}, u32[]{:S(2)}) collective-permute-start(f32[136,128]{1,0:T(8,128)S(1)} %add.15), channel_id=1, source_target_pairs={{0,4},{1,5},{2,6},{3,7},{4,0},{5,1},{6,2},{7,3},{8,12},{9,13},{10,... | collective-permute-start | bytes 208904 | tf_op jit(solution)/shard_map/ppermute | solution.py:376
  11.9 5.2 %collective-permute-start.5 = (f32[136,128]{1,0:T(8,128)S(1)}, f32[136,128]{1,0:T(8,128)S(1)}, u32[]{:S(2)}, u32[]{:S(2)}) collective-permute-start(f32[136,128]{1,0:T(8,128)S(1)} %add.15), channel_id=1, source_target_pairs={{0,6},{1,7},{2,4},{3,5},{4,2},{5,3},{6,0},{7,1},{8,14},{9,15},{10,... | collective-permute-start | bytes 208904 | tf_op jit(solution)/shard_map/ppermute | solution.py:376
  17.1 6.0 %collective-permute-start.6 = (f32[136,128]{1,0:T(8,128)S(1)}, f32[136,128]{1,0:T(8,128)S(1)}, u32[]{:S(2)}, u32[]{:S(2)}) collective-permute-start(f32[136,128]{1,0:T(8,128)S(1)} %add_add_fusion), channel_id=1, source_target_pairs={{0,8},{1,9},{2,10},{3,11},{4,12},{5,13},{6,14},{7,15},{8,0},{9,1},... | collective-permute-start | bytes 208904 | tf_op jit(solution)/shard_map/ppermute | solution.py:376
  23.8 1.2 %collective-permute-start.7 = (f32[16,128]{1,0:T(8,128)S(1)}, f32[16,128]{1,0:T(8,128)S(1)}, u32[]{:S(2)}, u32[]{:S(2)}) collective-permute-start(f32[16,128]{1,0:T(8,128)S(1)} %get-tuple-element.30.mine_ref), channel_id=1, source_target_pairs={{0,1},{1,0},{2,3},{3,2},{4,5},{5,4},{6,7},{7,6},{8,9},{9,8},{10,11... | collective-permute-start | bytes 24584 | tf_op jit(solution)/shard_map/ppermute | solution.py:376
